TPU v7x, 32 devices: a whole 2x2x4 slice. The times are simulated.
32 devices in a mesh: groups: 2 (over y), sector: 4 (over z), term: 2 (over x), sub: 2 (over core).
Axes of the slice: x: 2, y: 2, z: 4, core: 2. Of those that a mesh axis runs over, the one named last changes fastest.
Arguments:
- wavefunction: bfloat16 [8, 4, 512, 512], P(('groups', 'sector'), 'term', 'sub'), parts along dimension 0, may hold values from -6 to 6
- left_env: bfloat16 [2, 8, 512, 512], P('term', ('groups', 'sector')), parts along dimension 1, may hold values from -0.1875 to 0.1875
- right_env: bfloat16 [2, 8, 512, 512], P('term', ('groups', 'sector')), parts along dimension 1, may hold values from -0.25 to 0.25
- left_dims: int32 [8], P('groups'), parts along dimension 0, may hold values from 128 to 512
- right_dims: int32 [8], P('groups'), parts along dimension 0, may hold values from 128 to 512
Outputs:
- product: bfloat16 [8, 4, 512, 512], P(('groups', 'sector'), 'term', 'sub'), parts along dimension 0
There are 2 independent parts, one for each index of `groups`. A program takes and returns all parts, laid end to end along the dimension named above; each array names one. Nothing has to cross between parts.
All inputs are finite; a program needn't handle non-finite values.
Results may differ from a plain program's by a relative error of at most 0.0051.
Values may be sent and summed in bfloat16 or wider, within the bound.
No kernel may reach another device: no remote copies, remote signals or barrier semaphores. Data moves between devices by JAX's collectives and lax.ppermute only.
A program may use at most 64 MiB of HBM per device.

v0:
```python
import jax
import jax.numpy as jnp
from jax import lax
from jax.sharding import PartitionSpec as P


def on_device(wavefunction, left_env, right_env, left_dims, right_dims):
    sector_pos = lax.axis_index("sector")
    term_pos = lax.axis_index("term")
    sub_pos = lax.axis_index("sub")
    n_sub = lax.axis_size("sub")
    right_count = wavefunction.shape[0]
    left_local = wavefunction.shape[1]
    half = wavefunction.shape[2]
    width = wavefunction.shape[3]
    left_count = left_env.shape[1]
    states = jnp.arange(width, dtype=jnp.int32)
    rows_here = sub_pos * half + jnp.arange(half, dtype=jnp.int32)
    left_live = lax.dynamic_slice_in_dim(left_dims, term_pos * left_local, left_local)
    right_live = lax.dynamic_slice_in_dim(right_dims, sector_pos * right_count, right_count)
    rows_ok = rows_here[None, :] < left_live[:, None]
    cols_ok = states[None, :] < right_live[:, None]
    masked = jnp.where(
        rows_ok[None, :, :, None] & cols_ok[:, None, None, :],
        wavefunction,
        jnp.zeros((), wavefunction.dtype),
    )
    contracted = jnp.einsum(
        "bakj,wbcj->wbakc",
        lax.all_gather(masked, "term", axis=1, tiled=True),
        right_env,
        preferred_element_type=jnp.float32,
    ).astype(jnp.bfloat16)
    arrived = lax.all_to_all(contracted, "sector", split_axis=2, concat_axis=1, tiled=True)
    own_columns = lax.dynamic_slice_in_dim(left_env, sub_pos * half, half, 3)
    start = jnp.int32(0)
    outputs = []
    for group in range(lax.axis_size(("term", "sub")) * left_local // left_local):
        position = start // left_local + group
        term_group = position // n_sub
        row_group = position % n_sub
        arrived_part = lax.dynamic_slice_in_dim(arrived, term_group * left_local, left_local, 1)
        left_rows = lax.dynamic_slice_in_dim(own_columns, row_group * half, half, 2)
        outputs.append(
            jnp.einsum(
                "wark,wnakc->narc", left_rows, arrived_part, preferred_element_type=jnp.float32
            )
        )
    summed = lax.psum_scatter(
        jnp.concatenate(outputs, axis=0), ("term", "sub"), scatter_dimension=0, tiled=True
    )
    summed = jnp.transpose(summed, (1, 0, 2, 3))
    out_left = lax.dynamic_slice_in_dim(left_dims, sector_pos * left_count, left_count)
    out_right = lax.dynamic_slice_in_dim(right_dims, term_pos * left_local, left_local)
    out_rows_ok = rows_here[None, :] < out_left[:, None]
    out_cols_ok = states[None, :] < out_right[:, None]
    result = jnp.where(
        out_rows_ok[:, None, :, None] & out_cols_ok[None, :, None, :],
        summed,
        jnp.zeros((), jnp.float32),
    )
    return result.astype(jnp.bfloat16)


def solution(mesh):
    return jax.shard_map(
        on_device,
        mesh=mesh,
        in_specs=(
            P(("groups", "sector"), "term", "sub", None),
            P("term", ("groups", "sector"), None, None),
            P("term", ("groups", "sector"), None, None),
            P("groups"),
            P("groups"),
        ),
        out_specs=P(("groups", "sector"), "term", "sub", None),
        check_vma=False,
    )
```

profile of v0, /device:TPU:0, one launch (start us, length us, event | category | flops | bytes accessed | tf_op | source)
XLA Modules:
  0.0 125.0 jit_solution(8432902516072294281)
XLA Ops:
  6.5 0.0 copy-start
  6.5 0.0 all-gather.2.cloned.1.call-start
  6.5 1.3 %dynamic_slice.34 = s32[1]{0:T(128)} dynamic-slice(s32[4]{0:T(128)} %param.9, s32[]{:T(128)S(6)} %select_n.57), dynamic_slice_sizes={1} | dynamic-slice | bytes 12 | tf_op jit(solution)/shard_map/dynamic_slice | solution.py:20
  7.8 0.6 iota_compare_fusion.1
  8.5 0.7 dynamic_slice.33
  9.2 0.1 broadcast_compare_fusion
  9.3 2.1 %and_select_fusion = bf16[1,2,256,512]{3,2,0,1:T(8,128)(2,1)} fusion(bf16[1,2,256,512]{3,2,1,0:T(8,128)(2,1)} %param.5, pred[512]{0:T(512)(128)(4,1)S(1)} %iota_compare_fusion.1, pred[2,256]{1,0:T(4,128)(4,1)S(1)} %broadcast_compare_fusion), kind=kLoop, calls=%fused_computation.10 | loop fusion | flops 524288 | bytes 1049600 | tf_op jit(solution)/shard_map/jit(_where)/select_n | solution.py:23
  11.4 0.0 all-gather.2.cloned.1.call-update
  11.4 24.2 %all-gather.2.cloned.1.call-done = bf16[1,4,256,512]{3,2,0,1:T(8,128)(2,1)} async-done(((bf16[1,2,256,512]{3,2,0,1:T(8,128)(2,1)}), bf16[1,4,256,512]{3,2,0,1:T(8,128)(2,1)}) %all-gather.2.cloned.1.call-update) | async-done | bytes 1048592 | tf_op jit(solution)/shard_map/all_gather | solution.py:30
  35.5 3.1 %fusion = bf16[1,1,4,256,512]{4,3,0,1,2:T(8,128)(2,1)} fusion(bf16[1,4,256,512]{3,2,0,1:T(8,128)(2,1)} %all-gather.2.cloned.1.call-done, bf16[1,1,512,512]{3,2,1,0:T(8,128)(2,1)} %param.7), kind=kOutput, calls=%fused_computation.6 | convolution fusion | flops 537395200 | bytes 2621440 | tf_op jit(solution)/shard_map/bakj,wbcj->wbakc/dot_general | solution.py:28
  38.7 4.6 %all-to-all-start = ((bf16[1,1,4,256,512]{4,3,0,1,2:T(8,128)(2,1)}), bf16[1,1,4,256,512]{4,3,0,1,2:T(8,128)(2,1)S(1)}, u32[]{:S(2)}, u32[]{:S(2)}) async-start(bf16[1,1,4,256,512]{4,3,0,1,2:T(8,128)(2,1)} %fusion), calls=%async_computation | async-start | bytes 2097152 | tf_op jit(solution)/shard_map/all_to_all | solution.py:34
  43.3 0.0 reduce-scatter.2.cloned.1.call-start
  43.3 25.7 %all-to-all-done = bf16[1,1,4,256,512]{4,3,0,1,2:T(8,128)(2,1)S(1)} async-done(((bf16[1,1,4,256,512]{4,3,0,1,2:T(8,128)(2,1)}), bf16[1,1,4,256,512]{4,3,0,1,2:T(8,128)(2,1)S(1)}, u32[]{:S(2)}, u32[]{:S(2)}) %all-to-all-start) | async-done | bytes 1048608 | tf_op jit(solution)/shard_map/all_to_all | solution.py:34
  69.0 0.0 copy-done
  69.0 0.4 convolution_bitcast_fusion.1
  69.4 0.4 convolution_bitcast_fusion.2
  69.8 0.4 convolution_bitcast_fusion.3
  70.3 0.4 convolution_bitcast_fusion
  70.7 2.2 %pad_maximum_fusion = f32[8,1,256,512]{2,3,0,1:T(8,128)} fusion(f32[2,1,256,512]{2,3,0,1:T(8,128)S(1)} %convolution_bitcast_fusion, f32[2,1,256,512]{2,3,0,1:T(8,128)S(1)} %convolution_bitcast_fusion.1, f32[2,1,256,512]{2,3,0,1:T(8,128)S(1)} %convolution_bitcast_fusion.2, f32[2,1,256,512]{2,3,0,1:T(8,128)S(1)} %convolution_bitcast_fusion.3), kind=kLoop, calls=%fused_computation | loop fusion | flops 3145728 | bytes 8388608 | tf_op jit(solution)/shard_map/concatenate | solution.py:50
  72.9 0.0 copy-start.1
  72.9 0.0 copy-start.2
  72.9 0.0 reduce-scatter.2.cloned.1.call-update
  72.9 0.6 copy-done.1
  73.6 0.6 dynamic_slice.31
  74.2 0.0 copy-done.2
  74.2 0.1 dynamic_slice.32
  74.2 0.7 broadcast_compare_fusion.1
  74.9 0.1 iota_compare_fusion
  75.0 40.8 %reduce-scatter.2.cloned.1.call-done = f32[2,1,256,512]{2,3,0,1:T(8,128)} async-done(((f32[8,1,256,512]{2,3,0,1:T(8,128)}), f32[2,1,256,512]{2,3,0,1:T(8,128)}) %reduce-scatter.2.cloned.1.call-update) | async-done | bytes 1048592 | tf_op jit(solution)/shard_map/reduce_scatter | solution.py:49
  115.7 1.4 %fusion.1 = bf16[1,2,256,512]{2,3,1,0:T(8,128)(2,1)S(1)} fusion(f32[2,1,256,512]{2,3,0,1:T(8,128)} %reduce-scatter.2.cloned.1.call-done, pred[2,512]{1,0:T(4,128)(4,1)S(1)} %iota_compare_fusion, pred[256]{0:T(512)(128)(4,1)S(1)} %broadcast_compare_fusion.1), kind=kLoop, calls=%fused_computation.8 | loop fusion | flops 524288 | bytes 1574144 | tf_op jit(solution)/shard_map/convert_element_type | solution.py:62
  117.2 1.0 copy.15
  (1 shorter events, 0.0 us)
Async XLA Ops:
  6.5 62.5 %copy-start = (bf16[1,1,512,512]{3,2,1,0:T(8,128)(2,1)S(1)}, bf16[1,1,512,512]{3,2,1,0:T(8,128)(2,1)}, u32[]{:S(2)}) copy-start(bf16[1,1,512,512]{3,2,1,0:T(8,128)(2,1)} %param.6) | copy-start | bytes 1572868
  6.5 29.0 %all-gather.2.cloned.1.call-start = ((), (), s32[]{:S(2)}) async-start(), calls=%async_computation.2 | async-start | bytes 1572864 | tf_op jit(solution)/shard_map/all_gather | solution.py:30
  38.7 30.3 %all-to-all-start = ((bf16[1,1,4,256,512]{4,3,0,1,2:T(8,128)(2,1)}), bf16[1,1,4,256,512]{4,3,0,1,2:T(8,128)(2,1)S(1)}, u32[]{:S(2)}, u32[]{:S(2)}) async-start(bf16[1,1,4,256,512]{4,3,0,1,2:T(8,128)(2,1)} %fusion), calls=%async_computation | async-start | bytes 2097152 | tf_op jit(solution)/shard_map/all_to_all | solution.py:34
  43.3 72.5 %reduce-scatter.2.cloned.1.call-start = ((), (), s32[]{:S(2)}) async-start(), calls=%async_computation.3 | async-start | bytes 5242880 | tf_op jit(solution)/shard_map/reduce_scatter | solution.py:49
  72.9 0.7 copy-start.1
  72.9 1.2 copy-start.2
Sparse Core Ops, SparseCore 0:
  11.5 23.9 all-gather.1
  73.1 42.6 reduce-scatter.1
where the time goes:
time: 125 us
  waiting for transfers between devices  90.7 us (73%)
  between operations  13.4 us (11%)
  other arithmetic  7.14 us (6%)
  matrix products  4.83 us (4%)
  starting transfers between devices  4.6 us (4%)
  local copies, waits for them, and re-layouts  4.33 us (3%)
    reduce_scatter x1, waiting for transfers between devices, on_device(): lax.psum_scatter(jnp.concatenate(outputs, axis=0), ('term', 'sub'), scatt...  40.8 us
    all_to_all x1, waiting for transfers between devices, on_device(): lax.all_to_all(contracted, 'sector', split_axis=2, concat_axis=1, tiled=T...  25.7 us
    all_gather x1, waiting for transfers between devices, on_device(): lax.all_gather(masked, 'term', axis=1, tiled=True)  24.2 us
    all_to_all x1, starting transfers between devices, on_device(): lax.all_to_all(contracted, 'sector', split_axis=2, concat_axis=1, tiled=T...  4.6 us
    dot_general x1, matrix products, on_device(): jnp.einsum('bakj,wbcj->wbakc', lax.all_gather(masked, 'term', axis=1, til...  3.12 us
  transfers between devices with their start and end apart: 3, of which 3 were waited for; matrix products, arithmetic and copies ran while one was open for 1% of the time, Pallas kernels for 0%

commit v1 on v0

v1 whole, which is shorter than its diff:
```python
import jax
import jax.numpy as jnp
from jax import lax
from jax.sharding import PartitionSpec as P

LINE = ("sector", "term", "sub")
F32 = jnp.float32
BF16 = jnp.bfloat16


def masked_envs(left_env, right_env, left_dims, right_dims, sector_pos):
    states = jnp.arange(left_env.shape[-1], dtype=jnp.int32)
    left_live = states < lax.dynamic_index_in_dim(left_dims, sector_pos, 0, keepdims=False)
    right_live = states < lax.dynamic_index_in_dim(right_dims, sector_pos, 0, keepdims=False)
    left = jnp.where(left_live[:, None] & left_live[None, :], left_env[0, 0], jnp.zeros((), left_env.dtype))
    right = jnp.where(right_live[:, None] & right_live[None, :], right_env[0, 0], jnp.zeros((), right_env.dtype))
    return left, right


def two_by_four(wavefunction, left_env, right_env, left_dims, right_dims):
    z, t, u = (lax.axis_index(name) for name in LINE)
    sectors, terms, subs = (lax.axis_size(name) for name in LINE)
    half = wavefunction.shape[2]
    home = (z // 2) == t
    odd = (z & 1) == 1

    def index(zz, tt, uu):
        return (zz * terms + tt) * subs + uu

    def permute(value, target):
        pairs = []
        for zz in range(sectors):
            for tt in range(terms):
                for uu in range(subs):
                    place = target(zz, tt, uu)
                    if place is not None:
                        pairs.append((index(zz, tt, uu), index(*place)))
        return lax.ppermute(value, LINE, pairs)

    def over_term(value):
        return permute(value, lambda zz, tt, uu: (zz, 1 - tt, uu))

    def over_core(value):
        return permute(value, lambda zz, tt, uu: (zz, tt, 1 - uu))

    def from_home(value, flip):
        return permute(value, lambda zz, tt, uu: (zz ^ flip, tt, uu) if zz // 2 == tt else None)

    def from_away(value, flip):
        return permute(value, lambda zz, tt, uu: (zz ^ flip, tt, uu) if zz // 2 != tt else None)

    own_same = jnp.where(odd, wavefunction[0, 1], wavefunction[0, 0])
    own_flip = jnp.where(odd, wavefunction[0, 0], wavefunction[0, 1])
    other_same = over_term(own_same)
    other_flip = over_term(own_flip)
    left, right = masked_envs(left_env, right_env, left_dims, right_dims, z)
    rows = lax.dynamic_slice_in_dim(left, u * half, half, 0)
    left_mine = lax.dynamic_slice_in_dim(rows, u * half, half, 1)
    left_theirs = lax.dynamic_slice_in_dim(rows, (1 - u) * half, half, 1)

    def contract(block):
        return lax.dot_general(block, right, (((1,), (1,)), ((), ())), preferred_element_type=F32).astype(BF16)

    def apply_left(mine, theirs):
        return jnp.dot(left_mine, mine, preferred_element_type=F32) + jnp.dot(
            left_theirs, theirs, preferred_element_type=F32
        )

    moved_own_same = contract(own_same)
    moved_own_flip = contract(own_flip)
    early_same = from_away(moved_own_same, 2)
    early_flip = from_away(moved_own_flip, 3)
    moved_other_same = contract(other_same)
    late_same = from_home(moved_other_same, 2)
    moved_other_flip = contract(other_flip)
    late_flip = from_home(moved_other_flip, 3)
    near = permute(jnp.where(home, moved_own_flip, moved_other_flip), lambda zz, tt, uu: (zz ^ 1, tt, uu))

    away1 = jnp.where(home, early_same, moved_other_same)
    away1_sent = over_term(apply_left(away1, over_core(away1)).astype(BF16))
    away2 = jnp.where(home, early_flip, near)
    away2_sent = over_term(apply_left(away2, over_core(away2)).astype(BF16))
    kept1 = jnp.where(home, moved_own_same, late_same)
    out1 = (apply_left(kept1, over_core(kept1)) + away1_sent.astype(F32)).astype(BF16)
    kept2 = jnp.where(home, near, late_flip)
    out2 = (apply_left(kept2, over_core(kept2)) + away2_sent.astype(F32)).astype(BF16)
    return jnp.stack([jnp.where(odd, out2, out1), jnp.where(odd, out1, out2)])[None]


def any_size(wavefunction, left_env, right_env, left_dims, right_dims):
    z, t, u = (lax.axis_index(name) for name in LINE)
    half = wavefunction.shape[2]
    left, right = masked_envs(left_env, right_env, left_dims, right_dims, z)
    rows = lax.dynamic_slice_in_dim(left, u * half, half, 0)
    blocks = lax.all_gather(wavefunction[0], "term", axis=0, tiled=True)
    moved = jnp.einsum("akj,cj->akc", blocks, right, preferred_element_type=F32).astype(BF16)
    arrived = lax.all_to_all(moved, "sector", split_axis=0, concat_axis=0, tiled=True)
    both = lax.all_gather(arrived, "sub", axis=1, tiled=True)
    partial = jnp.einsum("rk,bkc->brc", rows, both, preferred_element_type=F32)
    return lax.psum_scatter(partial, "term", scatter_dimension=0, tiled=True).astype(BF16)[None]


def solution(mesh):
    sizes = tuple(mesh.shape[name] for name in LINE)
    return jax.shard_map(
        two_by_four if sizes == (4, 2, 2) else any_size,
        mesh=mesh,
        in_specs=(
            P(("groups", "sector"), "term", "sub", None),
            P("term", ("groups", "sector"), None, None),
            P("term", ("groups", "sector"), None, None),
            P("groups"),
            P("groups"),
        ),
        out_specs=P(("groups", "sector"), "term", "sub", None),
        check_vma=False,
    )
```

time: 125 us -> 61.2 us (0.49)
  waiting for transfers between devices: 90.7 us -> 29.7 us
  starting transfers between devices: 4.6 us -> 20.8 us
  between operations: 13.4 us -> 0.24 us
  other arithmetic: 7.14 us -> 3.56 us
  local copies, waits for them, and re-layouts: 4.33 us -> 2.54 us
    reduce_scatter x1 -> x0, waiting for transfers between devices: 40.8 us -> none  [on_device(): lax.psum_scatter(jnp.concatenate(outputs, axis=0), ('term', 'sub'), scatt...]
    ppermute x0 -> x13, waiting for transfers between devices: none -> 29.7 us  [permute(): return lax.ppermute(value, LINE, pairs)]
    all_to_all x1 -> x0, waiting for transfers between devices: 25.7 us -> none  [on_device(): lax.all_to_all(contracted, 'sector', split_axis=2, concat_axis=1, tiled=T...]
    all_gather x1 -> x0, waiting for transfers between devices: 24.2 us -> none  [on_device(): lax.all_gather(masked, 'term', axis=1, tiled=True)]
    ppermute x0 -> x13, starting transfers between devices: none -> 20.8 us  [permute(): return lax.ppermute(value, LINE, pairs)]
    all_to_all x1 -> x0, starting transfers between devices: 4.6 us -> none  [on_device(): lax.all_to_all(contracted, 'sector', split_axis=2, concat_axis=1, tiled=T...]
    concatenate x1 -> x0, other arithmetic: 2.21 us -> none  [on_device(): jnp.concatenate(outputs, axis=0)]
    dynamic_slice x4 -> x2, local copies, waits for them, and re-layouts: 2.68 us -> 1.16 us  [the longest x1 0.58 us: masked_envs(): lax.dynamic_index_in_dim(right_dims, sector_pos, 0, keepdims=False)]
  transfers between devices with their start and end apart: 3 -> 13, of which waited for: 3 -> 6; matrix products, arithmetic and copies ran while one was open for 1% -> 8% of each run, Pallas kernels for 0% -> 0%
where the time goes in v1:
time: 61.2 us; the launch traced here: 60.9 us
  waiting for transfers between devices  29.7 us (49%)
  starting transfers between devices  20.8 us (34%)
  matrix products  4.13 us (7%)
  other arithmetic  3.56 us (6%)
  local copies, waits for them, and re-layouts  2.54 us (4%)
    ppermute x13, waiting for transfers between devices, permute(): return lax.ppermute(value, LINE, pairs)  29.7 us
    ppermute x13, starting transfers between devices, permute(): return lax.ppermute(value, LINE, pairs)  20.8 us
    dot_general x4, matrix products, contract(): lax.dot_general(block, right, (((1,), (1,)), ((), ())), preferred_element...  1.77 us
    unnamed x8, local copies, waits for them, and re-layouts  1.38 us
  transfers between devices with their start and end apart: 13, of which 6 were waited for; matrix products, arithmetic and copies ran while one was open for 8% of the time, Pallas kernels for 0%

profile of v1, /device:TPU:0, one launch (start us, length us, event | category | flops | bytes accessed | tf_op | source)
XLA Modules:
  0.0 60.9 jit_solution(11864416882793791265)
XLA Ops:
  0.0 0.7 %copy-done.2 = s32[4]{0:T(128)S(1)} copy-done((s32[4]{0:T(128)S(1)}, s32[4]{0:T(128)}, u32[]{:S(2)}) %copy-start.2) | copy-done | bytes 40
  0.7 0.6 dynamic_slice.16
  1.2 0.6 %iota_compare_fusion = pred[512]{0:T(512)(128)(4,1)S(1)} fusion(s32[]{:T(128)} %bitcast.3), kind=kLoop, calls=%fused_computation.40 | loop fusion | flops 512 | bytes 516 | tf_op jit(solution)/shard_map/lt | solution.py:14
  1.9 1.1 %select_bitcast_fusion.3 = (bf16[256,512]{1,0:T(8,128)(2,1)S(1)}, bf16[256,512]{1,0:T(8,128)(2,1)S(1)}) fusion(pred[]{:T(512)S(6)} %eq.6, bf16[1,2,256,512]{3,2,1,0:T(8,128)(2,1)} %param.5), kind=kLoop, calls=%fused_computation.22 | loop fusion | flops 262144 | bytes 1048577 | tf_op jit(solution)/shard_map/jit(_where)/select_n | solution.py:53
  3.1 0.4 convolution_convert_fusion.1
  3.5 1.3 %collective-permute-start.10 = (bf16[256,512]{1,0:T(8,128)(2,1)S(1)}, bf16[256,512]{1,0:T(8,128)(2,1)S(1)}, u32[]{:S(2)}, u32[]{:S(2)}) collective-permute-start(bf16[256,512]{1,0:T(8,128)(2,1)S(1)} %convolution_convert_fusion.1), channel_id=1, source_target_pairs={{2,10},{3,11},{6,14},{7,15},{8,0},{9,1},{12,4},{13,5},{18,26},{19,... | collective-permute-start | bytes 786440 | tf_op jit(solution)/shard_map/ppermute | solution.py:38
  4.8 6.2 %collective-permute-start.7 = (bf16[256,512]{1,0:T(8,128)(2,1)S(1)}, bf16[256,512]{1,0:T(8,128)(2,1)S(1)}, u32[]{:S(2)}, u32[]{:S(2)}) collective-permute-start(bf16[256,512]{1,0:T(8,128)(2,1)S(1)} %get-tuple-element.8), channel_id=1, source_target_pairs={{0,2},{1,3},{2,0},{3,1},{4,6},{5,7},{6,4},{7,5},{8,10},{9,11},{10,... | collective-permute-start | bytes 786440 | tf_op jit(solution)/shard_map/ppermute | solution.py:38
  11.1 0.7 %copy-done.3 = s32[4]{0:T(128)S(1)} copy-done((s32[4]{0:T(128)S(1)}, s32[4]{0:T(128)}, u32[]{:S(2)}) %copy-start.3) | copy-done | bytes 40
  11.8 0.6 dynamic_slice.14
  12.4 0.6 %iota_compare_fusion.1 = pred[512]{0:T(512)(128)(4,1)S(1)} fusion(s32[]{:T(128)} %bitcast), kind=kLoop, calls=%fused_computation.41 | loop fusion | flops 512 | bytes 516 | tf_op jit(solution)/shard_map/lt | solution.py:13
  13.0 7.7 %collective-permute-done.10 = bf16[256,512]{1,0:T(8,128)(2,1)S(1)} collective-permute-done((bf16[256,512]{1,0:T(8,128)(2,1)S(1)}, bf16[256,512]{1,0:T(8,128)(2,1)S(1)}, u32[]{:S(2)}, u32[]{:S(2)}) %collective-permute-start.10) | collective-permute-done | bytes 262176 | tf_op jit(solution)/shard_map/ppermute | solution.py:38
  20.8 0.4 broadcast_select_fusion
  21.2 1.5 %collective-permute-start.8 = (bf16[256,512]{1,0:T(8,128)(2,1)S(1)}, bf16[256,512]{1,0:T(8,128)(2,1)S(1)}, u32[]{:S(2)}, u32[]{:S(2)}) collective-permute-start(bf16[256,512]{1,0:T(8,128)(2,1)S(1)} %get-tuple-element.14), channel_id=1, source_target_pairs={{0,8},{1,9},{4,12},{5,13},{10,2},{11,3},{14,6},{15,7},{16,24},{17,... | collective-permute-start | bytes 786440 | tf_op jit(solution)/shard_map/ppermute | solution.py:38
  22.7 0.4 convolution_convert_fusion.2
  23.2 0.4 broadcast_select_fusion.4
  23.6 3.5 %collective-permute-start.2 = (bf16[256,512]{1,0:T(8,128)(2,1)S(1)}, bf16[256,512]{1,0:T(8,128)(2,1)S(1)}, u32[]{:S(2)}, u32[]{:S(2)}) collective-permute-start(bf16[256,512]{1,0:T(8,128)(2,1)S(1)} %convolution_convert_fusion.2), channel_id=1, source_target_pairs={{0,12},{1,13},{4,8},{5,9},{10,6},{11,7},{14,2},{15,3},{16,28},{17,... | collective-permute-start | bytes 786440 | tf_op jit(solution)/shard_map/ppermute | solution.py:38
  27.1 1.3 %collective-permute-start.4 = (bf16[256,512]{1,0:T(8,128)(2,1)S(1)}, bf16[256,512]{1,0:T(8,128)(2,1)S(1)}, u32[]{:S(2)}, u32[]{:S(2)}) collective-permute-start(bf16[256,512]{1,0:T(8,128)(2,1)S(1)} %get-tuple-element.12), channel_id=1, source_target_pairs={{2,14},{3,15},{6,10},{7,11},{8,4},{9,5},{12,0},{13,1},{18,30},{19,... | collective-permute-start | bytes 786440 | tf_op jit(solution)/shard_map/ppermute | solution.py:38
  28.9 0.6 %collective-permute-done.8 = bf16[256,512]{1,0:T(8,128)(2,1)S(1)} collective-permute-done((bf16[256,512]{1,0:T(8,128)(2,1)S(1)}, bf16[256,512]{1,0:T(8,128)(2,1)S(1)}, u32[]{:S(2)}, u32[]{:S(2)}) %collective-permute-start.8) | collective-permute-done | bytes 262176 | tf_op jit(solution)/shard_map/ppermute | solution.py:38
  29.6 10.5 %collective-permute-done.4 = bf16[256,512]{1,0:T(8,128)(2,1)S(1)} collective-permute-done((bf16[256,512]{1,0:T(8,128)(2,1)S(1)}, bf16[256,512]{1,0:T(8,128)(2,1)S(1)}, u32[]{:S(2)}, u32[]{:S(2)}) %collective-permute-start.4) | collective-permute-done | bytes 262176 | tf_op jit(solution)/shard_map/ppermute | solution.py:38
  40.1 0.6 %collective-permute-done.1 = bf16[256,512]{1,0:T(8,128)(2,1)S(1)} collective-permute-done((bf16[256,512]{1,0:T(8,128)(2,1)S(1)}, bf16[256,512]{1,0:T(8,128)(2,1)S(1)}, u32[]{:S(2)}, u32[]{:S(2)}) %collective-permute-start.1) | collective-permute-done | bytes 262176 | tf_op jit(solution)/shard_map/ppermute | solution.py:38
  40.9 0.3 fusion.13
  41.1 0.3 fusion.5
  41.4 5.7 %collective-permute-start.12 = (bf16[256,512]{1,0:T(8,128)(2,1)S(1)}, bf16[256,512]{1,0:T(8,128)(2,1)S(1)}, u32[]{:S(2)}, u32[]{:S(2)}) collective-permute-start(bf16[256,512]{1,0:T(8,128)(2,1)S(1)} %fusion.5), channel_id=1, source_target_pairs={{0,2},{1,3},{2,0},{3,1},{4,6},{5,7},{6,4},{7,5},{8,10},{9,11},{10,... | collective-permute-start | bytes 786440 | tf_op jit(solution)/shard_map/ppermute | solution.py:38
  47.7 0.3 fusion.4
  48.0 0.7 %collective-permute-start.6 = (bf16[256,512]{1,0:T(8,128)(2,1)S(1)}, bf16[256,512]{1,0:T(8,128)(2,1)S(1)}, u32[]{:S(2)}, u32[]{:S(2)}) collective-permute-start(bf16[256,512]{1,0:T(8,128)(2,1)S(1)} %fusion.4), channel_id=1, source_target_pairs={{0,2},{1,3},{2,0},{3,1},{4,6},{5,7},{6,4},{7,5},{8,10},{9,11},{10,... | collective-permute-start | bytes 786440 | tf_op jit(solution)/shard_map/ppermute | solution.py:38
  48.7 0.3 fusion.15
  49.0 0.3 fusion.19
  49.3 5.1 %collective-permute-done.12 = bf16[256,512]{1,0:T(8,128)(2,1)S(1)} collective-permute-done((bf16[256,512]{1,0:T(8,128)(2,1)S(1)}, bf16[256,512]{1,0:T(8,128)(2,1)S(1)}, u32[]{:S(2)}, u32[]{:S(2)}) %collective-permute-start.12) | collective-permute-done | bytes 262176 | tf_op jit(solution)/shard_map/ppermute | solution.py:38
  54.3 0.3 fusion.3
  54.6 5.1 %collective-permute-done.6 = bf16[256,512]{1,0:T(8,128)(2,1)S(1)} collective-permute-done((bf16[256,512]{1,0:T(8,128)(2,1)S(1)}, bf16[256,512]{1,0:T(8,128)(2,1)S(1)}, u32[]{:S(2)}, u32[]{:S(2)}) %collective-permute-start.6) | collective-permute-done | bytes 262176 | tf_op jit(solution)/shard_map/ppermute | solution.py:38
  59.7 0.3 select_bitcast_fusion.1
  60.1 0.8 %maximum_bitcast_fusion = bf16[1,2,256,512]{3,2,1,0:T(8,128)(2,1)} fusion(bf16[1,256,512]{2,1,0:T(8,128)(2,1)S(1)} %get-tuple-element.6, bf16[1,256,512]{2,1,0:T(8,128)(2,1)S(1)} %get-tuple-element.5), kind=kLoop, calls=%fused_computation.18 | loop fusion | flops 262144 | bytes 1048576 | tf_op jit(solution)/shard_map/broadcast_in_dim | solution.py:87
  (23 shorter events, 1.2 us)
Async XLA Ops:
  0.0 0.7 %copy-start.2 = (s32[4]{0:T(128)S(1)}, s32[4]{0:T(128)}, u32[]{:S(2)}) copy-start(s32[4]{0:T(128)} %param.9) | copy-start | bytes 52
  1.9 1.2 %copy-start.1 = (bf16[1,1,512,512]{3,2,1,0:T(8,128)(2,1)S(1)}, bf16[1,1,512,512]{3,2,1,0:T(8,128)(2,1)}, u32[]{:S(2)}) copy-start(bf16[1,1,512,512]{3,2,1,0:T(8,128)(2,1)} %param.7) | copy-start | bytes 1572868
  3.5 17.2 %collective-permute-start.10 = (bf16[256,512]{1,0:T(8,128)(2,1)S(1)}, bf16[256,512]{1,0:T(8,128)(2,1)S(1)}, u32[]{:S(2)}, u32[]{:S(2)}) collective-permute-start(bf16[256,512]{1,0:T(8,128)(2,1)S(1)} %convolution_convert_fusion.1), channel_id=1, source_target_pairs={{2,10},{3,11},{6,14},{7,15},{8,0},{9,1},{12,4},{13,5},{18,26},{19,... | collective-permute-start | bytes 786440 | tf_op jit(solution)/shard_map/ppermute | solution.py:38
  4.8 15.9 %collective-permute-start.7 = (bf16[256,512]{1,0:T(8,128)(2,1)S(1)}, bf16[256,512]{1,0:T(8,128)(2,1)S(1)}, u32[]{:S(2)}, u32[]{:S(2)}) collective-permute-start(bf16[256,512]{1,0:T(8,128)(2,1)S(1)} %get-tuple-element.8), channel_id=1, source_target_pairs={{0,2},{1,3},{2,0},{3,1},{4,6},{5,7},{6,4},{7,5},{8,10},{9,11},{10,... | collective-permute-start | bytes 786440 | tf_op jit(solution)/shard_map/ppermute | solution.py:38
  11.1 11.6 %collective-permute-start = (bf16[256,512]{1,0:T(8,128)(2,1)S(1)}, bf16[256,512]{1,0:T(8,128)(2,1)S(1)}, u32[]{:S(2)}, u32[]{:S(2)}) collective-permute-start(bf16[256,512]{1,0:T(8,128)(2,1)S(1)} %get-tuple-element.7), channel_id=1, source_target_pairs={{0,2},{1,3},{2,0},{3,1},{4,6},{5,7},{6,4},{7,5},{8,10},{9,11},{10,... | collective-permute-start | bytes 786440 | tf_op jit(solution)/shard_map/ppermute | solution.py:38
  11.1 0.7 %copy-start.3 = (s32[4]{0:T(128)S(1)}, s32[4]{0:T(128)}, u32[]{:S(2)}) copy-start(s32[4]{0:T(128)} %param.8) | copy-start | bytes 52
  21.2 8.2 %collective-permute-start.8 = (bf16[256,512]{1,0:T(8,128)(2,1)S(1)}, bf16[256,512]{1,0:T(8,128)(2,1)S(1)}, u32[]{:S(2)}, u32[]{:S(2)}) collective-permute-start(bf16[256,512]{1,0:T(8,128)(2,1)S(1)} %get-tuple-element.14), channel_id=1, source_target_pairs={{0,8},{1,9},{4,12},{5,13},{10,2},{11,3},{14,6},{15,7},{16,24},{17,... | collective-permute-start | bytes 786440 | tf_op jit(solution)/shard_map/ppermute | solution.py:38
  23.2 5.4 %copy-start = (bf16[1,1,512,512]{3,2,1,0:T(8,128)(2,1)S(1)}, bf16[1,1,512,512]{3,2,1,0:T(8,128)(2,1)}, u32[]{:S(2)}) copy-start(bf16[1,1,512,512]{3,2,1,0:T(8,128)(2,1)} %param.6) | copy-start | bytes 1572868
  23.6 17.1 %collective-permute-start.2 = (bf16[256,512]{1,0:T(8,128)(2,1)S(1)}, bf16[256,512]{1,0:T(8,128)(2,1)S(1)}, u32[]{:S(2)}, u32[]{:S(2)}) collective-permute-start(bf16[256,512]{1,0:T(8,128)(2,1)S(1)} %convolution_convert_fusion.2), channel_id=1, source_target_pairs={{0,12},{1,13},{4,8},{5,9},{10,6},{11,7},{14,2},{15,3},{16,28},{17,... | collective-permute-start | bytes 786440 | tf_op jit(solution)/shard_map/ppermute | solution.py:38
  27.1 12.9 %collective-permute-start.4 = (bf16[256,512]{1,0:T(8,128)(2,1)S(1)}, bf16[256,512]{1,0:T(8,128)(2,1)S(1)}, u32[]{:S(2)}, u32[]{:S(2)}) collective-permute-start(bf16[256,512]{1,0:T(8,128)(2,1)S(1)} %get-tuple-element.12), channel_id=1, source_target_pairs={{2,14},{3,15},{6,10},{7,11},{8,4},{9,5},{12,0},{13,1},{18,30},{19,... | collective-permute-start | bytes 786440 | tf_op jit(solution)/shard_map/ppermute | solution.py:38
  28.4 12.3 %collective-permute-start.1 = (bf16[256,512]{1,0:T(8,128)(2,1)S(1)}, bf16[256,512]{1,0:T(8,128)(2,1)S(1)}, u32[]{:S(2)}, u32[]{:S(2)}) collective-permute-start(bf16[256,512]{1,0:T(8,128)(2,1)S(1)} %get-tuple-element.11), channel_id=1, source_target_pairs={{0,4},{1,5},{2,6},{3,7},{4,0},{5,1},{6,2},{7,3},{8,12},{9,13},{10,... | collective-permute-start | bytes 786440 | tf_op jit(solution)/shard_map/ppermute | solution.py:38
  28.8 12.1 %collective-permute-start.11 = (bf16[256,512]{1,0:T(8,128)(2,1)S(1)}, bf16[256,512]{1,0:T(8,128)(2,1)S(1)}, u32[]{:S(2)}, u32[]{:S(2)}) collective-permute-start(bf16[256,512]{1,0:T(8,128)(2,1)S(1)} %get-tuple-element.13), channel_id=1, source_target_pairs={{0,1},{1,0},{2,3},{3,2},{4,5},{5,4},{6,7},{7,6},{8,9},{9,8},{10,11... | collective-permute-start | bytes 786440 | tf_op jit(solution)/shard_map/ppermute | solution.py:38
  29.5 19.2 %collective-permute-start.9 = (bf16[256,512]{1,0:T(8,128)(2,1)S(1)}, bf16[256,512]{1,0:T(8,128)(2,1)S(1)}, u32[]{:S(2)}, u32[]{:S(2)}) collective-permute-start(bf16[256,512]{1,0:T(8,128)(2,1)S(1)} %broadcast_select_fusion.1), channel_id=1, source_target_pairs={{0,1},{1,0},{2,3},{3,2},{4,5},{5,4},{6,7},{7,6},{8,9},{9,8},{10,11... | collective-permute-start | bytes 786440 | tf_op jit(solution)/shard_map/ppermute | solution.py:38
  40.8 6.6 %collective-permute-start.5 = (bf16[256,512]{1,0:T(8,128)(2,1)S(1)}, bf16[256,512]{1,0:T(8,128)(2,1)S(1)}, u32[]{:S(2)}, u32[]{:S(2)}) collective-permute-start(bf16[256,512]{1,0:T(8,128)(2,1)S(1)} %get-tuple-element.9), channel_id=1, source_target_pairs={{0,1},{1,0},{2,3},{3,2},{4,5},{5,4},{6,7},{7,6},{8,9},{9,8},{10,11... | collective-permute-start | bytes 786440 | tf_op jit(solution)/shard_map/ppermute | solution.py:38
  41.4 12.9 %collective-permute-start.12 = (bf16[256,512]{1,0:T(8,128)(2,1)S(1)}, bf16[256,512]{1,0:T(8,128)(2,1)S(1)}, u32[]{:S(2)}, u32[]{:S(2)}) collective-permute-start(bf16[256,512]{1,0:T(8,128)(2,1)S(1)} %fusion.5), channel_id=1, source_target_pairs={{0,2},{1,3},{2,0},{3,1},{4,6},{5,7},{6,4},{7,5},{8,10},{9,11},{10,... | collective-permute-start | bytes 786440 | tf_op jit(solution)/shard_map/ppermute | solution.py:38
  47.2 1.8 %collective-permute-start.3 = (bf16[256,512]{1,0:T(8,128)(2,1)S(1)}, bf16[256,512]{1,0:T(8,128)(2,1)S(1)}, u32[]{:S(2)}, u32[]{:S(2)}) collective-permute-start(bf16[256,512]{1,0:T(8,128)(2,1)S(1)} %get-tuple-element.10), channel_id=1, source_target_pairs={{0,1},{1,0},{2,3},{3,2},{4,5},{5,4},{6,7},{7,6},{8,9},{9,8},{10,11... | collective-permute-start | bytes 786440 | tf_op jit(solution)/shard_map/ppermute | solution.py:38
  48.0 11.8 %collective-permute-start.6 = (bf16[256,512]{1,0:T(8,128)(2,1)S(1)}, bf16[256,512]{1,0:T(8,128)(2,1)S(1)}, u32[]{:S(2)}, u32[]{:S(2)}) collective-permute-start(bf16[256,512]{1,0:T(8,128)(2,1)S(1)} %fusion.4), channel_id=1, source_target_pairs={{0,2},{1,3},{2,0},{3,1},{4,6},{5,7},{6,4},{7,5},{8,10},{9,11},{10,... | collective-permute-start | bytes 786440 | tf_op jit(solution)/shard_map/ppermute | solution.py:38

commit v2 on v1

v2 whole, which is shorter than its diff:
```python
import jax
import jax.numpy as jnp
from jax import lax
from jax.sharding import PartitionSpec as P

LINE = ("sector", "term", "sub")
F32 = jnp.float32
BF16 = jnp.bfloat16


def masked_envs(left_env, right_env, left_dims, right_dims, sector_pos):
    states = jnp.arange(left_env.shape[-1], dtype=jnp.int32)
    left_live = states < lax.dynamic_index_in_dim(left_dims, sector_pos, 0, keepdims=False)
    right_live = states < lax.dynamic_index_in_dim(right_dims, sector_pos, 0, keepdims=False)
    left = jnp.where(left_live[:, None] & left_live[None, :], left_env[0, 0], jnp.zeros((), left_env.dtype))
    right = jnp.where(right_live[:, None] & right_live[None, :], right_env[0, 0], jnp.zeros((), right_env.dtype))
    return left, right


def take(values, position):
    places = jnp.arange(values.shape[0], dtype=jnp.int32)
    return jnp.sum(jnp.where(places == position, values, 0))


def contract(block, right):
    return lax.dot_general(block, right, (((1,), (1,)), ((), ())), preferred_element_type=F32).astype(BF16)


def two_by_four(wavefunction, left_env, right_env, left_dims, right_dims):
    z, t, u = (lax.axis_index(name) for name in LINE)
    sectors, terms, subs = (lax.axis_size(name) for name in LINE)
    half, width = wavefunction.shape[2:]
    states = jnp.arange(width, dtype=jnp.int32)
    at_home = (z // 2) == t
    odd = z & 1

    def index(zz, tt, uu):
        return (zz * terms + tt) * subs + uu

    def permute(value, home, away):
        pairs = []
        for zz in range(sectors):
            for tt in range(terms):
                flip_sector, flip_term, flip_sub = home if zz // 2 == tt else away
                for uu in range(subs):
                    pairs.append((index(zz, tt, uu), index(zz ^ flip_sector, tt ^ flip_term, uu ^ flip_sub)))
        return lax.ppermute(value, LINE, pairs)

    def over_term(value):
        return permute(value, (0, 1, 0), (0, 1, 0))

    def over_core(value):
        return permute(value, (0, 0, 1), (0, 0, 1))

    own_same = lax.dynamic_index_in_dim(wavefunction[0], odd, 0, keepdims=False)
    own_flip = lax.dynamic_index_in_dim(wavefunction[0], 1 - odd, 0, keepdims=False)
    other_same = over_term(own_same)
    other_flip = over_term(own_flip)

    live = states < take(right_dims, z)
    right = jnp.where(live[:, None] & live[None, :], right_env[0, 0], jnp.zeros((), BF16))
    same_first = permute(contract(own_same, right), (0, 0, 0), (2, 1, 0))
    flip_first = permute(contract(own_flip, right), (1, 0, 0), (3, 1, 0))
    same_second = permute(contract(other_same, right), (2, 0, 0), (0, 1, 0))
    moved_last = contract(other_flip, right)
    flip_second = permute(moved_last, (3, 0, 0), (1, 1, 0))

    later_u, moved_last = lax.optimization_barrier((u, moved_last))
    own_rows = lax.dynamic_slice_in_dim(left_env[0, 0], later_u * half, half, 0)
    other_rows = over_term(own_rows)
    count = take(left_dims, z)
    rows_live = (u * half + states[:half]) < count
    cols_live = states < count
    lefts = []
    for rows in (jnp.where(at_home, own_rows, other_rows), jnp.where(at_home, other_rows, own_rows)):
        rows = jnp.where(rows_live[:, None] & cols_live[None, :], rows, jnp.zeros((), BF16))
        lefts.append([lax.dynamic_slice_in_dim(rows, part * half, half, 1) for part in (u, 1 - u)])

    def apply_left(left, mine):
        return jnp.dot(left[0], mine, preferred_element_type=F32) + jnp.dot(
            left[1], over_core(mine), preferred_element_type=F32
        )

    same = apply_left(lefts[0], same_first) + apply_left(lefts[1], same_second)
    flip = apply_left(lefts[0], flip_first) + apply_left(lefts[1], flip_second)
    same, flip = same.astype(BF16), flip.astype(BF16)
    return jnp.stack([jnp.where(odd == 1, flip, same), jnp.where(odd == 1, same, flip)])[None]


def any_size(wavefunction, left_env, right_env, left_dims, right_dims):
    z, t, u = (lax.axis_index(name) for name in LINE)
    half = wavefunction.shape[2]
    left, right = masked_envs(left_env, right_env, left_dims, right_dims, z)
    rows = lax.dynamic_slice_in_dim(left, u * half, half, 0)
    blocks = lax.all_gather(wavefunction[0], "term", axis=0, tiled=True)
    moved = jnp.einsum("akj,cj->akc", blocks, right, preferred_element_type=F32).astype(BF16)
    arrived = lax.all_to_all(moved, "sector", split_axis=0, concat_axis=0, tiled=True)
    both = lax.all_gather(arrived, "sub", axis=1, tiled=True)
    partial = jnp.einsum("rk,bkc->brc", rows, both, preferred_element_type=F32)
    return lax.psum_scatter(partial, "term", scatter_dimension=0, tiled=True).astype(BF16)[None]


def solution(mesh):
    sizes = tuple(mesh.shape[name] for name in LINE)
    return jax.shard_map(
        two_by_four if sizes == (4, 2, 2) else any_size,
        mesh=mesh,
        in_specs=(
            P(("groups", "sector"), "term", "sub", None),
            P("term", ("groups", "sector"), None, None),
            P("term", ("groups", "sector"), None, None),
            P("groups"),
            P("groups"),
        ),
        out_specs=P(("groups", "sector"), "term", "sub", None),
        check_vma=False,
    )
```

time: 61.2 us -> 47 us (0.77)
  the two profiles are of different devices: /device:TPU:0 before, /device:TPU:7 now
where the time goes in v2:
time: 47 us; the launch traced here: 46.8 us
  waiting for transfers between devices  18.2 us (39%)
  starting transfers between devices  16.6 us (35%)
  matrix products  5.28 us (11%)
  other arithmetic  4.39 us (9%)
  local copies, waits for them, and re-layouts  2.13 us (5%)
    ppermute x11, waiting for transfers between devices, permute(): return lax.ppermute(value, LINE, pairs)  18.2 us
    ppermute x11, starting transfers between devices, permute(): return lax.ppermute(value, LINE, pairs)  16.6 us
    dot_general x4, matrix products, contract(): lax.dot_general(block, right, (((1,), (1,)), ((), ())), preferred_element...  3.43 us
    reduce_sum x2, other arithmetic, take(): return jnp.sum(jnp.where(places == position, values, 0))  1.34 us
    squeeze x1, local copies, waits for them, and re-layouts, two_by_four(): lax.dynamic_index_in_dim(wavefunction[0], 1 - odd, 0, keepdims=False)  1.12 us
    unnamed x8, local copies, waits for them, and re-layouts  0.99 us
    dot_general x4, matrix products, apply_left(): jnp.dot(left[1], over_core(mine), preferred_element_type=F32)  0.96 us
  transfers between devices with their start and end apart: 11, of which 2 were waited for; matrix products, arithmetic and copies ran while one was open for 18% of the time, Pallas kernels for 0%

profile of v2, /device:TPU:7, one launch (start us, length us, event | category | flops | bytes accessed | tf_op | source)
XLA Modules:
  0.0 46.8 jit_solution(4347843042315174525)
XLA Ops:
  0.0 1.1 %dynamic-slice_bitcast_fusion.2 = (bf16[256,512]{1,0:T(8,128)(2,1)S(1)}, bf16[256,512]{1,0:T(8,128)(2,1)S(1)}) fusion(bf16[1,2,256,512]{3,2,1,0:T(8,128)(2,1)} %param.5, s32[]{:T(128)S(6)} %select_n.73, s32[]{:T(128)S(6)} %select_n.85), kind=kLoop, calls=%fused_computation.22 | loop fusion | bytes 1048584 | tf_op jit(solution)/shard_map/jit(dynamic_index_in_dim)/squeeze | solution.py:56
  1.1 0.3 collective-permute-start.8
  1.5 0.3 copy-done.2
  1.8 0.6 %fusion.28 = s32[]{:T(128)} fusion(s32[4]{0:T(128)S(1)} %copy-done.2, s32[]{:T(128)S(6)} %axis_index.33), kind=kLoop, calls=%fused_computation.49 | loop fusion | flops 11 | bytes 24 | tf_op jit(solution)/shard_map/reduce_sum | solution.py:22
  2.4 0.6 %iota_compare_fusion = pred[512]{0:T(512)(128)(4,1)S(1)} fusion(s32[]{:T(128)} %fusion.28), kind=kLoop, calls=%fused_computation.35 | loop fusion | flops 512 | bytes 516 | tf_op jit(solution)/shard_map/lt | solution.py:60
  3.1 0.4 convolution_convert_fusion.1
  3.5 4.8 %collective-permute-start.6 = (bf16[256,512]{1,0:T(8,128)(2,1)S(1)}, bf16[256,512]{1,0:T(8,128)(2,1)S(1)}, u32[]{:S(2)}, u32[]{:S(2)}) collective-permute-start(bf16[256,512]{1,0:T(8,128)(2,1)S(1)} %convolution_convert_fusion.1), channel_id=1, source_target_pairs={{0,0},{1,1},{2,8},{3,9},{4,4},{5,5},{6,12},{7,13},{8,2},{9,3},{10,... | collective-permute-start | bytes 786440 | tf_op jit(solution)/shard_map/ppermute | solution.py:47
  8.4 0.4 convolution_convert_fusion.2
  8.9 1.4 %collective-permute-start.2 = (bf16[256,512]{1,0:T(8,128)(2,1)S(1)}, bf16[256,512]{1,0:T(8,128)(2,1)S(1)}, u32[]{:S(2)}, u32[]{:S(2)}) collective-permute-start(bf16[256,512]{1,0:T(8,128)(2,1)S(1)} %convolution_convert_fusion.2), channel_id=1, source_target_pairs={{0,4},{1,5},{2,12},{3,13},{4,0},{5,1},{6,8},{7,9},{8,6},{9,7},{10,... | collective-permute-start | bytes 786440 | tf_op jit(solution)/shard_map/ppermute | solution.py:47
  10.3 0.7 %copy-done.3 = s32[4]{0:T(128)S(1)} copy-done((s32[4]{0:T(128)S(1)}, s32[4]{0:T(128)}, u32[]{:S(2)}) %copy-start.3) | copy-done | bytes 40
  11.0 0.7 %fusion.27 = s32[]{:T(128)} fusion(s32[4]{0:T(128)S(1)} %copy-done.3, s32[]{:T(128)S(6)} %axis_index.33), kind=kLoop, calls=%fused_computation.48 | loop fusion | flops 11 | bytes 24 | tf_op jit(solution)/shard_map/reduce_sum | solution.py:22
  11.7 3.3 %collective-permute-done = bf16[256,512]{1,0:T(8,128)(2,1)S(1)} collective-permute-done((bf16[256,512]{1,0:T(8,128)(2,1)S(1)}, bf16[256,512]{1,0:T(8,128)(2,1)S(1)}, u32[]{:S(2)}, u32[]{:S(2)}) %collective-permute-start) | collective-permute-done | bytes 262176 | tf_op jit(solution)/shard_map/ppermute | solution.py:47
  15.0 0.4 convolution_convert_fusion.3
  15.5 6.5 %collective-permute-start.4 = (bf16[256,512]{1,0:T(8,128)(2,1)S(1)}, bf16[256,512]{1,0:T(8,128)(2,1)S(1)}, u32[]{:S(2)}, u32[]{:S(2)}) collective-permute-start(bf16[256,512]{1,0:T(8,128)(2,1)S(1)} %convolution_convert_fusion.3), channel_id=1, source_target_pairs={{0,12},{1,13},{2,4},{3,5},{4,8},{5,9},{6,0},{7,1},{8,14},{9,15},{1... | collective-permute-start | bytes 786440 | tf_op jit(solution)/shard_map/ppermute | solution.py:47
  22.1 2.1 %convolution_convert_fusion = bf16[256,512]{1,0:T(8,128)(2,1)} fusion(bf16[256,512]{1,0:T(8,128)(2,1)} %collective-permute-done.8, bf16[1,1,512,512]{3,2,1,0:T(8,128)(2,1)S(1)} %copy-done.1, pred[512]{0:T(512)(128)(4,1)S(1)} %iota_compare_fusion), kind=kOutput, calls=%fused_computation.8 | convolution fusion | flops 134873088 | bytes 1049088 | tf_op jit(solution)/shard_map/dot_general | solution.py:26
  24.2 1.4 %collective-permute-start.9 = (bf16[256,512]{1,0:T(8,128)(2,1)}, bf16[256,512]{1,0:T(8,128)(2,1)S(1)}, u32[]{:S(2)}, u32[]{:S(2)}) collective-permute-start(bf16[256,512]{1,0:T(8,128)(2,1)} %convolution_convert_fusion), channel_id=1, source_target_pairs={{0,8},{1,9},{2,0},{3,1},{4,12},{5,13},{6,4},{7,5},{8,10},{9,11},{1... | collective-permute-start | bytes 786440 | tf_op jit(solution)/shard_map/ppermute | solution.py:47
  25.6 0.7 %iota_compare_fusion.1 = pred[512]{0:T(512)(128)(4,1)S(1)} fusion(s32[]{:T(128)} %fusion.27), kind=kLoop, calls=%fused_computation.36 | loop fusion | flops 512 | bytes 516 | tf_op jit(solution)/shard_map/lt | solution.py:73
  26.3 0.7 %add_compare_fusion = pred[256]{0:T(512)(128)(4,1)S(1)} fusion(s32[512]{0:T(512)S(1)} %iota.17, s32[]{:T(128)} %fusion.27, s32[]{:T(128)S(6)} %mul.12), kind=kLoop, calls=%fused_computation.47 | loop fusion | flops 512 | bytes 1288 | tf_op jit(solution)/shard_map/lt | solution.py:72
  27.0 1.4 %collective-permute-start.7 = (bf16[256,512]{1,0:T(8,128)(2,1)S(1)}, bf16[256,512]{1,0:T(8,128)(2,1)S(1)}, u32[]{:S(2)}, u32[]{:S(2)}) collective-permute-start(bf16[256,512]{1,0:T(8,128)(2,1)S(1)} %collective-permute-done.6), channel_id=1, source_target_pairs={{0,1},{1,0},{2,3},{3,2},{4,5},{5,4},{6,7},{7,6},{8,9},{9,8},{10,11... | collective-permute-start | bytes 786440 | tf_op jit(solution)/shard_map/ppermute | solution.py:47
  28.4 0.1 collective-permute-start.3
  28.5 14.8 %collective-permute-done.9 = bf16[256,512]{1,0:T(8,128)(2,1)S(1)} collective-permute-done((bf16[256,512]{1,0:T(8,128)(2,1)}, bf16[256,512]{1,0:T(8,128)(2,1)S(1)}, u32[]{:S(2)}, u32[]{:S(2)}) %collective-permute-start.9) | collective-permute-done | bytes 262176 | tf_op jit(solution)/shard_map/ppermute | solution.py:47
  43.3 0.5 %collective-permute-start.10 = (bf16[256,512]{1,0:T(8,128)(2,1)S(1)}, bf16[256,512]{1,0:T(8,128)(2,1)S(1)}, u32[]{:S(2)}, u32[]{:S(2)}) collective-permute-start(bf16[256,512]{1,0:T(8,128)(2,1)S(1)} %collective-permute-done.9), channel_id=1, source_target_pairs={{0,1},{1,0},{2,3},{3,2},{4,5},{5,4},{6,7},{7,6},{8,9},{9,8},{10,11... | collective-permute-start | bytes 786440 | tf_op jit(solution)/shard_map/ppermute | solution.py:47
  43.9 0.2 and_select_fusion.2
  44.0 0.2 fusion.15
  44.3 0.2 fusion.11
  44.5 0.2 convolution_add_fusion.1
  44.8 0.2 fusion.9
  45.0 0.2 fusion.17
  45.2 0.2 convolution_add_fusion.3
  45.5 0.2 fusion.3
  45.7 0.3 select_bitcast_fusion.1
  46.0 0.8 %maximum_bitcast_fusion = bf16[1,2,256,512]{3,2,1,0:T(8,128)(2,1)} fusion(bf16[1,256,512]{2,1,0:T(8,128)(2,1)S(1)} %get-tuple-element.10, bf16[1,256,512]{2,1,0:T(8,128)(2,1)S(1)} %get-tuple-element.9), kind=kLoop, calls=%fused_computation.17 | loop fusion | flops 262144 | bytes 1048576 | tf_op jit(solution)/shard_map/broadcast_in_dim | solution.py:87
  (20 shorter events, 0.2 us)
Async XLA Ops:
  0.0 3.1 %copy-start.1 = (bf16[1,1,512,512]{3,2,1,0:T(8,128)(2,1)S(1)}, bf16[1,1,512,512]{3,2,1,0:T(8,128)(2,1)}, u32[]{:S(2)}) copy-start(bf16[1,1,512,512]{3,2,1,0:T(8,128)(2,1)} %param.7) | copy-start | bytes 1572868
  1.1 0.7 %copy-start.2 = (s32[4]{0:T(128)S(1)}, s32[4]{0:T(128)}, u32[]{:S(2)}) copy-start(s32[4]{0:T(128)} %param.9) | copy-start | bytes 52
  1.1 20.9 %collective-permute-start.8 = (bf16[256,512]{1,0:T(8,128)(2,1)S(1)}, bf16[256,512]{1,0:T(8,128)(2,1)}, u32[]{:S(2)}, u32[]{:S(2)}) collective-permute-start(bf16[256,512]{1,0:T(8,128)(2,1)S(1)} %get-tuple-element.12), channel_id=1, source_target_pairs={{0,2},{1,3},{2,0},{3,1},{4,6},{5,7},{6,4},{7,5},{8,10},{9,11},{10,... | collective-permute-start | bytes 786440 | tf_op jit(solution)/shard_map/ppermute | solution.py:47
  3.5 23.5 %collective-permute-start.6 = (bf16[256,512]{1,0:T(8,128)(2,1)S(1)}, bf16[256,512]{1,0:T(8,128)(2,1)S(1)}, u32[]{:S(2)}, u32[]{:S(2)}) collective-permute-start(bf16[256,512]{1,0:T(8,128)(2,1)S(1)} %convolution_convert_fusion.1), channel_id=1, source_target_pairs={{0,0},{1,1},{2,8},{3,9},{4,4},{5,5},{6,12},{7,13},{8,2},{9,3},{10,... | collective-permute-start | bytes 786440 | tf_op jit(solution)/shard_map/ppermute | solution.py:47
  8.4 6.7 %collective-permute-start = (bf16[256,512]{1,0:T(8,128)(2,1)S(1)}, bf16[256,512]{1,0:T(8,128)(2,1)S(1)}, u32[]{:S(2)}, u32[]{:S(2)}) collective-permute-start(bf16[256,512]{1,0:T(8,128)(2,1)S(1)} %get-tuple-element.11), channel_id=1, source_target_pairs={{0,2},{1,3},{2,0},{3,1},{4,6},{5,7},{6,4},{7,5},{8,10},{9,11},{10,... | collective-permute-start | bytes 786440 | tf_op jit(solution)/shard_map/ppermute | solution.py:47
  8.9 19.6 %collective-permute-start.2 = (bf16[256,512]{1,0:T(8,128)(2,1)S(1)}, bf16[256,512]{1,0:T(8,128)(2,1)S(1)}, u32[]{:S(2)}, u32[]{:S(2)}) collective-permute-start(bf16[256,512]{1,0:T(8,128)(2,1)S(1)} %convolution_convert_fusion.2), channel_id=1, source_target_pairs={{0,4},{1,5},{2,12},{3,13},{4,0},{5,1},{6,8},{7,9},{8,6},{9,7},{10,... | collective-permute-start | bytes 786440 | tf_op jit(solution)/shard_map/ppermute | solution.py:47
  10.3 0.7 %copy-start.3 = (s32[4]{0:T(128)S(1)}, s32[4]{0:T(128)}, u32[]{:S(2)}) copy-start(s32[4]{0:T(128)} %param.8) | copy-start | bytes 52
  11.7 10.3 %copy-start = (bf16[1,1,512,512]{3,2,1,0:T(8,128)(2,1)S(1)}, bf16[1,1,512,512]{3,2,1,0:T(8,128)(2,1)}, u32[]{:S(2)}) copy-start(bf16[1,1,512,512]{3,2,1,0:T(8,128)(2,1)} %param.6) | copy-start | bytes 1572868
  15.5 28.3 %collective-permute-start.4 = (bf16[256,512]{1,0:T(8,128)(2,1)S(1)}, bf16[256,512]{1,0:T(8,128)(2,1)S(1)}, u32[]{:S(2)}, u32[]{:S(2)}) collective-permute-start(bf16[256,512]{1,0:T(8,128)(2,1)S(1)} %convolution_convert_fusion.3), channel_id=1, source_target_pairs={{0,12},{1,13},{2,4},{3,5},{4,8},{5,9},{6,0},{7,1},{8,14},{9,15},{1... | collective-permute-start | bytes 786440 | tf_op jit(solution)/shard_map/ppermute | solution.py:47
  22.0 21.9 %collective-permute-start.1 = (bf16[256,512]{1,0:T(8,128)(2,1)S(1)}, bf16[256,512]{1,0:T(8,128)(2,1)S(1)}, u32[]{:S(2)}, u32[]{:S(2)}) collective-permute-start(bf16[256,512]{1,0:T(8,128)(2,1)S(1)} %dynamic-slice_bitcast_fusion.1), channel_id=1, source_target_pairs={{0,2},{1,3},{2,0},{3,1},{4,6},{5,7},{6,4},{7,5},{8,10},{9,11},{10,... | collective-permute-start | bytes 786440 | tf_op jit(solution)/shard_map/ppermute | solution.py:47
  24.2 19.2 %collective-permute-start.9 = (bf16[256,512]{1,0:T(8,128)(2,1)}, bf16[256,512]{1,0:T(8,128)(2,1)S(1)}, u32[]{:S(2)}, u32[]{:S(2)}) collective-permute-start(bf16[256,512]{1,0:T(8,128)(2,1)} %convolution_convert_fusion), channel_id=1, source_target_pairs={{0,8},{1,9},{2,0},{3,1},{4,12},{5,13},{6,4},{7,5},{8,10},{9,11},{1... | collective-permute-start | bytes 786440 | tf_op jit(solution)/shard_map/ppermute | solution.py:47
  27.0 17.5 %collective-permute-start.7 = (bf16[256,512]{1,0:T(8,128)(2,1)S(1)}, bf16[256,512]{1,0:T(8,128)(2,1)S(1)}, u32[]{:S(2)}, u32[]{:S(2)}) collective-permute-start(bf16[256,512]{1,0:T(8,128)(2,1)S(1)} %collective-permute-done.6), channel_id=1, source_target_pairs={{0,1},{1,0},{2,3},{3,2},{4,5},{5,4},{6,7},{7,6},{8,9},{9,8},{10,11... | collective-permute-start | bytes 786440 | tf_op jit(solution)/shard_map/ppermute | solution.py:47
  28.4 16.8 %collective-permute-start.3 = (bf16[256,512]{1,0:T(8,128)(2,1)S(1)}, bf16[256,512]{1,0:T(8,128)(2,1)S(1)}, u32[]{:S(2)}, u32[]{:S(2)}) collective-permute-start(bf16[256,512]{1,0:T(8,128)(2,1)S(1)} %collective-permute-done.2), channel_id=1, source_target_pairs={{0,1},{1,0},{2,3},{3,2},{4,5},{5,4},{6,7},{7,6},{8,9},{9,8},{10,11... | collective-permute-start | bytes 786440 | tf_op jit(solution)/shard_map/ppermute | solution.py:47
  43.3 2.1 %collective-permute-start.10 = (bf16[256,512]{1,0:T(8,128)(2,1)S(1)}, bf16[256,512]{1,0:T(8,128)(2,1)S(1)}, u32[]{:S(2)}, u32[]{:S(2)}) collective-permute-start(bf16[256,512]{1,0:T(8,128)(2,1)S(1)} %collective-permute-done.9), channel_id=1, source_target_pairs={{0,1},{1,0},{2,3},{3,2},{4,5},{5,4},{6,7},{7,6},{8,9},{9,8},{10,11... | collective-permute-start | bytes 786440 | tf_op jit(solution)/shard_map/ppermute | solution.py:47
  43.8 1.9 %collective-permute-start.5 = (bf16[256,512]{1,0:T(8,128)(2,1)S(1)}, bf16[256,512]{1,0:T(8,128)(2,1)S(1)}, u32[]{:S(2)}, u32[]{:S(2)}) collective-permute-start(bf16[256,512]{1,0:T(8,128)(2,1)S(1)} %collective-permute-done.4), channel_id=1, source_target_pairs={{0,1},{1,0},{2,3},{3,2},{4,5},{5,4},{6,7},{7,6},{8,9},{9,8},{10,11... | collective-permute-start | bytes 786440 | tf_op jit(solution)/shard_map/ppermute | solution.py:47

commit v3 on v2

--- a/solution.py
+++ b/solution.py
@@ -61,7 +61,9 @@
     right = jnp.where(live[:, None] & live[None, :], right_env[0, 0], jnp.zeros((), BF16))
     same_first = permute(contract(own_same, right), (0, 0, 0), (2, 1, 0))
     flip_first = permute(contract(own_flip, right), (1, 0, 0), (3, 1, 0))
-    same_second = permute(contract(other_same, right), (2, 0, 0), (0, 1, 0))
+    moved_same = contract(other_same, right)
+    same_second = permute(moved_same, (2, 0, 0), (0, 1, 0))
+    other_flip, moved_same = lax.optimization_barrier((other_flip, moved_same))
     moved_last = contract(other_flip, right)
     flip_second = permute(moved_last, (3, 0, 0), (1, 1, 0))
 

time: 47 us -> 42.4 us (0.902)
  the two profiles are of different devices: /device:TPU:7 before, /device:TPU:0 now
where the time goes in v3:
time: 42.4 us; the launch traced here: 42.2 us
  starting transfers between devices  18 us (42%)
  waiting for transfers between devices  14.9 us (35%)
  other arithmetic  4.23 us (10%)
  matrix products  3.62 us (9%)
  local copies, waits for them, and re-layouts  1.16 us (3%)
    ppermute x11, starting transfers between devices, permute(): return lax.ppermute(value, LINE, pairs)  18 us
    ppermute x11, waiting for transfers between devices, permute(): return lax.ppermute(value, LINE, pairs)  14.9 us
    dot_general x4, matrix products, contract(): lax.dot_general(block, right, (((1,), (1,)), ((), ())), preferred_element...  1.77 us
    reduce_sum x2, other arithmetic, take(): return jnp.sum(jnp.where(places == position, values, 0))  1.26 us
    squeeze x1, local copies, waits for them, and re-layouts, two_by_four(): lax.dynamic_index_in_dim(wavefunction[0], 1 - odd, 0, keepdims=False)  1.12 us
    dot_general x4, matrix products, apply_left(): jnp.dot(left[1], over_core(mine), preferred_element_type=F32)  0.96 us
    dot_general x4, matrix products, apply_left(): jnp.dot(left[0], mine, preferred_element_type=F32)  0.89 us
  transfers between devices with their start and end apart: 11, of which 3 were waited for; matrix products, arithmetic and copies ran while one was open for 16% of the time, Pallas kernels for 0%

profile of v3, /device:TPU:0, one launch (start us, length us, event | category | flops | bytes accessed | tf_op | source)
XLA Modules:
  0.0 42.2 jit_solution(17987444444127556021)
XLA Ops:
  0.0 1.1 %dynamic-slice_bitcast_fusion.2 = (bf16[256,512]{1,0:T(8,128)(2,1)S(1)}, bf16[256,512]{1,0:T(8,128)(2,1)S(1)}) fusion(bf16[1,2,256,512]{3,2,1,0:T(8,128)(2,1)} %param.5, s32[]{:T(128)S(6)} %select_n.73, s32[]{:T(128)S(6)} %select_n.74), kind=kLoop, calls=%fused_computation.22 | loop fusion | bytes 1048584 | tf_op jit(solution)/shard_map/jit(dynamic_index_in_dim)/squeeze | solution.py:56
  1.1 3.0 %collective-permute-start.1 = (bf16[256,512]{1,0:T(8,128)(2,1)S(1)}, bf16[256,512]{1,0:T(8,128)(2,1)S(1)}, u32[]{:S(2)}, u32[]{:S(2)}) collective-permute-start(bf16[256,512]{1,0:T(8,128)(2,1)S(1)} %get-tuple-element.14), channel_id=1, source_target_pairs={{0,2},{1,3},{2,0},{3,1},{4,6},{5,7},{6,4},{7,5},{8,10},{9,11},{10,... | collective-permute-start | bytes 786440 | tf_op jit(solution)/shard_map/ppermute | solution.py:47
  4.1 0.6 %fusion.28 = s32[]{:T(128)} fusion(s32[4]{0:T(128)S(1)} %copy-done.2, s32[]{:T(128)S(6)} %axis_index.33), kind=kLoop, calls=%fused_computation.49 | loop fusion | flops 11 | bytes 24 | tf_op jit(solution)/shard_map/reduce_sum | solution.py:22
  4.8 0.6 %iota_compare_fusion = pred[512]{0:T(512)(128)(4,1)S(1)} fusion(s32[]{:T(128)} %fusion.28), kind=kLoop, calls=%fused_computation.35 | loop fusion | flops 512 | bytes 516 | tf_op jit(solution)/shard_map/lt | solution.py:60
  5.4 0.4 %convolution_convert_fusion = bf16[256,512]{1,0:T(8,128)(2,1)S(1)} fusion(bf16[256,512]{1,0:T(8,128)(2,1)S(1)} %get-tuple-element.14, bf16[1,1,512,512]{3,2,1,0:T(8,128)(2,1)S(1)} %copy-done.1, pred[512]{0:T(512)(128)(4,1)S(1)} %iota_compare_fusion), kind=kOutput, calls=%fused_computation.8 | convolution fusion | flops 134873088 | bytes 1049088 | tf_op jit(solution)/shard_map/dot_general | solution.py:26
  5.9 0.7 %collective-permute-start.7 = (bf16[256,512]{1,0:T(8,128)(2,1)S(1)}, bf16[256,512]{1,0:T(8,128)(2,1)S(1)}, u32[]{:S(2)}, u32[]{:S(2)}) collective-permute-start(bf16[256,512]{1,0:T(8,128)(2,1)S(1)} %convolution_convert_fusion), channel_id=1, source_target_pairs={{0,0},{1,1},{2,8},{3,9},{4,4},{5,5},{6,12},{7,13},{8,2},{9,3},{10,... | collective-permute-start | bytes 786440 | tf_op jit(solution)/shard_map/ppermute | solution.py:47
  6.6 5.3 %collective-permute-start = (bf16[256,512]{1,0:T(8,128)(2,1)S(1)}, bf16[256,512]{1,0:T(8,128)(2,1)S(1)}, u32[]{:S(2)}, u32[]{:S(2)}) collective-permute-start(bf16[256,512]{1,0:T(8,128)(2,1)S(1)} %get-tuple-element.13), channel_id=1, source_target_pairs={{0,2},{1,3},{2,0},{3,1},{4,6},{5,7},{6,4},{7,5},{8,10},{9,11},{10,... | collective-permute-start | bytes 786440 | tf_op jit(solution)/shard_map/ppermute | solution.py:47
  11.9 0.4 %convolution_convert_fusion.1 = bf16[256,512]{1,0:T(8,128)(2,1)S(1)} fusion(bf16[256,512]{1,0:T(8,128)(2,1)S(1)} %get-tuple-element.13, bf16[1,1,512,512]{3,2,1,0:T(8,128)(2,1)S(1)} %copy-done.1, pred[512]{0:T(512)(128)(4,1)S(1)} %iota_compare_fusion), kind=kOutput, calls=%fused_computation.9 | convolution fusion | flops 134873088 | bytes 1049088 | tf_op jit(solution)/shard_map/dot_general | solution.py:26
  12.4 1.6 %collective-permute-start.3 = (bf16[256,512]{1,0:T(8,128)(2,1)S(1)}, bf16[256,512]{1,0:T(8,128)(2,1)S(1)}, u32[]{:S(2)}, u32[]{:S(2)}) collective-permute-start(bf16[256,512]{1,0:T(8,128)(2,1)S(1)} %convolution_convert_fusion.1), channel_id=1, source_target_pairs={{0,4},{1,5},{2,12},{3,13},{4,0},{5,1},{6,8},{7,9},{8,6},{9,7},{10,... | collective-permute-start | bytes 786440 | tf_op jit(solution)/shard_map/ppermute | solution.py:47
  14.0 0.6 %fusion.27 = s32[]{:T(128)} fusion(s32[4]{0:T(128)S(1)} %copy-done.3, s32[]{:T(128)S(6)} %axis_index.33), kind=kLoop, calls=%fused_computation.48 | loop fusion | flops 11 | bytes 24 | tf_op jit(solution)/shard_map/reduce_sum | solution.py:22
  14.7 0.4 %convolution_convert_fusion.3 = bf16[256,512]{1,0:T(8,128)(2,1)S(1)} fusion(bf16[256,512]{1,0:T(8,128)(2,1)S(1)} %collective-permute-done.1, bf16[1,1,512,512]{3,2,1,0:T(8,128)(2,1)S(1)} %copy-done.1, pred[512]{0:T(512)(128)(4,1)S(1)} %iota_compare_fusion), kind=kOutput, calls=%fused_computation.11 | convolution fusion | flops 134873088 | bytes 1049088 | tf_op jit(solution)/shard_map/dot_general | solution.py:26
  15.1 1.0 %collective-permute-start.9 = (bf16[256,512]{1,0:T(8,128)(2,1)S(1)}, bf16[256,512]{1,0:T(8,128)(2,1)S(1)}, u32[]{:S(2)}, u32[]{:S(2)}) collective-permute-start(bf16[256,512]{1,0:T(8,128)(2,1)S(1)} %convolution_convert_fusion.3), channel_id=1, source_target_pairs={{0,8},{1,9},{2,0},{3,1},{4,12},{5,13},{6,4},{7,5},{8,10},{9,11},{1... | collective-permute-start | bytes 786440 | tf_op jit(solution)/shard_map/ppermute | solution.py:47
  16.1 2.7 %collective-permute-done = bf16[256,512]{1,0:T(8,128)(2,1)S(1)} collective-permute-done((bf16[256,512]{1,0:T(8,128)(2,1)S(1)}, bf16[256,512]{1,0:T(8,128)(2,1)S(1)}, u32[]{:S(2)}, u32[]{:S(2)}) %collective-permute-start) | collective-permute-done | bytes 262176 | tf_op jit(solution)/shard_map/ppermute | solution.py:47
  18.8 0.4 %convolution_convert_fusion.2 = bf16[256,512]{1,0:T(8,128)(2,1)S(1)} fusion(bf16[256,512]{1,0:T(8,128)(2,1)S(1)} %collective-permute-done, bf16[1,1,512,512]{3,2,1,0:T(8,128)(2,1)S(1)} %copy-done.1, pred[512]{0:T(512)(128)(4,1)S(1)} %iota_compare_fusion), kind=kOutput, calls=%fused_computation.10 | convolution fusion | flops 134873088 | bytes 1049088 | tf_op jit(solution)/shard_map/dot_general | solution.py:26
  19.3 1.8 %collective-permute-start.5 = (bf16[256,512]{1,0:T(8,128)(2,1)S(1)}, bf16[256,512]{1,0:T(8,128)(2,1)S(1)}, u32[]{:S(2)}, u32[]{:S(2)}) collective-permute-start(bf16[256,512]{1,0:T(8,128)(2,1)S(1)} %convolution_convert_fusion.2), channel_id=1, source_target_pairs={{0,12},{1,13},{2,4},{3,5},{4,8},{5,9},{6,0},{7,1},{8,14},{9,15},{1... | collective-permute-start | bytes 786440 | tf_op jit(solution)/shard_map/ppermute | solution.py:47
  21.1 4.0 %collective-permute-start.2 = (bf16[256,512]{1,0:T(8,128)(2,1)S(1)}, bf16[256,512]{1,0:T(8,128)(2,1)S(1)}, u32[]{:S(2)}, u32[]{:S(2)}) collective-permute-start(bf16[256,512]{1,0:T(8,128)(2,1)S(1)} %dynamic-slice_bitcast_fusion), channel_id=1, source_target_pairs={{0,2},{1,3},{2,0},{3,1},{4,6},{5,7},{6,4},{7,5},{8,10},{9,11},{10,... | collective-permute-start | bytes 786440 | tf_op jit(solution)/shard_map/ppermute | solution.py:47
  25.1 0.6 %iota_compare_fusion.1 = pred[512]{0:T(512)(128)(4,1)S(1)} fusion(s32[]{:T(128)} %fusion.27), kind=kLoop, calls=%fused_computation.36 | loop fusion | flops 512 | bytes 516 | tf_op jit(solution)/shard_map/lt | solution.py:75
  25.8 0.7 %add_compare_fusion = pred[256]{0:T(512)(128)(4,1)S(1)} fusion(s32[512]{0:T(512)S(1)} %iota.17, s32[]{:T(128)} %fusion.27, s32[]{:T(128)S(6)} %mul.12), kind=kLoop, calls=%fused_computation.47 | loop fusion | flops 512 | bytes 1288 | tf_op jit(solution)/shard_map/lt | solution.py:74
  26.4 0.1 collective-permute-start.8
  26.5 3.3 %collective-permute-done.3 = bf16[256,512]{1,0:T(8,128)(2,1)S(1)} collective-permute-done((bf16[256,512]{1,0:T(8,128)(2,1)S(1)}, bf16[256,512]{1,0:T(8,128)(2,1)S(1)}, u32[]{:S(2)}, u32[]{:S(2)}) %collective-permute-start.3) | collective-permute-done | bytes 262176 | tf_op jit(solution)/shard_map/ppermute | solution.py:47
  29.8 0.5 %collective-permute-start.10 = (bf16[256,512]{1,0:T(8,128)(2,1)S(1)}, bf16[256,512]{1,0:T(8,128)(2,1)S(1)}, u32[]{:S(2)}, u32[]{:S(2)}) collective-permute-start(bf16[256,512]{1,0:T(8,128)(2,1)S(1)} %collective-permute-done.9), channel_id=1, source_target_pairs={{0,1},{1,0},{2,3},{3,2},{4,5},{5,4},{6,7},{7,6},{8,9},{9,8},{10,11... | collective-permute-start | bytes 786440 | tf_op jit(solution)/shard_map/ppermute | solution.py:47
  30.3 8.9 %collective-permute-done.5 = bf16[256,512]{1,0:T(8,128)(2,1)S(1)} collective-permute-done((bf16[256,512]{1,0:T(8,128)(2,1)S(1)}, bf16[256,512]{1,0:T(8,128)(2,1)S(1)}, u32[]{:S(2)}, u32[]{:S(2)}) %collective-permute-start.5) | collective-permute-done | bytes 262176 | tf_op jit(solution)/shard_map/ppermute | solution.py:47
  39.2 0.2 and_select_fusion.2
  39.4 0.2 fusion.15
  39.6 0.2 fusion.11
  39.9 0.2 convolution_add_fusion.1
  40.1 0.2 fusion.9
  40.3 0.2 fusion.17
  40.6 0.2 convolution_add_fusion.3
  40.8 0.2 fusion.3
  41.1 0.3 select_bitcast_fusion.1
  41.3 0.8 %maximum_bitcast_fusion = bf16[1,2,256,512]{3,2,1,0:T(8,128)(2,1)} fusion(bf16[1,256,512]{2,1,0:T(8,128)(2,1)S(1)} %get-tuple-element.12, bf16[1,256,512]{2,1,0:T(8,128)(2,1)S(1)} %get-tuple-element.11), kind=kLoop, calls=%fused_computation.17 | loop fusion | flops 262144 | bytes 1048576 | tf_op jit(solution)/shard_map/broadcast_in_dim | solution.py:89
  (20 shorter events, 0.1 us)
Async XLA Ops:
  0.0 5.4 %copy-start.1 = (bf16[1,1,512,512]{3,2,1,0:T(8,128)(2,1)S(1)}, bf16[1,1,512,512]{3,2,1,0:T(8,128)(2,1)}, u32[]{:S(2)}) copy-start(bf16[1,1,512,512]{3,2,1,0:T(8,128)(2,1)} %param.7) | copy-start | bytes 1572868
  1.1 3.0 %copy-start.2 = (s32[4]{0:T(128)S(1)}, s32[4]{0:T(128)}, u32[]{:S(2)}) copy-start(s32[4]{0:T(128)} %param.9) | copy-start | bytes 52
  1.1 13.5 %collective-permute-start.1 = (bf16[256,512]{1,0:T(8,128)(2,1)S(1)}, bf16[256,512]{1,0:T(8,128)(2,1)S(1)}, u32[]{:S(2)}, u32[]{:S(2)}) collective-permute-start(bf16[256,512]{1,0:T(8,128)(2,1)S(1)} %get-tuple-element.14), channel_id=1, source_target_pairs={{0,2},{1,3},{2,0},{3,1},{4,6},{5,7},{6,4},{7,5},{8,10},{9,11},{10,... | collective-permute-start | bytes 786440 | tf_op jit(solution)/shard_map/ppermute | solution.py:47
  5.9 20.5 %collective-permute-start.7 = (bf16[256,512]{1,0:T(8,128)(2,1)S(1)}, bf16[256,512]{1,0:T(8,128)(2,1)S(1)}, u32[]{:S(2)}, u32[]{:S(2)}) collective-permute-start(bf16[256,512]{1,0:T(8,128)(2,1)S(1)} %convolution_convert_fusion), channel_id=1, source_target_pairs={{0,0},{1,1},{2,8},{3,9},{4,4},{5,5},{6,12},{7,13},{8,2},{9,3},{10,... | collective-permute-start | bytes 786440 | tf_op jit(solution)/shard_map/ppermute | solution.py:47
  6.6 7.4 %copy-start.3 = (s32[4]{0:T(128)S(1)}, s32[4]{0:T(128)}, u32[]{:S(2)}) copy-start(s32[4]{0:T(128)} %param.8) | copy-start | bytes 52
  6.6 12.2 %collective-permute-start = (bf16[256,512]{1,0:T(8,128)(2,1)S(1)}, bf16[256,512]{1,0:T(8,128)(2,1)S(1)}, u32[]{:S(2)}, u32[]{:S(2)}) collective-permute-start(bf16[256,512]{1,0:T(8,128)(2,1)S(1)} %get-tuple-element.13), channel_id=1, source_target_pairs={{0,2},{1,3},{2,0},{3,1},{4,6},{5,7},{6,4},{7,5},{8,10},{9,11},{10,... | collective-permute-start | bytes 786440 | tf_op jit(solution)/shard_map/ppermute | solution.py:47
  12.4 17.4 %collective-permute-start.3 = (bf16[256,512]{1,0:T(8,128)(2,1)S(1)}, bf16[256,512]{1,0:T(8,128)(2,1)S(1)}, u32[]{:S(2)}, u32[]{:S(2)}) collective-permute-start(bf16[256,512]{1,0:T(8,128)(2,1)S(1)} %convolution_convert_fusion.1), channel_id=1, source_target_pairs={{0,4},{1,5},{2,12},{3,13},{4,0},{5,1},{6,8},{7,9},{8,6},{9,7},{10,... | collective-permute-start | bytes 786440 | tf_op jit(solution)/shard_map/ppermute | solution.py:47
  15.1 5.9 %copy-start = (bf16[1,1,512,512]{3,2,1,0:T(8,128)(2,1)S(1)}, bf16[1,1,512,512]{3,2,1,0:T(8,128)(2,1)}, u32[]{:S(2)}) copy-start(bf16[1,1,512,512]{3,2,1,0:T(8,128)(2,1)} %param.6) | copy-start | bytes 1572868
  15.1 14.7 %collective-permute-start.9 = (bf16[256,512]{1,0:T(8,128)(2,1)S(1)}, bf16[256,512]{1,0:T(8,128)(2,1)S(1)}, u32[]{:S(2)}, u32[]{:S(2)}) collective-permute-start(bf16[256,512]{1,0:T(8,128)(2,1)S(1)} %convolution_convert_fusion.3), channel_id=1, source_target_pairs={{0,8},{1,9},{2,0},{3,1},{4,12},{5,13},{6,4},{7,5},{8,10},{9,11},{1... | collective-permute-start | bytes 786440 | tf_op jit(solution)/shard_map/ppermute | solution.py:47
  19.3 19.9 %collective-permute-start.5 = (bf16[256,512]{1,0:T(8,128)(2,1)S(1)}, bf16[256,512]{1,0:T(8,128)(2,1)S(1)}, u32[]{:S(2)}, u32[]{:S(2)}) collective-permute-start(bf16[256,512]{1,0:T(8,128)(2,1)S(1)} %convolution_convert_fusion.2), channel_id=1, source_target_pairs={{0,12},{1,13},{2,4},{3,5},{4,8},{5,9},{6,0},{7,1},{8,14},{9,15},{1... | collective-permute-start | bytes 786440 | tf_op jit(solution)/shard_map/ppermute | solution.py:47
  21.1 18.1 %collective-permute-start.2 = (bf16[256,512]{1,0:T(8,128)(2,1)S(1)}, bf16[256,512]{1,0:T(8,128)(2,1)S(1)}, u32[]{:S(2)}, u32[]{:S(2)}) collective-permute-start(bf16[256,512]{1,0:T(8,128)(2,1)S(1)} %dynamic-slice_bitcast_fusion), channel_id=1, source_target_pairs={{0,2},{1,3},{2,0},{3,1},{4,6},{5,7},{6,4},{7,5},{8,10},{9,11},{10,... | collective-permute-start | bytes 786440 | tf_op jit(solution)/shard_map/ppermute | solution.py:47
  26.4 13.4 %collective-permute-start.8 = (bf16[256,512]{1,0:T(8,128)(2,1)S(1)}, bf16[256,512]{1,0:T(8,128)(2,1)S(1)}, u32[]{:S(2)}, u32[]{:S(2)}) collective-permute-start(bf16[256,512]{1,0:T(8,128)(2,1)S(1)} %collective-permute-done.7), channel_id=1, source_target_pairs={{0,1},{1,0},{2,3},{3,2},{4,5},{5,4},{6,7},{7,6},{8,9},{9,8},{10,11... | collective-permute-start | bytes 786440 | tf_op jit(solution)/shard_map/ppermute | solution.py:47
  29.8 10.8 %collective-permute-start.4 = (bf16[256,512]{1,0:T(8,128)(2,1)S(1)}, bf16[256,512]{1,0:T(8,128)(2,1)S(1)}, u32[]{:S(2)}, u32[]{:S(2)}) collective-permute-start(bf16[256,512]{1,0:T(8,128)(2,1)S(1)} %collective-permute-done.3), channel_id=1, source_target_pairs={{0,1},{1,0},{2,3},{3,2},{4,5},{5,4},{6,7},{7,6},{8,9},{9,8},{10,11... | collective-permute-start | bytes 786440 | tf_op jit(solution)/shard_map/ppermute | solution.py:47
  29.8 11.0 %collective-permute-start.10 = (bf16[256,512]{1,0:T(8,128)(2,1)S(1)}, bf16[256,512]{1,0:T(8,128)(2,1)S(1)}, u32[]{:S(2)}, u32[]{:S(2)}) collective-permute-start(bf16[256,512]{1,0:T(8,128)(2,1)S(1)} %collective-permute-done.9), channel_id=1, source_target_pairs={{0,1},{1,0},{2,3},{3,2},{4,5},{5,4},{6,7},{7,6},{8,9},{9,8},{10,11... | collective-permute-start | bytes 786440 | tf_op jit(solution)/shard_map/ppermute | solution.py:47
  39.2 1.8 %collective-permute-start.6 = (bf16[256,512]{1,0:T(8,128)(2,1)S(1)}, bf16[256,512]{1,0:T(8,128)(2,1)S(1)}, u32[]{:S(2)}, u32[]{:S(2)}) collective-permute-start(bf16[256,512]{1,0:T(8,128)(2,1)S(1)} %collective-permute-done.5), channel_id=1, source_target_pairs={{0,1},{1,0},{2,3},{3,2},{4,5},{5,4},{6,7},{7,6},{8,9},{9,8},{10,11... | collective-permute-start | bytes 786440 | tf_op jit(solution)/shard_map/ppermute | solution.py:47

commit v4 on v3

--- a/solution.py
+++ b/solution.py
@@ -17,9 +17,9 @@
     return left, right
 
 
-def take(values, position):
-    places = jnp.arange(values.shape[0], dtype=jnp.int32)
-    return jnp.sum(jnp.where(places == position, values, 0))
+def live_states(dims, sector, states):
+    places = jnp.arange(dims.shape[0], dtype=jnp.int32)
+    return jnp.any((places[:, None] == sector) & (states[None, :] < dims[:, None]), axis=0)
 
 
 def contract(block, right):
@@ -57,22 +57,21 @@
     other_same = over_term(own_same)
     other_flip = over_term(own_flip)
 
-    live = states < take(right_dims, z)
+    live = live_states(right_dims, z, states)
     right = jnp.where(live[:, None] & live[None, :], right_env[0, 0], jnp.zeros((), BF16))
     same_first = permute(contract(own_same, right), (0, 0, 0), (2, 1, 0))
-    flip_first = permute(contract(own_flip, right), (1, 0, 0), (3, 1, 0))
     moved_same = contract(other_same, right)
     same_second = permute(moved_same, (2, 0, 0), (0, 1, 0))
-    other_flip, moved_same = lax.optimization_barrier((other_flip, moved_same))
+    own_flip, other_flip, moved_same = lax.optimization_barrier((own_flip, other_flip, moved_same))
+    flip_first = permute(contract(own_flip, right), (1, 0, 0), (3, 1, 0))
     moved_last = contract(other_flip, right)
     flip_second = permute(moved_last, (3, 0, 0), (1, 1, 0))
 
     later_u, moved_last = lax.optimization_barrier((u, moved_last))
     own_rows = lax.dynamic_slice_in_dim(left_env[0, 0], later_u * half, half, 0)
     other_rows = over_term(own_rows)
-    count = take(left_dims, z)
-    rows_live = (u * half + states[:half]) < count
-    cols_live = states < count
+    cols_live = live_states(left_dims, z, states)
+    rows_live = lax.dynamic_slice_in_dim(cols_live, u * half, half)
     lefts = []
     for rows in (jnp.where(at_home, own_rows, other_rows), jnp.where(at_home, other_rows, own_rows)):
         rows = jnp.where(rows_live[:, None] & cols_live[None, :], rows, jnp.zeros((), BF16))
@@ -83,10 +82,14 @@
             left[1], over_core(mine), preferred_element_type=F32
         )
 
-    same = apply_left(lefts[0], same_first) + apply_left(lefts[1], same_second)
-    flip = apply_left(lefts[0], flip_first) + apply_left(lefts[1], flip_second)
-    same, flip = same.astype(BF16), flip.astype(BF16)
-    return jnp.stack([jnp.where(odd == 1, flip, same), jnp.where(odd == 1, same, flip)])[None]
+    same = apply_left(lefts[0], same_first)
+    flip = apply_left(lefts[0], flip_first)
+    same = (same + apply_left(lefts[1], same_second)).astype(BF16)
+    flip, flip_second, same = lax.optimization_barrier((flip, flip_second, same))
+    flip = (flip + apply_left(lefts[1], flip_second)).astype(BF16)
+    product = jnp.zeros((1, 2, half, width), BF16)
+    product = lax.dynamic_update_slice(product, same[None, None], (0, odd, 0, 0))
+    return lax.dynamic_update_slice(product, flip[None, None], (0, 1 - odd, 0, 0))
 
 
 def any_size(wavefunction, left_env, right_env, left_dims, right_dims):

time: 42.4 us -> 40.7 us (0.960)
  other arithmetic: 4.23 us -> 1.05 us
  waiting for transfers between devices: 14.9 us -> 16.2 us
  local copies, waits for them, and re-layouts: 1.16 us -> 1.86 us
    lt x3 -> x0, other arithmetic: 1.95 us -> none  [the longest x1 0.65 us: two_by_four(): rows_live = u * half + states[:half] < count]
    ppermute x11, waiting for transfers between devices: 14.9 us -> 16.2 us  [permute(): return lax.ppermute(value, LINE, pairs)]
    reduce_sum x2 -> x0, other arithmetic: 1.26 us -> none  [take(): return jnp.sum(jnp.where(places == position, values, 0))]
    broadcast_in_dim x1 -> x0, other arithmetic: 0.84 us -> none  [two_by_four(): jnp.stack([jnp.where(odd == 1, flip, same), jnp.where(odd == 1, same, fli...]
    dynamic_update_slice x0 -> x1, other arithmetic: none -> 0.78 us  [two_by_four(): lax.dynamic_update_slice(product, flip[None, None], (0, 1 - odd, 0, 0))]
    unnamed x8 -> x10, local copies, waits for them, and re-layouts: 0.02 us -> 0.58 us
    ppermute x11, starting transfers between devices: 18 us -> 17.6 us  [permute(): return lax.ppermute(value, LINE, pairs)]
  transfers between devices with their start and end apart: 11 -> 11, of which waited for: 3 -> 4; matrix products, arithmetic and copies ran while one was open for 16% -> 9% of each run, Pallas kernels for 0% -> 0%
where the time goes in v4:
time: 40.7 us; the launch traced here: 40.6 us
  starting transfers between devices  17.6 us (43%)
  waiting for transfers between devices  16.2 us (40%)
  matrix products  3.61 us (9%)
  local copies, waits for them, and re-layouts  1.86 us (5%)
  other arithmetic  1.05 us (3%)
    ppermute x11, starting transfers between devices, permute(): return lax.ppermute(value, LINE, pairs)  17.6 us
    ppermute x11, waiting for transfers between devices, permute(): return lax.ppermute(value, LINE, pairs)  16.2 us
    dot_general x4, matrix products, contract(): lax.dot_general(block, right, (((1,), (1,)), ((), ())), preferred_element...  1.8 us
    squeeze x1, local copies, waits for them, and re-layouts, two_by_four(): own_same = lax.dynamic_index_in_dim(wavefunction[0], odd, 0, keepdims=False)  1.12 us
    dot_general x4, matrix products, apply_left(): jnp.dot(left[0], mine, preferred_element_type=F32)  0.91 us
    dot_general x4, matrix products, apply_left(): jnp.dot(left[1], over_core(mine), preferred_element_type=F32)  0.9 us
  transfers between devices with their start and end apart: 11, of which 4 were waited for; matrix products, arithmetic and copies ran while one was open for 9% of the time, Pallas kernels for 0%

profile of v4, /device:TPU:0, one launch (start us, length us, event | category | flops | bytes accessed | tf_op | source)
XLA Modules:
  0.0 40.6 jit_solution(3972368573641762274)
XLA Ops:
  0.0 1.1 %dynamic-slice_bitcast_fusion.1 = (bf16[256,512]{1,0:T(8,128)(2,1)S(1)}, bf16[256,512]{1,0:T(8,128)(2,1)S(1)}) fusion(bf16[1,2,256,512]{3,2,1,0:T(8,128)(2,1)} %param.5, s32[]{:T(128)S(6)} %select_n.58, s32[]{:T(128)S(6)} %select_n.57), kind=kLoop, calls=%fused_computation.23 | loop fusion | bytes 1048584 | tf_op jit(solution)/shard_map/jit(dynamic_index_in_dim)/squeeze | solution.py:55
  1.1 3.0 %collective-permute-start.1 = (bf16[256,512]{1,0:T(8,128)(2,1)S(1)}, bf16[256,512]{1,0:T(8,128)(2,1)S(1)}, u32[]{:S(2)}, u32[]{:S(2)}) collective-permute-start(bf16[256,512]{1,0:T(8,128)(2,1)S(1)} %get-tuple-element.21), channel_id=1, source_target_pairs={{0,2},{1,3},{2,0},{3,1},{4,6},{5,7},{6,4},{7,5},{8,10},{9,11},{10,... | collective-permute-start | bytes 786440 | tf_op jit(solution)/shard_map/ppermute | solution.py:47
  4.1 0.1 collective-permute-start
  4.2 0.5 %copy-done.2 = s32[4]{0:T(128)S(1)} copy-done((s32[4]{0:T(128)S(1)}, s32[4]{0:T(128)}, u32[]{:S(2)}) %copy-start.2) | copy-done | bytes 40
  4.8 0.1 fusion.22
  4.9 0.5 %convolution_convert_fusion = bf16[256,512]{1,0:T(8,128)(2,1)S(1)} fusion(bf16[256,512]{1,0:T(8,128)(2,1)S(1)} %get-tuple-element.21, bf16[1,1,512,512]{3,2,1,0:T(8,128)(2,1)S(1)} %copy-done.4, pred[512]{0:T(512)(128)(4,1)S(1)} %get-tuple-element.18), kind=kOutput, calls=%fused_computation.6 | convolution fusion | flops 134873088 | bytes 1049088 | tf_op jit(solution)/shard_map/dot_general | solution.py:26
  5.4 0.7 %collective-permute-start.6 = (bf16[256,512]{1,0:T(8,128)(2,1)S(1)}, bf16[256,512]{1,0:T(8,128)(2,1)S(1)}, u32[]{:S(2)}, u32[]{:S(2)}) collective-permute-start(bf16[256,512]{1,0:T(8,128)(2,1)S(1)} %convolution_convert_fusion), channel_id=1, source_target_pairs={{0,0},{1,1},{2,8},{3,9},{4,4},{5,5},{6,12},{7,13},{8,2},{9,3},{10,... | collective-permute-start | bytes 786440 | tf_op jit(solution)/shard_map/ppermute | solution.py:47
  6.0 5.9 %collective-permute-done.1 = bf16[256,512]{1,0:T(8,128)(2,1)S(1)} collective-permute-done((bf16[256,512]{1,0:T(8,128)(2,1)S(1)}, bf16[256,512]{1,0:T(8,128)(2,1)S(1)}, u32[]{:S(2)}, u32[]{:S(2)}) %collective-permute-start.1) | collective-permute-done | bytes 262176 | tf_op jit(solution)/shard_map/ppermute | solution.py:47
  12.0 0.4 %convolution_convert_fusion.3 = bf16[256,512]{1,0:T(8,128)(2,1)S(1)} fusion(bf16[256,512]{1,0:T(8,128)(2,1)S(1)} %collective-permute-done.1, bf16[1,1,512,512]{3,2,1,0:T(8,128)(2,1)S(1)} %copy-done.4, pred[512]{0:T(512)(128)(4,1)S(1)} %get-tuple-element.18), kind=kOutput, calls=%fused_computation.9 | convolution fusion | flops 134873088 | bytes 1049088 | tf_op jit(solution)/shard_map/dot_general | solution.py:26
  12.4 8.1 %collective-permute-start.8 = (bf16[256,512]{1,0:T(8,128)(2,1)S(1)}, bf16[256,512]{1,0:T(8,128)(2,1)S(1)}, u32[]{:S(2)}, u32[]{:S(2)}) collective-permute-start(bf16[256,512]{1,0:T(8,128)(2,1)S(1)} %convolution_convert_fusion.3), channel_id=1, source_target_pairs={{0,8},{1,9},{2,0},{3,1},{4,12},{5,13},{6,4},{7,5},{8,10},{9,11},{1... | collective-permute-start | bytes 786440 | tf_op jit(solution)/shard_map/ppermute | solution.py:47
  20.6 0.4 %convolution_convert_fusion.2 = bf16[256,512]{1,0:T(8,128)(2,1)S(1)} fusion(bf16[256,512]{1,0:T(8,128)(2,1)S(1)} %collective-permute-done, bf16[1,1,512,512]{3,2,1,0:T(8,128)(2,1)S(1)} %copy-done.4, pred[512]{0:T(512)(128)(4,1)S(1)} %get-tuple-element.18), kind=kOutput, calls=%fused_computation.8 | convolution fusion | flops 134873088 | bytes 1049088 | tf_op jit(solution)/shard_map/dot_general | solution.py:26
  21.0 0.5 %convolution_convert_fusion.1 = bf16[256,512]{1,0:T(8,128)(2,1)S(1)} fusion(bf16[256,512]{1,0:T(8,128)(2,1)S(1)} %get-tuple-element.13, bf16[1,1,512,512]{3,2,1,0:T(8,128)(2,1)S(1)} %copy-done.4, pred[512]{0:T(512)(128)(4,1)S(1)} %get-tuple-element.18), kind=kOutput, calls=%fused_computation.7 | convolution fusion | flops 134873088 | bytes 1049088 | tf_op jit(solution)/shard_map/dot_general | solution.py:26
  21.5 2.0 %collective-permute-start.3 = (bf16[256,512]{1,0:T(8,128)(2,1)S(1)}, bf16[256,512]{1,0:T(8,128)(2,1)S(1)}, u32[]{:S(2)}, u32[]{:S(2)}) collective-permute-start(bf16[256,512]{1,0:T(8,128)(2,1)S(1)} %convolution_convert_fusion.1), channel_id=1, source_target_pairs={{0,4},{1,5},{2,12},{3,13},{4,0},{5,1},{6,8},{7,9},{8,6},{9,7},{10,... | collective-permute-start | bytes 786440 | tf_op jit(solution)/shard_map/ppermute | solution.py:47
  23.5 0.1 collective-permute-start.2
  23.6 0.1 dynamic_slice.27
  23.7 3.0 %collective-permute-start.5 = (bf16[256,512]{1,0:T(8,128)(2,1)S(1)}, bf16[256,512]{1,0:T(8,128)(2,1)S(1)}, u32[]{:S(2)}, u32[]{:S(2)}) collective-permute-start(bf16[256,512]{1,0:T(8,128)(2,1)S(1)} %convolution_convert_fusion.2), channel_id=1, source_target_pairs={{0,12},{1,13},{2,4},{3,5},{4,8},{5,9},{6,0},{7,1},{8,14},{9,15},{1... | collective-permute-start | bytes 786440 | tf_op jit(solution)/shard_map/ppermute | solution.py:47
  26.7 0.5 %collective-permute-start.9 = (bf16[256,512]{1,0:T(8,128)(2,1)S(1)}, bf16[256,512]{1,0:T(8,128)(2,1)S(1)}, u32[]{:S(2)}, u32[]{:S(2)}) collective-permute-start(bf16[256,512]{1,0:T(8,128)(2,1)S(1)} %collective-permute-done.8), channel_id=1, source_target_pairs={{0,1},{1,0},{2,3},{3,2},{4,5},{5,4},{6,7},{7,6},{8,9},{9,8},{10,11... | collective-permute-start | bytes 786440 | tf_op jit(solution)/shard_map/ppermute | solution.py:47
  27.2 6.7 %collective-permute-done.3 = bf16[256,512]{1,0:T(8,128)(2,1)S(1)} collective-permute-done((bf16[256,512]{1,0:T(8,128)(2,1)S(1)}, bf16[256,512]{1,0:T(8,128)(2,1)S(1)}, u32[]{:S(2)}, u32[]{:S(2)}) %collective-permute-start.3) | collective-permute-done | bytes 262176 | tf_op jit(solution)/shard_map/ppermute | solution.py:47
  33.9 0.0 collective-permute-start.4
  33.9 2.2 %collective-permute-done.2 = bf16[256,512]{1,0:T(8,128)(2,1)S(1)} collective-permute-done((bf16[256,512]{1,0:T(8,128)(2,1)S(1)}, bf16[256,512]{1,0:T(8,128)(2,1)S(1)}, u32[]{:S(2)}, u32[]{:S(2)}) %collective-permute-start.2) | collective-permute-done | bytes 262176 | tf_op jit(solution)/shard_map/ppermute | solution.py:47
  36.1 0.2 and_select_fusion.2
  36.3 0.2 fusion.17
  36.5 0.2 convolution_add_fusion.2
  36.8 0.2 fusion.19
  37.0 0.2 fusion.13
  37.2 0.2 convolution_add_fusion.3
  37.5 0.2 fusion.1
  37.7 0.1 collective-permute-start.10
  37.9 1.4 %collective-permute-done.10 = bf16[256,512]{1,0:T(8,128)(2,1)S(1)} collective-permute-done((bf16[256,512]{1,0:T(8,128)(2,1)S(1)}, bf16[256,512]{1,0:T(8,128)(2,1)S(1)}, u32[]{:S(2)}, u32[]{:S(2)}) %collective-permute-start.10) | collective-permute-done | bytes 262176 | tf_op jit(solution)/shard_map/ppermute | solution.py:47
  39.3 0.2 fusion.9
  39.5 0.2 convolution_add_fusion
  39.8 0.8 %fusion.7 = bf16[1,2,256,512]{3,2,1,0:T(8,128)(2,1)} fusion(bf16[1,2,256,512]{3,2,1,0:T(8,128)(2,1)} %copy-done, s32[]{:T(128)S(6)} %select_n.57, f32[256,512]{1,0:T(8,128)S(1)} %convolution_add_fusion.3, f32[256,512]{1,0:T(8,128)S(1)} %convolution_add_fusion), kind=kLoop, calls=%fused_computation.19 | loop fusion | flops 262144 | bytes 1310724 | tf_op jit(solution)/shard_map/dynamic_update_slice | solution.py:92
  (21 shorter events, 0.1 us)
Async XLA Ops:
  0.0 4.9 %copy-start.4 = (bf16[1,1,512,512]{3,2,1,0:T(8,128)(2,1)S(1)}, bf16[1,1,512,512]{3,2,1,0:T(8,128)(2,1)}, u32[]{:S(2)}) copy-start(bf16[1,1,512,512]{3,2,1,0:T(8,128)(2,1)} %param.7) | copy-start | bytes 1572868
  1.1 10.8 %collective-permute-start.1 = (bf16[256,512]{1,0:T(8,128)(2,1)S(1)}, bf16[256,512]{1,0:T(8,128)(2,1)S(1)}, u32[]{:S(2)}, u32[]{:S(2)}) collective-permute-start(bf16[256,512]{1,0:T(8,128)(2,1)S(1)} %get-tuple-element.21), channel_id=1, source_target_pairs={{0,2},{1,3},{2,0},{3,1},{4,6},{5,7},{6,4},{7,5},{8,10},{9,11},{10,... | collective-permute-start | bytes 786440 | tf_op jit(solution)/shard_map/ppermute | solution.py:47
  4.1 0.7 %copy-start.2 = (s32[4]{0:T(128)S(1)}, s32[4]{0:T(128)}, u32[]{:S(2)}) copy-start(s32[4]{0:T(128)} %param.8) | copy-start | bytes 52
  4.1 0.7 %copy-start.3 = (s32[4]{0:T(128)S(1)}, s32[4]{0:T(128)}, u32[]{:S(2)}) copy-start(s32[4]{0:T(128)} %param.9) | copy-start | bytes 52
  4.1 16.4 %collective-permute-start = (bf16[256,512]{1,0:T(8,128)(2,1)S(1)}, bf16[256,512]{1,0:T(8,128)(2,1)S(1)}, u32[]{:S(2)}, u32[]{:S(2)}) collective-permute-start(bf16[256,512]{1,0:T(8,128)(2,1)S(1)} %get-tuple-element.13), channel_id=1, source_target_pairs={{0,2},{1,3},{2,0},{3,1},{4,6},{5,7},{6,4},{7,5},{8,10},{9,11},{10,... | collective-permute-start | bytes 786440 | tf_op jit(solution)/shard_map/ppermute | solution.py:47
  5.4 21.3 %collective-permute-start.6 = (bf16[256,512]{1,0:T(8,128)(2,1)S(1)}, bf16[256,512]{1,0:T(8,128)(2,1)S(1)}, u32[]{:S(2)}, u32[]{:S(2)}) collective-permute-start(bf16[256,512]{1,0:T(8,128)(2,1)S(1)} %convolution_convert_fusion), channel_id=1, source_target_pairs={{0,0},{1,1},{2,8},{3,9},{4,4},{5,5},{6,12},{7,13},{8,2},{9,3},{10,... | collective-permute-start | bytes 786440 | tf_op jit(solution)/shard_map/ppermute | solution.py:47
  12.4 14.3 %collective-permute-start.8 = (bf16[256,512]{1,0:T(8,128)(2,1)S(1)}, bf16[256,512]{1,0:T(8,128)(2,1)S(1)}, u32[]{:S(2)}, u32[]{:S(2)}) collective-permute-start(bf16[256,512]{1,0:T(8,128)(2,1)S(1)} %convolution_convert_fusion.3), channel_id=1, source_target_pairs={{0,8},{1,9},{2,0},{3,1},{4,12},{5,13},{6,4},{7,5},{8,10},{9,11},{1... | collective-permute-start | bytes 786440 | tf_op jit(solution)/shard_map/ppermute | solution.py:47
  21.0 2.5 %copy-start.1 = (bf16[1,1,512,512]{3,2,1,0:T(8,128)(2,1)S(1)}, bf16[1,1,512,512]{3,2,1,0:T(8,128)(2,1)}, u32[]{:S(2)}) copy-start(bf16[1,1,512,512]{3,2,1,0:T(8,128)(2,1)} %param.6) | copy-start | bytes 1572868
  21.5 12.4 %collective-permute-start.3 = (bf16[256,512]{1,0:T(8,128)(2,1)S(1)}, bf16[256,512]{1,0:T(8,128)(2,1)S(1)}, u32[]{:S(2)}, u32[]{:S(2)}) collective-permute-start(bf16[256,512]{1,0:T(8,128)(2,1)S(1)} %convolution_convert_fusion.1), channel_id=1, source_target_pairs={{0,4},{1,5},{2,12},{3,13},{4,0},{5,1},{6,8},{7,9},{8,6},{9,7},{10,... | collective-permute-start | bytes 786440 | tf_op jit(solution)/shard_map/ppermute | solution.py:47
  23.5 12.6 %collective-permute-start.2 = (bf16[256,512]{1,0:T(8,128)(2,1)S(1)}, bf16[256,512]{1,0:T(8,128)(2,1)S(1)}, u32[]{:S(2)}, u32[]{:S(2)}) collective-permute-start(bf16[256,512]{1,0:T(8,128)(2,1)S(1)} %dynamic-slice_bitcast_fusion), channel_id=1, source_target_pairs={{0,2},{1,3},{2,0},{3,1},{4,6},{5,7},{6,4},{7,5},{8,10},{9,11},{10,... | collective-permute-start | bytes 786440 | tf_op jit(solution)/shard_map/ppermute | solution.py:47
  23.7 14.0 %collective-permute-start.5 = (bf16[256,512]{1,0:T(8,128)(2,1)S(1)}, bf16[256,512]{1,0:T(8,128)(2,1)S(1)}, u32[]{:S(2)}, u32[]{:S(2)}) collective-permute-start(bf16[256,512]{1,0:T(8,128)(2,1)S(1)} %convolution_convert_fusion.2), channel_id=1, source_target_pairs={{0,12},{1,13},{2,4},{3,5},{4,8},{5,9},{6,0},{7,1},{8,14},{9,15},{1... | collective-permute-start | bytes 786440 | tf_op jit(solution)/shard_map/ppermute | solution.py:47
  26.7 9.8 %collective-permute-start.7 = (bf16[256,512]{1,0:T(8,128)(2,1)S(1)}, bf16[256,512]{1,0:T(8,128)(2,1)S(1)}, u32[]{:S(2)}, u32[]{:S(2)}) collective-permute-start(bf16[256,512]{1,0:T(8,128)(2,1)S(1)} %collective-permute-done.6), channel_id=1, source_target_pairs={{0,1},{1,0},{2,3},{3,2},{4,5},{5,4},{6,7},{7,6},{8,9},{9,8},{10,11... | collective-permute-start | bytes 786440 | tf_op jit(solution)/shard_map/ppermute | solution.py:47
  26.7 10.8 %collective-permute-start.9 = (bf16[256,512]{1,0:T(8,128)(2,1)S(1)}, bf16[256,512]{1,0:T(8,128)(2,1)S(1)}, u32[]{:S(2)}, u32[]{:S(2)}) collective-permute-start(bf16[256,512]{1,0:T(8,128)(2,1)S(1)} %collective-permute-done.8), channel_id=1, source_target_pairs={{0,1},{1,0},{2,3},{3,2},{4,5},{5,4},{6,7},{7,6},{8,9},{9,8},{10,11... | collective-permute-start | bytes 786440 | tf_op jit(solution)/shard_map/ppermute | solution.py:47
  33.9 3.3 %collective-permute-start.4 = (bf16[256,512]{1,0:T(8,128)(2,1)S(1)}, bf16[256,512]{1,0:T(8,128)(2,1)S(1)}, u32[]{:S(2)}, u32[]{:S(2)}) collective-permute-start(bf16[256,512]{1,0:T(8,128)(2,1)S(1)} %collective-permute-done.3), channel_id=1, source_target_pairs={{0,1},{1,0},{2,3},{3,2},{4,5},{5,4},{6,7},{7,6},{8,9},{9,8},{10,11... | collective-permute-start | bytes 786440 | tf_op jit(solution)/shard_map/ppermute | solution.py:47
  37.7 1.6 %collective-permute-start.10 = (bf16[256,512]{1,0:T(8,128)(2,1)S(1)}, bf16[256,512]{1,0:T(8,128)(2,1)S(1)}, u32[]{:S(2)}, u32[]{:S(2)}) collective-permute-start(bf16[256,512]{1,0:T(8,128)(2,1)S(1)} %collective-permute-done.5), channel_id=1, source_target_pairs={{0,1},{1,0},{2,3},{3,2},{4,5},{5,4},{6,7},{7,6},{8,9},{9,8},{10,11... | collective-permute-start | bytes 786440 | tf_op jit(solution)/shard_map/ppermute | solution.py:47
  37.9 1.9 %copy-start = (bf16[1,2,256,512]{3,2,1,0:T(8,128)(2,1)}, bf16[1,2,256,512]{3,2,1,0:T(8,128)(2,1)S(1)}, u32[]{:S(2)}) copy-start(bf16[1,2,256,512]{3,2,1,0:T(8,128)(2,1)S(1)} %bitcast_dynamic-update-slice_fusion) | copy-start | bytes 1572868

commit v5 on v4

--- a/solution.py
+++ b/solution.py
@@ -41,7 +41,10 @@
         pairs = []
         for zz in range(sectors):
             for tt in range(terms):
-                flip_sector, flip_term, flip_sub = home if zz // 2 == tt else away
+                flips = home if zz // 2 == tt else away
+                if flips is None:
+                    continue
+                flip_sector, flip_term, flip_sub = flips
                 for uu in range(subs):
                     pairs.append((index(zz, tt, uu), index(zz ^ flip_sector, tt ^ flip_term, uu ^ flip_sub)))
         return lax.ppermute(value, LINE, pairs)
@@ -54,22 +57,27 @@
 
     own_same = lax.dynamic_index_in_dim(wavefunction[0], odd, 0, keepdims=False)
     own_flip = lax.dynamic_index_in_dim(wavefunction[0], 1 - odd, 0, keepdims=False)
-    other_same = over_term(own_same)
-    other_flip = over_term(own_flip)
-
+    other_same = permute(own_same, (0, 1, 0), (0, 1, 0))
+    second_flip = own_flip
+    other_flip = permute(second_flip, (0, 1, 0), (0, 1, 0))
     live = live_states(right_dims, z, states)
     right = jnp.where(live[:, None] & live[None, :], right_env[0, 0], jnp.zeros((), BF16))
-    same_first = permute(contract(own_same, right), (0, 0, 0), (2, 1, 0))
+    moved_first = contract(own_same, right)
+    same_first = permute(moved_first, (0, 0, 0), (2, 1, 0))
+    other_same, _ = lax.optimization_barrier((other_same, moved_first))
     moved_same = contract(other_same, right)
     same_second = permute(moved_same, (2, 0, 0), (0, 1, 0))
-    own_flip, other_flip, moved_same = lax.optimization_barrier((own_flip, other_flip, moved_same))
-    flip_first = permute(contract(own_flip, right), (1, 0, 0), (3, 1, 0))
+    later_u = u
+    later_u, _ = lax.optimization_barrier((later_u, moved_same))
+    own_rows = lax.dynamic_slice_in_dim(left_env[0, 0], later_u * half, half, 0)
+    other_rows = over_term(own_rows)
+    early_flip, own_rows = lax.optimization_barrier((own_flip, own_rows))
+    early_flip, _ = lax.optimization_barrier((early_flip, moved_same))
+    moved_flip = contract(early_flip, right)
+    flip_first = permute(moved_flip, (1, 0, 0), (3, 1, 0))
+    other_flip, _, _ = lax.optimization_barrier((other_flip, moved_same, moved_flip))
     moved_last = contract(other_flip, right)
     flip_second = permute(moved_last, (3, 0, 0), (1, 1, 0))
-
-    later_u, moved_last = lax.optimization_barrier((u, moved_last))
-    own_rows = lax.dynamic_slice_in_dim(left_env[0, 0], later_u * half, half, 0)
-    other_rows = over_term(own_rows)
     cols_live = live_states(left_dims, z, states)
     rows_live = lax.dynamic_slice_in_dim(cols_live, u * half, half)
     lefts = []

time: 40.7 us -> 39.7 us (0.975)
  waiting for transfers between devices: 16.2 us -> 8.86 us
  starting transfers between devices: 17.6 us -> 23.8 us
  matrix products: 3.61 us -> 4.3 us
  local copies, waits for them, and re-layouts: 1.86 us -> 1.33 us
    ppermute x11, waiting for transfers between devices: 16.2 us -> 8.86 us  [permute(): return lax.ppermute(value, LINE, pairs)]
    ppermute x11, starting transfers between devices: 17.6 us -> 23.8 us  [permute(): return lax.ppermute(value, LINE, pairs)]
    dot_general x4, matrix products: 1.8 us -> 2.5 us  [contract(): lax.dot_general(block, right, (((1,), (1,)), ((), ())), preferred_element...]
    unnamed x10, local copies, waits for them, and re-layouts: 0.58 us -> 0.03 us
  transfers between devices with their start and end apart: 11 -> 11, of which waited for: 4 -> 6; matrix products, arithmetic and copies ran while one was open for 9% -> 11% of each run, Pallas kernels for 0% -> 0%
where the time goes in v5:
time: 39.7 us; the launch traced here: 39.5 us
  starting transfers between devices  23.8 us (60%)
  waiting for transfers between devices  8.86 us (22%)
  matrix products  4.3 us (11%)
  local copies, waits for them, and re-layouts  1.33 us (3%)
  other arithmetic  1.06 us (3%)
    ppermute x11, starting transfers between devices, permute(): return lax.ppermute(value, LINE, pairs)  23.8 us
    ppermute x11, waiting for transfers between devices, permute(): return lax.ppermute(value, LINE, pairs)  8.86 us
    dot_general x4, matrix products, contract(): lax.dot_general(block, right, (((1,), (1,)), ((), ())), preferred_element...  2.5 us
    squeeze x1, local copies, waits for them, and re-layouts, two_by_four(): own_same = lax.dynamic_index_in_dim(wavefunction[0], odd, 0, keepdims=False)  1.15 us
    dot_general x4, matrix products, apply_left(): jnp.dot(left[1], over_core(mine), preferred_element_type=F32)  0.91 us
    dot_general x4, matrix products, apply_left(): jnp.dot(left[0], mine, preferred_element_type=F32)  0.9 us
  transfers between devices with their start and end apart: 11, of which 6 were waited for; matrix products, arithmetic and copies ran while one was open for 11% of the time, Pallas kernels for 0%

profile of v5, /device:TPU:0, one launch (start us, length us, event | category | flops | bytes accessed | tf_op | source)
XLA Modules:
  0.0 39.5 jit_solution(365809444077244011)
XLA Ops:
  0.0 1.2 %dynamic-slice_bitcast_fusion.1 = (bf16[256,512]{1,0:T(8,128)(2,1)S(1)}, bf16[256,512]{1,0:T(8,128)(2,1)S(1)}) fusion(bf16[1,2,256,512]{3,2,1,0:T(8,128)(2,1)} %param.5, s32[]{:T(128)S(6)} %select_n.58, s32[]{:T(128)S(6)} %select_n.57), kind=kLoop, calls=%fused_computation.23 | loop fusion | bytes 1048584 | tf_op jit(solution)/shard_map/jit(dynamic_index_in_dim)/squeeze | solution.py:58
  1.2 0.0 copy-start.2
  1.2 0.0 copy-start.3
  1.2 3.0 %collective-permute-start = (bf16[256,512]{1,0:T(8,128)(2,1)S(1)}, bf16[256,512]{1,0:T(8,128)(2,1)S(1)}, u32[]{:S(2)}, u32[]{:S(2)}) collective-permute-start(bf16[256,512]{1,0:T(8,128)(2,1)S(1)} %get-tuple-element.27), channel_id=1, source_target_pairs={{0,2},{1,3},{2,0},{3,1},{4,6},{5,7},{6,4},{7,5},{8,10},{9,11},{10,... | collective-permute-start | bytes 786440 | tf_op jit(solution)/shard_map/ppermute | solution.py:50
  4.2 0.1 fusion.22
  4.3 0.5 %convolution_convert_fusion.3 = bf16[256,512]{1,0:T(8,128)(2,1)S(1)} fusion(bf16[256,512]{1,0:T(8,128)(2,1)S(1)} %get-tuple-element.27, bf16[1,1,512,512]{3,2,1,0:T(8,128)(2,1)S(1)} %copy-done.4, pred[512]{0:T(512)(128)(4,1)S(1)} %get-tuple-element.24), kind=kOutput, calls=%fused_computation.9 | convolution fusion | flops 134873088 | bytes 1049088 | tf_op jit(solution)/shard_map/dot_general | solution.py:26
  4.8 0.7 %collective-permute-start.6 = (bf16[256,512]{1,0:T(8,128)(2,1)S(1)}, bf16[256,512]{1,0:T(8,128)(2,1)S(1)}, u32[]{:S(2)}, u32[]{:S(2)}) collective-permute-start(bf16[256,512]{1,0:T(8,128)(2,1)S(1)} %convolution_convert_fusion.3), channel_id=1, source_target_pairs={{0,0},{1,1},{2,8},{3,9},{4,4},{5,5},{6,12},{7,13},{8,2},{9,3},{10,... | collective-permute-start | bytes 786440 | tf_op jit(solution)/shard_map/ppermute | solution.py:50
  5.4 5.3 %collective-permute-start.4 = (bf16[256,512]{1,0:T(8,128)(2,1)S(1)}, bf16[256,512]{1,0:T(8,128)(2,1)S(1)}, u32[]{:S(2)}, u32[]{:S(2)}) collective-permute-start(bf16[256,512]{1,0:T(8,128)(2,1)S(1)} %get-tuple-element.18), channel_id=1, source_target_pairs={{0,2},{1,3},{2,0},{3,1},{4,6},{5,7},{6,4},{7,5},{8,10},{9,11},{10,... | collective-permute-start | bytes 786440 | tf_op jit(solution)/shard_map/ppermute | solution.py:50
  10.8 0.7 %collective-permute-done = bf16[256,512]{1,0:T(8,128)(2,1)S(1)} collective-permute-done((bf16[256,512]{1,0:T(8,128)(2,1)S(1)}, bf16[256,512]{1,0:T(8,128)(2,1)S(1)}, u32[]{:S(2)}, u32[]{:S(2)}) %collective-permute-start) | collective-permute-done | bytes 262176 | tf_op jit(solution)/shard_map/ppermute | solution.py:50
  11.5 0.4 %convolution_convert_fusion.2 = bf16[256,512]{1,0:T(8,128)(2,1)S(1)} fusion(bf16[256,512]{1,0:T(8,128)(2,1)S(1)} %collective-permute-done, bf16[1,1,512,512]{3,2,1,0:T(8,128)(2,1)S(1)} %copy-done.4, pred[512]{0:T(512)(128)(4,1)S(1)} %get-tuple-element.24), kind=kOutput, calls=%fused_computation.8 | convolution fusion | flops 134873088 | bytes 1049088 | tf_op jit(solution)/shard_map/dot_general | solution.py:26
  11.9 8.7 %collective-permute-start.8 = (bf16[256,512]{1,0:T(8,128)(2,1)S(1)}, bf16[256,512]{1,0:T(8,128)(2,1)S(1)}, u32[]{:S(2)}, u32[]{:S(2)}) collective-permute-start(bf16[256,512]{1,0:T(8,128)(2,1)S(1)} %convolution_convert_fusion.2), channel_id=1, source_target_pairs={{0,8},{1,9},{2,0},{3,1},{4,12},{5,13},{6,4},{7,5},{8,10},{9,11},{1... | collective-permute-start | bytes 786440 | tf_op jit(solution)/shard_map/ppermute | solution.py:50
  20.6 1.2 %convolution_convert_fusion.1 = bf16[256,512]{1,0:T(8,128)(2,1)} fusion(bf16[256,512]{1,0:T(8,128)(2,1)S(1)} %get-tuple-element.18, bf16[1,1,512,512]{3,2,1,0:T(8,128)(2,1)S(1)} %copy-done.4, pred[512]{0:T(512)(128)(4,1)S(1)} %get-tuple-element.24), kind=kOutput, calls=%fused_computation.7 | convolution fusion | flops 134873088 | bytes 1049088 | tf_op jit(solution)/shard_map/dot_general | solution.py:26
  21.8 0.1 dynamic_slice.27
  21.9 5.0 %collective-permute-done.4 = bf16[256,512]{1,0:T(8,128)(2,1)S(1)} collective-permute-done((bf16[256,512]{1,0:T(8,128)(2,1)S(1)}, bf16[256,512]{1,0:T(8,128)(2,1)S(1)}, u32[]{:S(2)}, u32[]{:S(2)}) %collective-permute-start.4) | collective-permute-done | bytes 262176 | tf_op jit(solution)/shard_map/ppermute | solution.py:50
  26.9 0.4 %convolution_convert_fusion = bf16[256,512]{1,0:T(8,128)(2,1)S(1)} fusion(bf16[256,512]{1,0:T(8,128)(2,1)S(1)} %collective-permute-done.4, bf16[1,1,512,512]{3,2,1,0:T(8,128)(2,1)S(1)} %copy-done.4, pred[512]{0:T(512)(128)(4,1)S(1)} %get-tuple-element.24), kind=kOutput, calls=%fused_computation.6 | convolution fusion | flops 134873088 | bytes 1049088 | tf_op jit(solution)/shard_map/dot_general | solution.py:26
  27.3 5.5 %collective-permute-start.5 = (bf16[256,512]{1,0:T(8,128)(2,1)S(1)}, bf16[256,512]{1,0:T(8,128)(2,1)S(1)}, u32[]{:S(2)}, u32[]{:S(2)}) collective-permute-start(bf16[256,512]{1,0:T(8,128)(2,1)S(1)} %convolution_convert_fusion), channel_id=1, source_target_pairs={{0,12},{1,13},{2,4},{3,5},{4,8},{5,9},{6,0},{7,1},{8,14},{9,15},{1... | collective-permute-start | bytes 786440 | tf_op jit(solution)/shard_map/ppermute | solution.py:50
  32.9 0.5 %collective-permute-start.9 = (bf16[256,512]{1,0:T(8,128)(2,1)S(1)}, bf16[256,512]{1,0:T(8,128)(2,1)S(1)}, u32[]{:S(2)}, u32[]{:S(2)}) collective-permute-start(bf16[256,512]{1,0:T(8,128)(2,1)S(1)} %collective-permute-done.8), channel_id=1, source_target_pairs={{0,1},{1,0},{2,3},{3,2},{4,5},{5,4},{6,7},{7,6},{8,9},{9,8},{10,11... | collective-permute-start | bytes 786440 | tf_op jit(solution)/shard_map/ppermute | solution.py:50
  33.4 0.1 collective-permute-start.3
  33.4 0.2 and_select_fusion.2
  33.6 0.2 fusion.17
  33.9 0.5 %collective-permute-done.7 = bf16[256,512]{1,0:T(8,128)(2,1)S(1)} collective-permute-done((bf16[256,512]{1,0:T(8,128)(2,1)S(1)}, bf16[256,512]{1,0:T(8,128)(2,1)S(1)}, u32[]{:S(2)}, u32[]{:S(2)}) %collective-permute-start.7) | collective-permute-done | bytes 262176 | tf_op jit(solution)/shard_map/ppermute | solution.py:50
  34.4 0.2 convolution_add_fusion.2
  34.6 0.2 fusion.19
  34.9 0.2 fusion.13
  35.1 0.1 collective-permute-done.3
  35.1 0.2 convolution_add_fusion.3
  35.4 0.2 fusion.1
  35.6 1.1 %collective-permute-done.5 = bf16[256,512]{1,0:T(8,128)(2,1)S(1)} collective-permute-done((bf16[256,512]{1,0:T(8,128)(2,1)S(1)}, bf16[256,512]{1,0:T(8,128)(2,1)S(1)}, u32[]{:S(2)}, u32[]{:S(2)}) %collective-permute-start.5) | collective-permute-done | bytes 262176 | tf_op jit(solution)/shard_map/ppermute | solution.py:50
  36.8 1.4 %collective-permute-done.10 = bf16[256,512]{1,0:T(8,128)(2,1)S(1)} collective-permute-done((bf16[256,512]{1,0:T(8,128)(2,1)S(1)}, bf16[256,512]{1,0:T(8,128)(2,1)S(1)}, u32[]{:S(2)}, u32[]{:S(2)}) %collective-permute-start.10) | collective-permute-done | bytes 262176 | tf_op jit(solution)/shard_map/ppermute | solution.py:50
  38.3 0.2 fusion.9
  38.5 0.2 convolution_add_fusion
  38.8 0.8 %fusion.7 = bf16[1,2,256,512]{3,2,1,0:T(8,128)(2,1)} fusion(bf16[1,2,256,512]{3,2,1,0:T(8,128)(2,1)} %copy-done.1, s32[]{:T(128)S(6)} %select_n.57, f32[256,512]{1,0:T(8,128)S(1)} %convolution_add_fusion.3, f32[256,512]{1,0:T(8,128)S(1)} %convolution_add_fusion), kind=kLoop, calls=%fused_computation.19 | loop fusion | flops 262144 | bytes 1310724 | tf_op jit(solution)/shard_map/dynamic_update_slice | solution.py:100
  (21 shorter events, 0.1 us)
Async XLA Ops:
  0.0 20.6 %copy-start = (bf16[1,1,512,512]{3,2,1,0:T(8,128)(2,1)S(1)}, bf16[1,1,512,512]{3,2,1,0:T(8,128)(2,1)}, u32[]{:S(2)}) copy-start(bf16[1,1,512,512]{3,2,1,0:T(8,128)(2,1)} %param.6) | copy-start | bytes 1572868
  0.0 4.3 %copy-start.4 = (bf16[1,1,512,512]{3,2,1,0:T(8,128)(2,1)S(1)}, bf16[1,1,512,512]{3,2,1,0:T(8,128)(2,1)}, u32[]{:S(2)}) copy-start(bf16[1,1,512,512]{3,2,1,0:T(8,128)(2,1)} %param.7) | copy-start | bytes 1572868
  1.2 3.0 %copy-start.2 = (s32[4]{0:T(128)S(1)}, s32[4]{0:T(128)}, u32[]{:S(2)}) copy-start(s32[4]{0:T(128)} %param.8) | copy-start | bytes 52
  1.2 3.0 %copy-start.3 = (s32[4]{0:T(128)S(1)}, s32[4]{0:T(128)}, u32[]{:S(2)}) copy-start(s32[4]{0:T(128)} %param.9) | copy-start | bytes 52
  1.2 10.3 %collective-permute-start = (bf16[256,512]{1,0:T(8,128)(2,1)S(1)}, bf16[256,512]{1,0:T(8,128)(2,1)S(1)}, u32[]{:S(2)}, u32[]{:S(2)}) collective-permute-start(bf16[256,512]{1,0:T(8,128)(2,1)S(1)} %get-tuple-element.27), channel_id=1, source_target_pairs={{0,2},{1,3},{2,0},{3,1},{4,6},{5,7},{6,4},{7,5},{8,10},{9,11},{10,... | collective-permute-start | bytes 786440 | tf_op jit(solution)/shard_map/ppermute | solution.py:50
  4.8 28.1 %collective-permute-start.6 = (bf16[256,512]{1,0:T(8,128)(2,1)S(1)}, bf16[256,512]{1,0:T(8,128)(2,1)S(1)}, u32[]{:S(2)}, u32[]{:S(2)}) collective-permute-start(bf16[256,512]{1,0:T(8,128)(2,1)S(1)} %convolution_convert_fusion.3), channel_id=1, source_target_pairs={{0,0},{1,1},{2,8},{3,9},{4,4},{5,5},{6,12},{7,13},{8,2},{9,3},{10,... | collective-permute-start | bytes 786440 | tf_op jit(solution)/shard_map/ppermute | solution.py:50
  5.4 21.4 %collective-permute-start.4 = (bf16[256,512]{1,0:T(8,128)(2,1)S(1)}, bf16[256,512]{1,0:T(8,128)(2,1)S(1)}, u32[]{:S(2)}, u32[]{:S(2)}) collective-permute-start(bf16[256,512]{1,0:T(8,128)(2,1)S(1)} %get-tuple-element.18), channel_id=1, source_target_pairs={{0,2},{1,3},{2,0},{3,1},{4,6},{5,7},{6,4},{7,5},{8,10},{9,11},{10,... | collective-permute-start | bytes 786440 | tf_op jit(solution)/shard_map/ppermute | solution.py:50
  11.9 20.9 %collective-permute-start.8 = (bf16[256,512]{1,0:T(8,128)(2,1)S(1)}, bf16[256,512]{1,0:T(8,128)(2,1)S(1)}, u32[]{:S(2)}, u32[]{:S(2)}) collective-permute-start(bf16[256,512]{1,0:T(8,128)(2,1)S(1)} %convolution_convert_fusion.2), channel_id=1, source_target_pairs={{0,8},{1,9},{2,0},{3,1},{4,12},{5,13},{6,4},{7,5},{8,10},{9,11},{1... | collective-permute-start | bytes 786440 | tf_op jit(solution)/shard_map/ppermute | solution.py:50
  21.8 11.6 %collective-permute-start.2 = (bf16[256,512]{1,0:T(8,128)(2,1)}, bf16[256,512]{1,0:T(8,128)(2,1)S(1)}, u32[]{:S(2)}, u32[]{:S(2)}) collective-permute-start(bf16[256,512]{1,0:T(8,128)(2,1)} %convolution_convert_fusion.1), channel_id=1, source_target_pairs={{0,4},{1,5},{2,12},{3,13},{4,0},{5,1},{6,8},{7,9},{8,6},{9,7},{10,... | collective-permute-start | bytes 786440 | tf_op jit(solution)/shard_map/ppermute | solution.py:50
  21.8 11.7 %collective-permute-start.1 = (bf16[256,512]{1,0:T(8,128)(2,1)S(1)}, bf16[256,512]{1,0:T(8,128)(2,1)S(1)}, u32[]{:S(2)}, u32[]{:S(2)}) collective-permute-start(bf16[256,512]{1,0:T(8,128)(2,1)S(1)} %dynamic-slice_bitcast_fusion), channel_id=1, source_target_pairs={{0,2},{1,3},{2,0},{3,1},{4,6},{5,7},{6,4},{7,5},{8,10},{9,11},{10,... | collective-permute-start | bytes 786440 | tf_op jit(solution)/shard_map/ppermute | solution.py:50
  27.3 9.4 %collective-permute-start.5 = (bf16[256,512]{1,0:T(8,128)(2,1)S(1)}, bf16[256,512]{1,0:T(8,128)(2,1)S(1)}, u32[]{:S(2)}, u32[]{:S(2)}) collective-permute-start(bf16[256,512]{1,0:T(8,128)(2,1)S(1)} %convolution_convert_fusion), channel_id=1, source_target_pairs={{0,12},{1,13},{2,4},{3,5},{4,8},{5,9},{6,0},{7,1},{8,14},{9,15},{1... | collective-permute-start | bytes 786440 | tf_op jit(solution)/shard_map/ppermute | solution.py:50
  32.9 1.5 %collective-permute-start.7 = (bf16[256,512]{1,0:T(8,128)(2,1)S(1)}, bf16[256,512]{1,0:T(8,128)(2,1)S(1)}, u32[]{:S(2)}, u32[]{:S(2)}) collective-permute-start(bf16[256,512]{1,0:T(8,128)(2,1)S(1)} %collective-permute-done.6), channel_id=1, source_target_pairs={{0,1},{1,0},{2,3},{3,2},{4,5},{5,4},{6,7},{7,6},{8,9},{9,8},{10,11... | collective-permute-start | bytes 786440 | tf_op jit(solution)/shard_map/ppermute | solution.py:50
  32.9 2.5 %collective-permute-start.9 = (bf16[256,512]{1,0:T(8,128)(2,1)S(1)}, bf16[256,512]{1,0:T(8,128)(2,1)S(1)}, u32[]{:S(2)}, u32[]{:S(2)}) collective-permute-start(bf16[256,512]{1,0:T(8,128)(2,1)S(1)} %collective-permute-done.8), channel_id=1, source_target_pairs={{0,1},{1,0},{2,3},{3,2},{4,5},{5,4},{6,7},{7,6},{8,9},{9,8},{10,11... | collective-permute-start | bytes 786440 | tf_op jit(solution)/shard_map/ppermute | solution.py:50
  33.4 1.8 %collective-permute-start.3 = (bf16[256,512]{1,0:T(8,128)(2,1)S(1)}, bf16[256,512]{1,0:T(8,128)(2,1)S(1)}, u32[]{:S(2)}, u32[]{:S(2)}) collective-permute-start(bf16[256,512]{1,0:T(8,128)(2,1)S(1)} %collective-permute-done.2), channel_id=1, source_target_pairs={{0,1},{1,0},{2,3},{3,2},{4,5},{5,4},{6,7},{7,6},{8,9},{9,8},{10,11... | collective-permute-start | bytes 786440 | tf_op jit(solution)/shard_map/ppermute | solution.py:50
  36.7 1.5 %collective-permute-start.10 = (bf16[256,512]{1,0:T(8,128)(2,1)S(1)}, bf16[256,512]{1,0:T(8,128)(2,1)S(1)}, u32[]{:S(2)}, u32[]{:S(2)}) collective-permute-start(bf16[256,512]{1,0:T(8,128)(2,1)S(1)} %collective-permute-done.5), channel_id=1, source_target_pairs={{0,1},{1,0},{2,3},{3,2},{4,5},{5,4},{6,7},{7,6},{8,9},{9,8},{10,11... | collective-permute-start | bytes 786440 | tf_op jit(solution)/shard_map/ppermute | solution.py:50
  36.8 1.9 %copy-start.1 = (bf16[1,2,256,512]{3,2,1,0:T(8,128)(2,1)}, bf16[1,2,256,512]{3,2,1,0:T(8,128)(2,1)S(1)}, u32[]{:S(2)}) copy-start(bf16[1,2,256,512]{3,2,1,0:T(8,128)(2,1)S(1)} %bitcast_dynamic-update-slice_fusion) | copy-start | bytes 1572868

commit v6 on v5

--- a/solution.py
+++ b/solution.py
@@ -56,26 +56,26 @@
         return permute(value, (0, 0, 1), (0, 0, 1))
 
     own_same = lax.dynamic_index_in_dim(wavefunction[0], odd, 0, keepdims=False)
-    own_flip = lax.dynamic_index_in_dim(wavefunction[0], 1 - odd, 0, keepdims=False)
-    other_same = permute(own_same, (0, 1, 0), (0, 1, 0))
+    other_same = over_term(own_same)
+    later_odd, _ = lax.optimization_barrier((odd, own_same))
+    own_flip = lax.dynamic_index_in_dim(wavefunction[0], 1 - later_odd, 0, keepdims=False)
     second_flip = own_flip
-    other_flip = permute(second_flip, (0, 1, 0), (0, 1, 0))
+    other_flip = over_term(second_flip)
     live = live_states(right_dims, z, states)
     right = jnp.where(live[:, None] & live[None, :], right_env[0, 0], jnp.zeros((), BF16))
+    right = lax.optimization_barrier(right)
     moved_first = contract(own_same, right)
     same_first = permute(moved_first, (0, 0, 0), (2, 1, 0))
     other_same, _ = lax.optimization_barrier((other_same, moved_first))
     moved_same = contract(other_same, right)
     same_second = permute(moved_same, (2, 0, 0), (0, 1, 0))
-    later_u = u
-    later_u, _ = lax.optimization_barrier((later_u, moved_same))
+    later_u, _ = lax.optimization_barrier((u, moved_first))
     own_rows = lax.dynamic_slice_in_dim(left_env[0, 0], later_u * half, half, 0)
     other_rows = over_term(own_rows)
-    early_flip, own_rows = lax.optimization_barrier((own_flip, own_rows))
-    early_flip, _ = lax.optimization_barrier((early_flip, moved_same))
+    early_flip, _ = lax.optimization_barrier((own_flip, moved_same))
     moved_flip = contract(early_flip, right)
     flip_first = permute(moved_flip, (1, 0, 0), (3, 1, 0))
-    other_flip, _, _ = lax.optimization_barrier((other_flip, moved_same, moved_flip))
+    other_flip, _, _ = lax.optimization_barrier((other_flip, moved_flip, own_rows))
     moved_last = contract(other_flip, right)
     flip_second = permute(moved_last, (3, 0, 0), (1, 1, 0))
     cols_live = live_states(left_dims, z, states)

time: 39.7 us -> 39.5 us (level)
  matrix products: 4.3 us -> 3.1 us
  other arithmetic: 1.06 us -> 2.24 us
  waiting for transfers between devices: 8.86 us -> 7.95 us
  local copies, waits for them, and re-layouts: 1.33 us -> 1.82 us
    unnamed x10 -> x12, local copies, waits for them, and re-layouts: 0.03 us -> 1.62 us
    dot_general x4, matrix products: 2.5 us -> 1.32 us  [contract(): lax.dot_general(block, right, (((1,), (1,)), ((), ())), preferred_element...]
    squeeze x1, local copies, waits for them, and re-layouts: 1.15 us -> 0.02 us  [two_by_four(): own_same = lax.dynamic_index_in_dim(wavefunction[0], odd, 0, keepdims=False)]
    select_n x1, other arithmetic: 0.18 us -> 1.13 us  [two_by_four(): jnp.where(rows_live[:, None] & cols_live[None, :], rows, jnp.zeros((), BF...]
    ppermute x11, waiting for transfers between devices: 8.86 us -> 7.95 us  [permute(): return lax.ppermute(value, LINE, pairs)]
where the time goes in v6:
time: 39.5 us; the launch traced here: 39.3 us
  starting transfers between devices  24 us (61%)
  waiting for transfers between devices  7.95 us (20%)
  matrix products  3.1 us (8%)
  other arithmetic  2.24 us (6%)
  local copies, waits for them, and re-layouts  1.82 us (5%)
    ppermute x11, starting transfers between devices, permute(): return lax.ppermute(value, LINE, pairs)  24 us
    ppermute x11, waiting for transfers between devices, permute(): return lax.ppermute(value, LINE, pairs)  7.95 us
    unnamed x12, local copies, waits for them, and re-layouts  1.62 us
    dot_general x4, matrix products, contract(): lax.dot_general(block, right, (((1,), (1,)), ((), ())), preferred_element...  1.32 us
    select_n x1, other arithmetic, two_by_four(): jnp.where(rows_live[:, None] & cols_live[None, :], rows, jnp.zeros((), BF...  1.13 us
    dot_general x4, matrix products, apply_left(): jnp.dot(left[0], mine, preferred_element_type=F32)  0.9 us
    dot_general x4, matrix products, apply_left(): jnp.dot(left[1], over_core(mine), preferred_element_type=F32)  0.89 us
    dynamic_update_slice x1, other arithmetic, two_by_four(): lax.dynamic_update_slice(product, flip[None, None], (0, 1 - odd, 0, 0))  0.79 us
  transfers between devices with their start and end apart: 11, of which 6 were waited for; matrix products, arithmetic and copies ran while one was open for 11% of the time, Pallas kernels for 0%

profile of v6, /device:TPU:0, one launch (start us, length us, event | category | flops | bytes accessed | tf_op | source)
XLA Modules:
  0.0 39.3 jit_solution(15456308048007449894)
XLA Ops:
  0.0 1.0 %copy-done = bf16[1,2,256,512]{3,2,1,0:T(8,128)(2,1)S(1)} copy-done((bf16[1,2,256,512]{3,2,1,0:T(8,128)(2,1)S(1)}, bf16[1,2,256,512]{3,2,1,0:T(8,128)(2,1)}, u32[]{:S(2)}) %copy-start) | copy-done | bytes 524312
  1.1 3.0 %collective-permute-start.1 = (bf16[256,512]{1,0:T(8,128)(2,1)S(1)}, bf16[256,512]{1,0:T(8,128)(2,1)S(1)}, u32[]{:S(2)}, u32[]{:S(2)}) collective-permute-start(bf16[256,512]{1,0:T(8,128)(2,1)S(1)} %dynamic-slice_bitcast_fusion.2), channel_id=1, source_target_pairs={{0,2},{1,3},{2,0},{3,1},{4,6},{5,7},{6,4},{7,5},{8,10},{9,11},{10,... | collective-permute-start | bytes 786440 | tf_op jit(solution)/shard_map/ppermute | solution.py:50
  4.1 0.1 collective-permute-start.4
  4.2 0.5 %copy-done.4 = s32[4]{0:T(128)S(1)} copy-done((s32[4]{0:T(128)S(1)}, s32[4]{0:T(128)}, u32[]{:S(2)}) %copy-start.4) | copy-done | bytes 40
  4.8 0.1 fusion.17
  4.9 0.2 and_select_fusion
  5.1 0.3 convolution_convert_fusion.3
  5.4 0.7 %collective-permute-start.6 = (bf16[256,512]{1,0:T(8,128)(2,1)S(1)}, bf16[256,512]{1,0:T(8,128)(2,1)S(1)}, u32[]{:S(2)}, u32[]{:S(2)}) collective-permute-start(bf16[256,512]{1,0:T(8,128)(2,1)S(1)} %convolution_convert_fusion.3), channel_id=1, source_target_pairs={{0,0},{1,1},{2,8},{3,9},{4,4},{5,5},{6,12},{7,13},{8,2},{9,3},{10,... | collective-permute-start | bytes 786440 | tf_op jit(solution)/shard_map/ppermute | solution.py:50
  6.2 5.3 %collective-permute-start = (bf16[256,512]{1,0:T(8,128)(2,1)S(1)}, bf16[256,512]{1,0:T(8,128)(2,1)}, u32[]{:S(2)}, u32[]{:S(2)}) collective-permute-start(bf16[256,512]{1,0:T(8,128)(2,1)S(1)} %dynamic-slice_bitcast_fusion.1), channel_id=1, source_target_pairs={{0,2},{1,3},{2,0},{3,1},{4,6},{5,7},{6,4},{7,5},{8,10},{9,11},{10,... | collective-permute-start | bytes 786440 | tf_op jit(solution)/shard_map/ppermute | solution.py:50
  11.6 0.1 collective-permute-done.1
  11.8 0.3 convolution_convert_fusion.2
  12.1 8.3 %collective-permute-start.8 = (bf16[256,512]{1,0:T(8,128)(2,1)S(1)}, bf16[256,512]{1,0:T(8,128)(2,1)S(1)}, u32[]{:S(2)}, u32[]{:S(2)}) collective-permute-start(bf16[256,512]{1,0:T(8,128)(2,1)S(1)} %convolution_convert_fusion.2), channel_id=1, source_target_pairs={{0,8},{1,9},{2,0},{3,1},{4,12},{5,13},{6,4},{7,5},{8,10},{9,11},{1... | collective-permute-start | bytes 786440 | tf_op jit(solution)/shard_map/ppermute | solution.py:50
  20.4 0.3 convolution_convert_fusion.1
  20.8 5.9 %collective-permute-done.4 = bf16[256,512]{1,0:T(8,128)(2,1)S(1)} collective-permute-done((bf16[256,512]{1,0:T(8,128)(2,1)S(1)}, bf16[256,512]{1,0:T(8,128)(2,1)S(1)}, u32[]{:S(2)}, u32[]{:S(2)}) %collective-permute-start.4) | collective-permute-done | bytes 262176 | tf_op jit(solution)/shard_map/ppermute | solution.py:50
  26.7 0.3 convolution_convert_fusion
  27.0 5.6 %collective-permute-start.5 = (bf16[256,512]{1,0:T(8,128)(2,1)S(1)}, bf16[256,512]{1,0:T(8,128)(2,1)S(1)}, u32[]{:S(2)}, u32[]{:S(2)}) collective-permute-start(bf16[256,512]{1,0:T(8,128)(2,1)S(1)} %convolution_convert_fusion), channel_id=1, source_target_pairs={{0,12},{1,13},{2,4},{3,5},{4,8},{5,9},{6,0},{7,1},{8,14},{9,15},{1... | collective-permute-start | bytes 786440 | tf_op jit(solution)/shard_map/ppermute | solution.py:50
  32.6 1.1 %and_select_fusion.1 = (bf16[256,512]{1,0:T(8,128)(2,1)S(1)}, bf16[256,512]{1,0:T(8,128)(2,1)S(1)}) fusion(bf16[256,512]{1,0:T(8,128)(2,1)} %collective-permute-done, pred[]{:T(512)S(6)} %eq.18, pred[512]{0:T(512)(128)(4,1)S(1)} %get-tuple-element.21, pred[256]{0:T(512)(128)(4,1)S(1)} %dynamic_slice.27, bf16[1,1,512,512]{3,2,1,0:T(8,128)(2,1)S(1)} %copy-done.3, ...), kind=kLoop, calls=%fused_computation.11 | loop fusion | flops 655360 | bytes 1049349 | tf_op jit(solution)/shard_map/jit(_where)/select_n | solution.py:85
  33.8 0.2 fusion.12
  34.0 0.6 %collective-permute-start.3 = (bf16[256,512]{1,0:T(8,128)(2,1)S(1)}, bf16[256,512]{1,0:T(8,128)(2,1)S(1)}, u32[]{:S(2)}, u32[]{:S(2)}) collective-permute-start(bf16[256,512]{1,0:T(8,128)(2,1)S(1)} %collective-permute-done.2), channel_id=1, source_target_pairs={{0,1},{1,0},{2,3},{3,2},{4,5},{5,4},{6,7},{7,6},{8,9},{9,8},{10,11... | collective-permute-start | bytes 786440 | tf_op jit(solution)/shard_map/ppermute | solution.py:50
  34.7 0.2 convolution_add_fusion.2
  34.9 0.2 fusion.14
  35.1 0.2 fusion.8
  35.3 0.4 collective-permute-done.3
  35.7 0.2 convolution_add_fusion.3
  36.0 0.1 collective-permute-done.9
  36.1 0.2 fusion.1
  36.3 0.2 collective-permute-done.5
  36.5 0.3 collective-permute-start.10
  36.9 1.2 %collective-permute-done.10 = bf16[256,512]{1,0:T(8,128)(2,1)S(1)} collective-permute-done((bf16[256,512]{1,0:T(8,128)(2,1)S(1)}, bf16[256,512]{1,0:T(8,128)(2,1)S(1)}, u32[]{:S(2)}, u32[]{:S(2)}) %collective-permute-start.10) | collective-permute-done | bytes 262176 | tf_op jit(solution)/shard_map/ppermute | solution.py:50
  38.0 0.2 fusion.4
  38.3 0.2 convolution_add_fusion
  38.5 0.8 %fusion.3 = bf16[1,2,256,512]{3,2,1,0:T(8,128)(2,1)} fusion(bf16[1,2,256,512]{3,2,1,0:T(8,128)(2,1)} %copy-done.2, s32[]{:T(128)S(6)} %select_n.63, f32[256,512]{1,0:T(8,128)S(1)} %convolution_add_fusion.3, f32[256,512]{1,0:T(8,128)S(1)} %convolution_add_fusion), kind=kLoop, calls=%fused_computation.15 | loop fusion | flops 262144 | bytes 1310724 | tf_op jit(solution)/shard_map/dynamic_update_slice | solution.py:100
  (25 shorter events, 0.4 us)
Async XLA Ops:
  0.0 1.0 %copy-start = (bf16[1,2,256,512]{3,2,1,0:T(8,128)(2,1)S(1)}, bf16[1,2,256,512]{3,2,1,0:T(8,128)(2,1)}, u32[]{:S(2)}) copy-start(bf16[1,2,256,512]{3,2,1,0:T(8,128)(2,1)} %param.5) | copy-start | bytes 1572868
  1.0 3.8 %copy-start.1 = (bf16[1,1,512,512]{3,2,1,0:T(8,128)(2,1)S(1)}, bf16[1,1,512,512]{3,2,1,0:T(8,128)(2,1)}, u32[]{:S(2)}) copy-start(bf16[1,1,512,512]{3,2,1,0:T(8,128)(2,1)} %param.7) | copy-start | bytes 1572868
  1.1 10.7 %collective-permute-start.1 = (bf16[256,512]{1,0:T(8,128)(2,1)S(1)}, bf16[256,512]{1,0:T(8,128)(2,1)S(1)}, u32[]{:S(2)}, u32[]{:S(2)}) collective-permute-start(bf16[256,512]{1,0:T(8,128)(2,1)S(1)} %dynamic-slice_bitcast_fusion.2), channel_id=1, source_target_pairs={{0,2},{1,3},{2,0},{3,1},{4,6},{5,7},{6,4},{7,5},{8,10},{9,11},{10,... | collective-permute-start | bytes 786440 | tf_op jit(solution)/shard_map/ppermute | solution.py:50
  4.1 0.7 %copy-start.4 = (s32[4]{0:T(128)S(1)}, s32[4]{0:T(128)}, u32[]{:S(2)}) copy-start(s32[4]{0:T(128)} %param.8) | copy-start | bytes 52
  4.1 0.7 %copy-start.5 = (s32[4]{0:T(128)S(1)}, s32[4]{0:T(128)}, u32[]{:S(2)}) copy-start(s32[4]{0:T(128)} %param.9) | copy-start | bytes 52
  4.1 22.6 %collective-permute-start.4 = (bf16[256,512]{1,0:T(8,128)(2,1)S(1)}, bf16[256,512]{1,0:T(8,128)(2,1)S(1)}, u32[]{:S(2)}, u32[]{:S(2)}) collective-permute-start(bf16[256,512]{1,0:T(8,128)(2,1)S(1)} %dynamic-slice_bitcast_fusion), channel_id=1, source_target_pairs={{0,2},{1,3},{2,0},{3,1},{4,6},{5,7},{6,4},{7,5},{8,10},{9,11},{10,... | collective-permute-start | bytes 786440 | tf_op jit(solution)/shard_map/ppermute | solution.py:50
  5.1 1.0 %copy-start.3 = (bf16[1,1,512,512]{3,2,1,0:T(8,128)(2,1)S(1)}, bf16[1,1,512,512]{3,2,1,0:T(8,128)(2,1)}, u32[]{:S(2)}) copy-start(bf16[1,1,512,512]{3,2,1,0:T(8,128)(2,1)} %param.6) | copy-start | bytes 1572868
  5.4 27.2 %collective-permute-start.6 = (bf16[256,512]{1,0:T(8,128)(2,1)S(1)}, bf16[256,512]{1,0:T(8,128)(2,1)S(1)}, u32[]{:S(2)}, u32[]{:S(2)}) collective-permute-start(bf16[256,512]{1,0:T(8,128)(2,1)S(1)} %convolution_convert_fusion.3), channel_id=1, source_target_pairs={{0,0},{1,1},{2,8},{3,9},{4,4},{5,5},{6,12},{7,13},{8,2},{9,3},{10,... | collective-permute-start | bytes 786440 | tf_op jit(solution)/shard_map/ppermute | solution.py:50
  6.2 26.4 %collective-permute-start = (bf16[256,512]{1,0:T(8,128)(2,1)S(1)}, bf16[256,512]{1,0:T(8,128)(2,1)}, u32[]{:S(2)}, u32[]{:S(2)}) collective-permute-start(bf16[256,512]{1,0:T(8,128)(2,1)S(1)} %dynamic-slice_bitcast_fusion.1), channel_id=1, source_target_pairs={{0,2},{1,3},{2,0},{3,1},{4,6},{5,7},{6,4},{7,5},{8,10},{9,11},{10,... | collective-permute-start | bytes 786440 | tf_op jit(solution)/shard_map/ppermute | solution.py:50
  12.1 22.5 %collective-permute-start.8 = (bf16[256,512]{1,0:T(8,128)(2,1)S(1)}, bf16[256,512]{1,0:T(8,128)(2,1)S(1)}, u32[]{:S(2)}, u32[]{:S(2)}) collective-permute-start(bf16[256,512]{1,0:T(8,128)(2,1)S(1)} %convolution_convert_fusion.2), channel_id=1, source_target_pairs={{0,8},{1,9},{2,0},{3,1},{4,12},{5,13},{6,4},{7,5},{8,10},{9,11},{1... | collective-permute-start | bytes 786440 | tf_op jit(solution)/shard_map/ppermute | solution.py:50
  20.7 13.3 %collective-permute-start.2 = (bf16[256,512]{1,0:T(8,128)(2,1)S(1)}, bf16[256,512]{1,0:T(8,128)(2,1)S(1)}, u32[]{:S(2)}, u32[]{:S(2)}) collective-permute-start(bf16[256,512]{1,0:T(8,128)(2,1)S(1)} %convolution_convert_fusion.1), channel_id=1, source_target_pairs={{0,4},{1,5},{2,12},{3,13},{4,0},{5,1},{6,8},{7,9},{8,6},{9,7},{10,... | collective-permute-start | bytes 786440 | tf_op jit(solution)/shard_map/ppermute | solution.py:50
  27.0 9.5 %collective-permute-start.5 = (bf16[256,512]{1,0:T(8,128)(2,1)S(1)}, bf16[256,512]{1,0:T(8,128)(2,1)S(1)}, u32[]{:S(2)}, u32[]{:S(2)}) collective-permute-start(bf16[256,512]{1,0:T(8,128)(2,1)S(1)} %convolution_convert_fusion), channel_id=1, source_target_pairs={{0,12},{1,13},{2,4},{3,5},{4,8},{5,9},{6,0},{7,1},{8,14},{9,15},{1... | collective-permute-start | bytes 786440 | tf_op jit(solution)/shard_map/ppermute | solution.py:50
  32.6 2.0 %collective-permute-start.7 = (bf16[256,512]{1,0:T(8,128)(2,1)S(1)}, bf16[256,512]{1,0:T(8,128)(2,1)S(1)}, u32[]{:S(2)}, u32[]{:S(2)}) collective-permute-start(bf16[256,512]{1,0:T(8,128)(2,1)S(1)} %collective-permute-done.6), channel_id=1, source_target_pairs={{0,1},{1,0},{2,3},{3,2},{4,5},{5,4},{6,7},{7,6},{8,9},{9,8},{10,11... | collective-permute-start | bytes 786440 | tf_op jit(solution)/shard_map/ppermute | solution.py:50
  34.0 1.7 %collective-permute-start.3 = (bf16[256,512]{1,0:T(8,128)(2,1)S(1)}, bf16[256,512]{1,0:T(8,128)(2,1)S(1)}, u32[]{:S(2)}, u32[]{:S(2)}) collective-permute-start(bf16[256,512]{1,0:T(8,128)(2,1)S(1)} %collective-permute-done.2), channel_id=1, source_target_pairs={{0,1},{1,0},{2,3},{3,2},{4,5},{5,4},{6,7},{7,6},{8,9},{9,8},{10,11... | collective-permute-start | bytes 786440 | tf_op jit(solution)/shard_map/ppermute | solution.py:50
  34.6 1.5 %collective-permute-start.9 = (bf16[256,512]{1,0:T(8,128)(2,1)S(1)}, bf16[256,512]{1,0:T(8,128)(2,1)S(1)}, u32[]{:S(2)}, u32[]{:S(2)}) collective-permute-start(bf16[256,512]{1,0:T(8,128)(2,1)S(1)} %collective-permute-done.8), channel_id=1, source_target_pairs={{0,1},{1,0},{2,3},{3,2},{4,5},{5,4},{6,7},{7,6},{8,9},{9,8},{10,11... | collective-permute-start | bytes 786440 | tf_op jit(solution)/shard_map/ppermute | solution.py:50
  36.5 1.5 %collective-permute-start.10 = (bf16[256,512]{1,0:T(8,128)(2,1)S(1)}, bf16[256,512]{1,0:T(8,128)(2,1)S(1)}, u32[]{:S(2)}, u32[]{:S(2)}) collective-permute-start(bf16[256,512]{1,0:T(8,128)(2,1)S(1)} %collective-permute-done.5), channel_id=1, source_target_pairs={{0,1},{1,0},{2,3},{3,2},{4,5},{5,4},{6,7},{7,6},{8,9},{9,8},{10,11... | collective-permute-start | bytes 786440 | tf_op jit(solution)/shard_map/ppermute | solution.py:50
  36.9 1.6 %copy-start.2 = (bf16[1,2,256,512]{3,2,1,0:T(8,128)(2,1)}, bf16[1,2,256,512]{3,2,1,0:T(8,128)(2,1)S(1)}, u32[]{:S(2)}) copy-start(bf16[1,2,256,512]{3,2,1,0:T(8,128)(2,1)S(1)} %bitcast_dynamic-update-slice_fusion) | copy-start | bytes 1572868

commit v7 on v6

--- a/solution.py
+++ b/solution.py
@@ -94,9 +94,11 @@
     flip = apply_left(lefts[0], flip_first)
     same = (same + apply_left(lefts[1], same_second)).astype(BF16)
     flip, flip_second, same = lax.optimization_barrier((flip, flip_second, same))
-    flip = (flip + apply_left(lefts[1], flip_second)).astype(BF16)
-    product = jnp.zeros((1, 2, half, width), BF16)
-    product = lax.dynamic_update_slice(product, same[None, None], (0, odd, 0, 0))
+    theirs = over_core(flip_second)
+    flip = flip + jnp.dot(lefts[1][0], flip_second, preferred_element_type=F32)
+    product = lax.dynamic_update_slice(jnp.zeros((1, 2, half, width), BF16), same[None, None], (0, odd, 0, 0))
+    flip, theirs, product = lax.optimization_barrier((flip, theirs, product))
+    flip = (flip + jnp.dot(lefts[1][1], theirs, preferred_element_type=F32)).astype(BF16)
     return lax.dynamic_update_slice(product, flip[None, None], (0, 1 - odd, 0, 0))
 
 

time: 39.5 us -> 39.3 us (level)
    dot_general x0 -> x2, matrix products: none -> 0.44 us  [the longest x1 0.22 us: two_by_four(): flip = flip + jnp.dot(lefts[1][0], flip_second, preferred_element_type=F32)]
    dot_general x4 -> x3, matrix products: 0.9 us -> 0.67 us  [apply_left(): jnp.dot(left[0], mine, preferred_element_type=F32)]
    dot_general x4 -> x3, matrix products: 0.89 us -> 0.67 us  [apply_left(): jnp.dot(left[1], over_core(mine), preferred_element_type=F32)]
  transfers between devices with their start and end apart: 11 -> 11, of which waited for: 6 -> 6; matrix products, arithmetic and copies ran while one was open for 11% -> 12% of each run, Pallas kernels for 0% -> 0%
where the time goes in v7:
time: 39.3 us; the launch traced here: 39.1 us
  starting transfers between devices  24 us (61%)
  waiting for transfers between devices  7.63 us (19%)
  matrix products  3.1 us (8%)
  other arithmetic  2.31 us (6%)
  local copies, waits for them, and re-layouts  1.82 us (5%)
    ppermute x11, starting transfers between devices, permute(): return lax.ppermute(value, LINE, pairs)  24 us
    ppermute x11, waiting for transfers between devices, permute(): return lax.ppermute(value, LINE, pairs)  7.63 us
    unnamed x12, local copies, waits for them, and re-layouts  1.62 us
    dot_general x4, matrix products, contract(): lax.dot_general(block, right, (((1,), (1,)), ((), ())), preferred_element...  1.32 us
    select_n x1, other arithmetic, two_by_four(): jnp.where(rows_live[:, None] & cols_live[None, :], rows, jnp.zeros((), BF...  1.13 us
  transfers between devices with their start and end apart: 11, of which 6 were waited for; matrix products, arithmetic and copies ran while one was open for 12% of the time, Pallas kernels for 0%

profile of v7, /device:TPU:0, one launch (start us, length us, event | category | flops | bytes accessed | tf_op | source)
XLA Modules:
  0.0 39.1 jit_solution(2940790681377060494)
XLA Ops:
  0.0 1.0 %copy-done = bf16[1,2,256,512]{3,2,1,0:T(8,128)(2,1)S(1)} copy-done((bf16[1,2,256,512]{3,2,1,0:T(8,128)(2,1)S(1)}, bf16[1,2,256,512]{3,2,1,0:T(8,128)(2,1)}, u32[]{:S(2)}) %copy-start) | copy-done | bytes 524312
  1.1 3.0 %collective-permute-start.1 = (bf16[256,512]{1,0:T(8,128)(2,1)S(1)}, bf16[256,512]{1,0:T(8,128)(2,1)S(1)}, u32[]{:S(2)}, u32[]{:S(2)}) collective-permute-start(bf16[256,512]{1,0:T(8,128)(2,1)S(1)} %dynamic-slice_bitcast_fusion.2), channel_id=1, source_target_pairs={{0,2},{1,3},{2,0},{3,1},{4,6},{5,7},{6,4},{7,5},{8,10},{9,11},{10,... | collective-permute-start | bytes 786440 | tf_op jit(solution)/shard_map/ppermute | solution.py:50
  4.1 0.1 collective-permute-start.4
  4.2 0.5 %copy-done.4 = s32[4]{0:T(128)S(1)} copy-done((s32[4]{0:T(128)S(1)}, s32[4]{0:T(128)}, u32[]{:S(2)}) %copy-start.4) | copy-done | bytes 40
  4.8 0.1 fusion.18
  4.9 0.2 and_select_fusion
  5.1 0.3 convolution_convert_fusion.3
  5.4 0.7 %collective-permute-start.6 = (bf16[256,512]{1,0:T(8,128)(2,1)S(1)}, bf16[256,512]{1,0:T(8,128)(2,1)S(1)}, u32[]{:S(2)}, u32[]{:S(2)}) collective-permute-start(bf16[256,512]{1,0:T(8,128)(2,1)S(1)} %convolution_convert_fusion.3), channel_id=1, source_target_pairs={{0,0},{1,1},{2,8},{3,9},{4,4},{5,5},{6,12},{7,13},{8,2},{9,3},{10,... | collective-permute-start | bytes 786440 | tf_op jit(solution)/shard_map/ppermute | solution.py:50
  6.2 5.3 %collective-permute-start = (bf16[256,512]{1,0:T(8,128)(2,1)S(1)}, bf16[256,512]{1,0:T(8,128)(2,1)}, u32[]{:S(2)}, u32[]{:S(2)}) collective-permute-start(bf16[256,512]{1,0:T(8,128)(2,1)S(1)} %dynamic-slice_bitcast_fusion.1), channel_id=1, source_target_pairs={{0,2},{1,3},{2,0},{3,1},{4,6},{5,7},{6,4},{7,5},{8,10},{9,11},{10,... | collective-permute-start | bytes 786440 | tf_op jit(solution)/shard_map/ppermute | solution.py:50
  11.6 0.1 collective-permute-done.1
  11.8 0.3 convolution_convert_fusion.2
  12.1 8.3 %collective-permute-start.8 = (bf16[256,512]{1,0:T(8,128)(2,1)S(1)}, bf16[256,512]{1,0:T(8,128)(2,1)S(1)}, u32[]{:S(2)}, u32[]{:S(2)}) collective-permute-start(bf16[256,512]{1,0:T(8,128)(2,1)S(1)} %convolution_convert_fusion.2), channel_id=1, source_target_pairs={{0,8},{1,9},{2,0},{3,1},{4,12},{5,13},{6,4},{7,5},{8,10},{9,11},{1... | collective-permute-start | bytes 786440 | tf_op jit(solution)/shard_map/ppermute | solution.py:50
  20.4 0.3 convolution_convert_fusion.1
  20.8 5.9 %collective-permute-done.4 = bf16[256,512]{1,0:T(8,128)(2,1)S(1)} collective-permute-done((bf16[256,512]{1,0:T(8,128)(2,1)S(1)}, bf16[256,512]{1,0:T(8,128)(2,1)S(1)}, u32[]{:S(2)}, u32[]{:S(2)}) %collective-permute-start.4) | collective-permute-done | bytes 262176 | tf_op jit(solution)/shard_map/ppermute | solution.py:50
  26.7 0.3 convolution_convert_fusion
  27.0 5.6 %collective-permute-start.5 = (bf16[256,512]{1,0:T(8,128)(2,1)S(1)}, bf16[256,512]{1,0:T(8,128)(2,1)S(1)}, u32[]{:S(2)}, u32[]{:S(2)}) collective-permute-start(bf16[256,512]{1,0:T(8,128)(2,1)S(1)} %convolution_convert_fusion), channel_id=1, source_target_pairs={{0,12},{1,13},{2,4},{3,5},{4,8},{5,9},{6,0},{7,1},{8,14},{9,15},{1... | collective-permute-start | bytes 786440 | tf_op jit(solution)/shard_map/ppermute | solution.py:50
  32.6 1.1 %and_select_fusion.1 = (bf16[256,512]{1,0:T(8,128)(2,1)S(1)}, bf16[256,512]{1,0:T(8,128)(2,1)S(1)}) fusion(bf16[256,512]{1,0:T(8,128)(2,1)} %collective-permute-done, pred[]{:T(512)S(6)} %eq.18, pred[512]{0:T(512)(128)(4,1)S(1)} %get-tuple-element.27, pred[256]{0:T(512)(128)(4,1)S(1)} %dynamic_slice.27, bf16[1,1,512,512]{3,2,1,0:T(8,128)(2,1)S(1)} %copy-done.3, ...), kind=kLoop, calls=%fused_computation.10 | loop fusion | flops 655360 | bytes 1049349 | tf_op jit(solution)/shard_map/jit(_where)/select_n | solution.py:85
  33.8 0.2 fusion.13
  34.0 0.6 %collective-permute-start.3 = (bf16[256,512]{1,0:T(8,128)(2,1)S(1)}, bf16[256,512]{1,0:T(8,128)(2,1)S(1)}, u32[]{:S(2)}, u32[]{:S(2)}) collective-permute-start(bf16[256,512]{1,0:T(8,128)(2,1)S(1)} %collective-permute-done.2), channel_id=1, source_target_pairs={{0,1},{1,0},{2,3},{3,2},{4,5},{5,4},{6,7},{7,6},{8,9},{9,8},{10,11... | collective-permute-start | bytes 786440 | tf_op jit(solution)/shard_map/ppermute | solution.py:50
  34.7 0.2 convolution_add_fusion.1
  34.9 0.2 fusion.15
  35.1 0.2 fusion.9
  35.3 0.4 collective-permute-done.3
  35.7 0.2 convolution_add_fusion.2
  36.0 0.1 collective-permute-done.9
  36.1 0.2 fusion.1
  36.3 0.2 collective-permute-done.5
  36.5 0.3 collective-permute-start.10
  36.8 0.2 fusion.7
  37.2 0.9 %collective-permute-done.10 = bf16[256,512]{1,0:T(8,128)(2,1)S(1)} collective-permute-done((bf16[256,512]{1,0:T(8,128)(2,1)S(1)}, bf16[256,512]{1,0:T(8,128)(2,1)S(1)}, u32[]{:S(2)}, u32[]{:S(2)}) %collective-permute-start.10) | collective-permute-done | bytes 262176 | tf_op jit(solution)/shard_map/ppermute | solution.py:50
  38.0 0.2 fusion.4
  38.3 0.8 %fusion.3 = bf16[1,2,256,512]{3,2,1,0:T(8,128)(2,1)} fusion(bf16[1,2,256,512]{3,2,1,0:T(8,128)(2,1)} %copy-done.2, s32[]{:T(128)S(6)} %select_n.63, f32[256,512]{1,0:T(8,128)S(1)} %add.53, f32[256,512]{1,0:T(8,128)S(1)} %fusion.4), kind=kLoop, calls=%fused_computation.14 | loop fusion | flops 262144 | bytes 1310724 | tf_op jit(solution)/shard_map/dynamic_update_slice | solution.py:102
  (26 shorter events, 0.5 us)
Async XLA Ops:
  0.0 1.0 %copy-start = (bf16[1,2,256,512]{3,2,1,0:T(8,128)(2,1)S(1)}, bf16[1,2,256,512]{3,2,1,0:T(8,128)(2,1)}, u32[]{:S(2)}) copy-start(bf16[1,2,256,512]{3,2,1,0:T(8,128)(2,1)} %param.5) | copy-start | bytes 1572868
  1.0 3.8 %copy-start.1 = (bf16[1,1,512,512]{3,2,1,0:T(8,128)(2,1)S(1)}, bf16[1,1,512,512]{3,2,1,0:T(8,128)(2,1)}, u32[]{:S(2)}) copy-start(bf16[1,1,512,512]{3,2,1,0:T(8,128)(2,1)} %param.7) | copy-start | bytes 1572868
  1.1 10.7 %collective-permute-start.1 = (bf16[256,512]{1,0:T(8,128)(2,1)S(1)}, bf16[256,512]{1,0:T(8,128)(2,1)S(1)}, u32[]{:S(2)}, u32[]{:S(2)}) collective-permute-start(bf16[256,512]{1,0:T(8,128)(2,1)S(1)} %dynamic-slice_bitcast_fusion.2), channel_id=1, source_target_pairs={{0,2},{1,3},{2,0},{3,1},{4,6},{5,7},{6,4},{7,5},{8,10},{9,11},{10,... | collective-permute-start | bytes 786440 | tf_op jit(solution)/shard_map/ppermute | solution.py:50
  4.1 0.7 %copy-start.4 = (s32[4]{0:T(128)S(1)}, s32[4]{0:T(128)}, u32[]{:S(2)}) copy-start(s32[4]{0:T(128)} %param.8) | copy-start | bytes 52
  4.1 0.7 %copy-start.5 = (s32[4]{0:T(128)S(1)}, s32[4]{0:T(128)}, u32[]{:S(2)}) copy-start(s32[4]{0:T(128)} %param.9) | copy-start | bytes 52
  4.1 22.6 %collective-permute-start.4 = (bf16[256,512]{1,0:T(8,128)(2,1)S(1)}, bf16[256,512]{1,0:T(8,128)(2,1)S(1)}, u32[]{:S(2)}, u32[]{:S(2)}) collective-permute-start(bf16[256,512]{1,0:T(8,128)(2,1)S(1)} %dynamic-slice_bitcast_fusion), channel_id=1, source_target_pairs={{0,2},{1,3},{2,0},{3,1},{4,6},{5,7},{6,4},{7,5},{8,10},{9,11},{10,... | collective-permute-start | bytes 786440 | tf_op jit(solution)/shard_map/ppermute | solution.py:50
  5.1 1.0 %copy-start.3 = (bf16[1,1,512,512]{3,2,1,0:T(8,128)(2,1)S(1)}, bf16[1,1,512,512]{3,2,1,0:T(8,128)(2,1)}, u32[]{:S(2)}) copy-start(bf16[1,1,512,512]{3,2,1,0:T(8,128)(2,1)} %param.6) | copy-start | bytes 1572868
  5.4 27.2 %collective-permute-start.6 = (bf16[256,512]{1,0:T(8,128)(2,1)S(1)}, bf16[256,512]{1,0:T(8,128)(2,1)S(1)}, u32[]{:S(2)}, u32[]{:S(2)}) collective-permute-start(bf16[256,512]{1,0:T(8,128)(2,1)S(1)} %convolution_convert_fusion.3), channel_id=1, source_target_pairs={{0,0},{1,1},{2,8},{3,9},{4,4},{5,5},{6,12},{7,13},{8,2},{9,3},{10,... | collective-permute-start | bytes 786440 | tf_op jit(solution)/shard_map/ppermute | solution.py:50
  6.2 26.4 %collective-permute-start = (bf16[256,512]{1,0:T(8,128)(2,1)S(1)}, bf16[256,512]{1,0:T(8,128)(2,1)}, u32[]{:S(2)}, u32[]{:S(2)}) collective-permute-start(bf16[256,512]{1,0:T(8,128)(2,1)S(1)} %dynamic-slice_bitcast_fusion.1), channel_id=1, source_target_pairs={{0,2},{1,3},{2,0},{3,1},{4,6},{5,7},{6,4},{7,5},{8,10},{9,11},{10,... | collective-permute-start | bytes 786440 | tf_op jit(solution)/shard_map/ppermute | solution.py:50
  12.1 22.5 %collective-permute-start.8 = (bf16[256,512]{1,0:T(8,128)(2,1)S(1)}, bf16[256,512]{1,0:T(8,128)(2,1)S(1)}, u32[]{:S(2)}, u32[]{:S(2)}) collective-permute-start(bf16[256,512]{1,0:T(8,128)(2,1)S(1)} %convolution_convert_fusion.2), channel_id=1, source_target_pairs={{0,8},{1,9},{2,0},{3,1},{4,12},{5,13},{6,4},{7,5},{8,10},{9,11},{1... | collective-permute-start | bytes 786440 | tf_op jit(solution)/shard_map/ppermute | solution.py:50
  20.7 13.3 %collective-permute-start.2 = (bf16[256,512]{1,0:T(8,128)(2,1)S(1)}, bf16[256,512]{1,0:T(8,128)(2,1)S(1)}, u32[]{:S(2)}, u32[]{:S(2)}) collective-permute-start(bf16[256,512]{1,0:T(8,128)(2,1)S(1)} %convolution_convert_fusion.1), channel_id=1, source_target_pairs={{0,4},{1,5},{2,12},{3,13},{4,0},{5,1},{6,8},{7,9},{8,6},{9,7},{10,... | collective-permute-start | bytes 786440 | tf_op jit(solution)/shard_map/ppermute | solution.py:50
  27.0 9.5 %collective-permute-start.5 = (bf16[256,512]{1,0:T(8,128)(2,1)S(1)}, bf16[256,512]{1,0:T(8,128)(2,1)S(1)}, u32[]{:S(2)}, u32[]{:S(2)}) collective-permute-start(bf16[256,512]{1,0:T(8,128)(2,1)S(1)} %convolution_convert_fusion), channel_id=1, source_target_pairs={{0,12},{1,13},{2,4},{3,5},{4,8},{5,9},{6,0},{7,1},{8,14},{9,15},{1... | collective-permute-start | bytes 786440 | tf_op jit(solution)/shard_map/ppermute | solution.py:50
  32.6 2.0 %collective-permute-start.7 = (bf16[256,512]{1,0:T(8,128)(2,1)S(1)}, bf16[256,512]{1,0:T(8,128)(2,1)S(1)}, u32[]{:S(2)}, u32[]{:S(2)}) collective-permute-start(bf16[256,512]{1,0:T(8,128)(2,1)S(1)} %collective-permute-done.6), channel_id=1, source_target_pairs={{0,1},{1,0},{2,3},{3,2},{4,5},{5,4},{6,7},{7,6},{8,9},{9,8},{10,11... | collective-permute-start | bytes 786440 | tf_op jit(solution)/shard_map/ppermute | solution.py:50
  34.0 1.7 %collective-permute-start.3 = (bf16[256,512]{1,0:T(8,128)(2,1)S(1)}, bf16[256,512]{1,0:T(8,128)(2,1)S(1)}, u32[]{:S(2)}, u32[]{:S(2)}) collective-permute-start(bf16[256,512]{1,0:T(8,128)(2,1)S(1)} %collective-permute-done.2), channel_id=1, source_target_pairs={{0,1},{1,0},{2,3},{3,2},{4,5},{5,4},{6,7},{7,6},{8,9},{9,8},{10,11... | collective-permute-start | bytes 786440 | tf_op jit(solution)/shard_map/ppermute | solution.py:50
  34.6 1.5 %collective-permute-start.9 = (bf16[256,512]{1,0:T(8,128)(2,1)S(1)}, bf16[256,512]{1,0:T(8,128)(2,1)S(1)}, u32[]{:S(2)}, u32[]{:S(2)}) collective-permute-start(bf16[256,512]{1,0:T(8,128)(2,1)S(1)} %collective-permute-done.8), channel_id=1, source_target_pairs={{0,1},{1,0},{2,3},{3,2},{4,5},{5,4},{6,7},{7,6},{8,9},{9,8},{10,11... | collective-permute-start | bytes 786440 | tf_op jit(solution)/shard_map/ppermute | solution.py:50
  36.5 1.5 %collective-permute-start.10 = (bf16[256,512]{1,0:T(8,128)(2,1)S(1)}, bf16[256,512]{1,0:T(8,128)(2,1)S(1)}, u32[]{:S(2)}, u32[]{:S(2)}) collective-permute-start(bf16[256,512]{1,0:T(8,128)(2,1)S(1)} %collective-permute-done.5), channel_id=1, source_target_pairs={{0,1},{1,0},{2,3},{3,2},{4,5},{5,4},{6,7},{7,6},{8,9},{9,8},{10,11... | collective-permute-start | bytes 786440 | tf_op jit(solution)/shard_map/ppermute | solution.py:50
  37.2 1.1 %copy-start.2 = (bf16[1,2,256,512]{3,2,1,0:T(8,128)(2,1)}, bf16[1,2,256,512]{3,2,1,0:T(8,128)(2,1)S(1)}, u32[]{:S(2)}) copy-start(bf16[1,2,256,512]{3,2,1,0:T(8,128)(2,1)S(1)} %bitcast_dynamic-update-slice_fusion) | copy-start | bytes 1572868

commit v8 on v7

--- a/solution.py
+++ b/solution.py
@@ -57,7 +57,7 @@
 
     own_same = lax.dynamic_index_in_dim(wavefunction[0], odd, 0, keepdims=False)
     other_same = over_term(own_same)
-    later_odd, _ = lax.optimization_barrier((odd, own_same))
+    later_odd = odd
     own_flip = lax.dynamic_index_in_dim(wavefunction[0], 1 - later_odd, 0, keepdims=False)
     second_flip = own_flip
     other_flip = over_term(second_flip)
@@ -69,15 +69,15 @@
     other_same, _ = lax.optimization_barrier((other_same, moved_first))
     moved_same = contract(other_same, right)
     same_second = permute(moved_same, (2, 0, 0), (0, 1, 0))
-    later_u, _ = lax.optimization_barrier((u, moved_first))
-    own_rows = lax.dynamic_slice_in_dim(left_env[0, 0], later_u * half, half, 0)
-    other_rows = over_term(own_rows)
     early_flip, _ = lax.optimization_barrier((own_flip, moved_same))
     moved_flip = contract(early_flip, right)
     flip_first = permute(moved_flip, (1, 0, 0), (3, 1, 0))
-    other_flip, _, _ = lax.optimization_barrier((other_flip, moved_flip, own_rows))
+    other_flip, _, _ = lax.optimization_barrier((other_flip, moved_same, moved_flip))
     moved_last = contract(other_flip, right)
     flip_second = permute(moved_last, (3, 0, 0), (1, 1, 0))
+    later_u, _ = lax.optimization_barrier((u, moved_last))
+    own_rows = lax.dynamic_slice_in_dim(left_env[0, 0], later_u * half, half, 0)
+    other_rows = over_term(own_rows)
     cols_live = live_states(left_dims, z, states)
     rows_live = lax.dynamic_slice_in_dim(cols_live, u * half, half)
     lefts = []
@@ -96,9 +96,10 @@
     flip, flip_second, same = lax.optimization_barrier((flip, flip_second, same))
     theirs = over_core(flip_second)
     flip = flip + jnp.dot(lefts[1][0], flip_second, preferred_element_type=F32)
-    product = lax.dynamic_update_slice(jnp.zeros((1, 2, half, width), BF16), same[None, None], (0, odd, 0, 0))
-    flip, theirs, product = lax.optimization_barrier((flip, theirs, product))
+    flip, theirs = lax.optimization_barrier((flip, theirs))
     flip = (flip + jnp.dot(lefts[1][1], theirs, preferred_element_type=F32)).astype(BF16)
+    product = jnp.zeros((1, 2, half, width), BF16)
+    product = lax.dynamic_update_slice(product, same[None, None], (0, odd, 0, 0))
     return lax.dynamic_update_slice(product, flip[None, None], (0, 1 - odd, 0, 0))
 
 

time: 39.3 us -> 38.4 us (0.977)
  starting transfers between devices: 24 us -> 14.3 us
  waiting for transfers between devices: 7.63 us -> 16.6 us
  other arithmetic: 2.31 us -> 1.35 us
  local copies, waits for them, and re-layouts: 1.82 us -> 2.46 us
    ppermute x11, starting transfers between devices: 24 us -> 14.3 us  [permute(): return lax.ppermute(value, LINE, pairs)]
    ppermute x11, waiting for transfers between devices: 7.63 us -> 16.6 us  [permute(): return lax.ppermute(value, LINE, pairs)]
    squeeze x1, local copies, waits for them, and re-layouts: 0.02 us -> 1.12 us  [two_by_four(): own_same = lax.dynamic_index_in_dim(wavefunction[0], odd, 0, keepdims=False)]
    select_n x1, other arithmetic: 1.13 us -> 0.17 us  [two_by_four(): jnp.where(rows_live[:, None] & cols_live[None, :], rows, jnp.zeros((), BF...]
    unnamed x12 -> x10, local copies, waits for them, and re-layouts: 1.62 us -> 1.18 us
  transfers between devices with their start and end apart: 11 -> 11, of which waited for: 6 -> 6; matrix products, arithmetic and copies ran while one was open for 12% -> 10% of each run, Pallas kernels for 0% -> 0%
where the time goes in v8:
time: 38.4 us; the launch traced here: 38 us
  waiting for transfers between devices  16.6 us (43%)
  starting transfers between devices  14.3 us (37%)
  matrix products  3.11 us (8%)
  local copies, waits for them, and re-layouts  2.46 us (6%)
  other arithmetic  1.35 us (4%)
    ppermute x11, waiting for transfers between devices, permute(): return lax.ppermute(value, LINE, pairs)  16.6 us
    ppermute x11, starting transfers between devices, permute(): return lax.ppermute(value, LINE, pairs)  14.3 us
    dot_general x4, matrix products, contract(): lax.dot_general(block, right, (((1,), (1,)), ((), ())), preferred_element...  1.33 us
    unnamed x10, local copies, waits for them, and re-layouts  1.18 us
    squeeze x1, local copies, waits for them, and re-layouts, two_by_four(): own_same = lax.dynamic_index_in_dim(wavefunction[0], odd, 0, keepdims=False)  1.12 us
    dynamic_update_slice x1, other arithmetic, two_by_four(): lax.dynamic_update_slice(product, flip[None, None], (0, 1 - odd, 0, 0))  0.78 us
  transfers between devices with their start and end apart: 11, of which 6 were waited for; matrix products, arithmetic and copies ran while one was open for 10% of the time, Pallas kernels for 0%

profile of v8, /device:TPU:0, one launch (start us, length us, event | category | flops | bytes accessed | tf_op | source)
XLA Modules:
  0.0 38.0 jit_solution(14529142077580825186)
XLA Ops:
  0.0 1.1 %dynamic-slice_bitcast_fusion.1 = (bf16[256,512]{1,0:T(8,128)(2,1)S(1)}, bf16[256,512]{1,0:T(8,128)(2,1)S(1)}) fusion(bf16[1,2,256,512]{3,2,1,0:T(8,128)(2,1)} %param.5, s32[]{:T(128)S(6)} %select_n.53, s32[]{:T(128)S(6)} %select_n.52), kind=kLoop, calls=%fused_computation.17 | loop fusion | bytes 1048584 | tf_op jit(solution)/shard_map/jit(dynamic_index_in_dim)/squeeze | solution.py:58
  1.1 3.0 %collective-permute-start.1 = (bf16[256,512]{1,0:T(8,128)(2,1)S(1)}, bf16[256,512]{1,0:T(8,128)(2,1)S(1)}, u32[]{:S(2)}, u32[]{:S(2)}) collective-permute-start(bf16[256,512]{1,0:T(8,128)(2,1)S(1)} %get-tuple-element.27), channel_id=1, source_target_pairs={{0,2},{1,3},{2,0},{3,1},{4,6},{5,7},{6,4},{7,5},{8,10},{9,11},{10,... | collective-permute-start | bytes 786440 | tf_op jit(solution)/shard_map/ppermute | solution.py:50
  4.1 0.1 collective-permute-start
  4.2 0.5 %copy-done.3 = s32[4]{0:T(128)S(1)} copy-done((s32[4]{0:T(128)S(1)}, s32[4]{0:T(128)}, u32[]{:S(2)}) %copy-start.3) | copy-done | bytes 40
  4.8 0.1 fusion.18
  4.9 0.2 and_select_fusion
  5.1 0.3 convolution_convert_fusion.3
  5.5 0.7 %collective-permute-start.6 = (bf16[256,512]{1,0:T(8,128)(2,1)S(1)}, bf16[256,512]{1,0:T(8,128)(2,1)S(1)}, u32[]{:S(2)}, u32[]{:S(2)}) collective-permute-start(bf16[256,512]{1,0:T(8,128)(2,1)S(1)} %convolution_convert_fusion.3), channel_id=1, source_target_pairs={{0,0},{1,1},{2,8},{3,9},{4,4},{5,5},{6,12},{7,13},{8,2},{9,3},{10,... | collective-permute-start | bytes 786440 | tf_op jit(solution)/shard_map/ppermute | solution.py:50
  6.2 5.8 %collective-permute-done.1 = bf16[256,512]{1,0:T(8,128)(2,1)S(1)} collective-permute-done((bf16[256,512]{1,0:T(8,128)(2,1)S(1)}, bf16[256,512]{1,0:T(8,128)(2,1)S(1)}, u32[]{:S(2)}, u32[]{:S(2)}) %collective-permute-start.1) | collective-permute-done | bytes 262176 | tf_op jit(solution)/shard_map/ppermute | solution.py:50
  12.0 0.3 convolution_convert_fusion.2
  12.3 8.1 %collective-permute-start.8 = (bf16[256,512]{1,0:T(8,128)(2,1)S(1)}, bf16[256,512]{1,0:T(8,128)(2,1)S(1)}, u32[]{:S(2)}, u32[]{:S(2)}) collective-permute-start(bf16[256,512]{1,0:T(8,128)(2,1)S(1)} %convolution_convert_fusion.2), channel_id=1, source_target_pairs={{0,8},{1,9},{2,0},{3,1},{4,12},{5,13},{6,4},{7,5},{8,10},{9,11},{1... | collective-permute-start | bytes 786440 | tf_op jit(solution)/shard_map/ppermute | solution.py:50
  20.4 0.3 convolution_convert_fusion.1
  20.9 0.3 convolution_convert_fusion
  21.2 0.6 %copy-done.2 = bf16[1,1,512,512]{3,2,1,0:T(8,128)(2,1)S(1)} copy-done((bf16[1,1,512,512]{3,2,1,0:T(8,128)(2,1)S(1)}, bf16[1,1,512,512]{3,2,1,0:T(8,128)(2,1)}, u32[]{:S(2)}) %copy-start.2) | copy-done | bytes 524312
  21.9 0.1 dynamic_slice.27
  22.0 2.2 %collective-permute-start.5 = (bf16[256,512]{1,0:T(8,128)(2,1)S(1)}, bf16[256,512]{1,0:T(8,128)(2,1)S(1)}, u32[]{:S(2)}, u32[]{:S(2)}) collective-permute-start(bf16[256,512]{1,0:T(8,128)(2,1)S(1)} %convolution_convert_fusion), channel_id=1, source_target_pairs={{0,12},{1,13},{2,4},{3,5},{4,8},{5,9},{6,0},{7,1},{8,14},{9,15},{1... | collective-permute-start | bytes 786440 | tf_op jit(solution)/shard_map/ppermute | solution.py:50
  24.2 2.2 %collective-permute-done.8 = bf16[256,512]{1,0:T(8,128)(2,1)S(1)} collective-permute-done((bf16[256,512]{1,0:T(8,128)(2,1)S(1)}, bf16[256,512]{1,0:T(8,128)(2,1)S(1)}, u32[]{:S(2)}, u32[]{:S(2)}) %collective-permute-start.8) | collective-permute-done | bytes 262176 | tf_op jit(solution)/shard_map/ppermute | solution.py:50
  26.4 4.7 %collective-permute-done.3 = bf16[256,512]{1,0:T(8,128)(2,1)S(1)} collective-permute-done((bf16[256,512]{1,0:T(8,128)(2,1)S(1)}, bf16[256,512]{1,0:T(8,128)(2,1)S(1)}, u32[]{:S(2)}, u32[]{:S(2)}) %collective-permute-start.3) | collective-permute-done | bytes 262176 | tf_op jit(solution)/shard_map/ppermute | solution.py:50
  31.1 1.4 %collective-permute-done.2 = bf16[256,512]{1,0:T(8,128)(2,1)S(1)} collective-permute-done((bf16[256,512]{1,0:T(8,128)(2,1)S(1)}, bf16[256,512]{1,0:T(8,128)(2,1)S(1)}, u32[]{:S(2)}, u32[]{:S(2)}) %collective-permute-start.2) | collective-permute-done | bytes 262176 | tf_op jit(solution)/shard_map/ppermute | solution.py:50
  32.5 0.2 and_select_fusion.1
  32.7 0.2 fusion.13
  32.9 0.2 convolution_add_fusion.1
  33.1 0.2 fusion.15
  33.4 0.2 fusion.9
  33.6 0.2 convolution_add_fusion.2
  33.8 0.2 fusion.1
  34.1 1.4 %collective-permute-done.5 = bf16[256,512]{1,0:T(8,128)(2,1)S(1)} collective-permute-done((bf16[256,512]{1,0:T(8,128)(2,1)S(1)}, bf16[256,512]{1,0:T(8,128)(2,1)S(1)}, u32[]{:S(2)}, u32[]{:S(2)}) %collective-permute-start.5) | collective-permute-done | bytes 262176 | tf_op jit(solution)/shard_map/ppermute | solution.py:50
  35.4 0.2 fusion.7
  35.7 0.1 add.50
  35.8 1.1 %collective-permute-done.10 = bf16[256,512]{1,0:T(8,128)(2,1)S(1)} collective-permute-done((bf16[256,512]{1,0:T(8,128)(2,1)S(1)}, bf16[256,512]{1,0:T(8,128)(2,1)S(1)}, u32[]{:S(2)}, u32[]{:S(2)}) %collective-permute-start.10) | collective-permute-done | bytes 262176 | tf_op jit(solution)/shard_map/ppermute | solution.py:50
  37.0 0.2 fusion.4
  37.2 0.8 %fusion.3 = bf16[1,2,256,512]{3,2,1,0:T(8,128)(2,1)} fusion(bf16[1,2,256,512]{3,2,1,0:T(8,128)(2,1)} %copy-done.1, s32[]{:T(128)S(6)} %select_n.52, f32[256,512]{1,0:T(8,128)S(1)} %add.50, f32[256,512]{1,0:T(8,128)S(1)} %fusion.4), kind=kLoop, calls=%fused_computation.14 | loop fusion | flops 262144 | bytes 1310724 | tf_op jit(solution)/shard_map/dynamic_update_slice | solution.py:103
  (23 shorter events, 0.3 us)
Async XLA Ops:
  0.0 4.9 %copy-start = (bf16[1,1,512,512]{3,2,1,0:T(8,128)(2,1)S(1)}, bf16[1,1,512,512]{3,2,1,0:T(8,128)(2,1)}, u32[]{:S(2)}) copy-start(bf16[1,1,512,512]{3,2,1,0:T(8,128)(2,1)} %param.7) | copy-start | bytes 1572868
  1.1 10.8 %collective-permute-start.1 = (bf16[256,512]{1,0:T(8,128)(2,1)S(1)}, bf16[256,512]{1,0:T(8,128)(2,1)S(1)}, u32[]{:S(2)}, u32[]{:S(2)}) collective-permute-start(bf16[256,512]{1,0:T(8,128)(2,1)S(1)} %get-tuple-element.27), channel_id=1, source_target_pairs={{0,2},{1,3},{2,0},{3,1},{4,6},{5,7},{6,4},{7,5},{8,10},{9,11},{10,... | collective-permute-start | bytes 786440 | tf_op jit(solution)/shard_map/ppermute | solution.py:50
  4.1 0.7 %copy-start.3 = (s32[4]{0:T(128)S(1)}, s32[4]{0:T(128)}, u32[]{:S(2)}) copy-start(s32[4]{0:T(128)} %param.8) | copy-start | bytes 52
  4.1 0.7 %copy-start.4 = (s32[4]{0:T(128)S(1)}, s32[4]{0:T(128)}, u32[]{:S(2)}) copy-start(s32[4]{0:T(128)} %param.9) | copy-start | bytes 52
  4.1 16.7 %collective-permute-start = (bf16[256,512]{1,0:T(8,128)(2,1)S(1)}, bf16[256,512]{1,0:T(8,128)(2,1)S(1)}, u32[]{:S(2)}, u32[]{:S(2)}) collective-permute-start(bf16[256,512]{1,0:T(8,128)(2,1)S(1)} %get-tuple-element.15), channel_id=1, source_target_pairs={{0,2},{1,3},{2,0},{3,1},{4,6},{5,7},{6,4},{7,5},{8,10},{9,11},{10,... | collective-permute-start | bytes 786440 | tf_op jit(solution)/shard_map/ppermute | solution.py:50
  5.5 18.7 %collective-permute-start.6 = (bf16[256,512]{1,0:T(8,128)(2,1)S(1)}, bf16[256,512]{1,0:T(8,128)(2,1)S(1)}, u32[]{:S(2)}, u32[]{:S(2)}) collective-permute-start(bf16[256,512]{1,0:T(8,128)(2,1)S(1)} %convolution_convert_fusion.3), channel_id=1, source_target_pairs={{0,0},{1,1},{2,8},{3,9},{4,4},{5,5},{6,12},{7,13},{8,2},{9,3},{10,... | collective-permute-start | bytes 786440 | tf_op jit(solution)/shard_map/ppermute | solution.py:50
  12.3 14.1 %collective-permute-start.8 = (bf16[256,512]{1,0:T(8,128)(2,1)S(1)}, bf16[256,512]{1,0:T(8,128)(2,1)S(1)}, u32[]{:S(2)}, u32[]{:S(2)}) collective-permute-start(bf16[256,512]{1,0:T(8,128)(2,1)S(1)} %convolution_convert_fusion.2), channel_id=1, source_target_pairs={{0,8},{1,9},{2,0},{3,1},{4,12},{5,13},{6,4},{7,5},{8,10},{9,11},{1... | collective-permute-start | bytes 786440 | tf_op jit(solution)/shard_map/ppermute | solution.py:50
  20.8 1.0 %copy-start.2 = (bf16[1,1,512,512]{3,2,1,0:T(8,128)(2,1)S(1)}, bf16[1,1,512,512]{3,2,1,0:T(8,128)(2,1)}, u32[]{:S(2)}) copy-start(bf16[1,1,512,512]{3,2,1,0:T(8,128)(2,1)} %param.6) | copy-start | bytes 1572868
  20.8 10.3 %collective-permute-start.3 = (bf16[256,512]{1,0:T(8,128)(2,1)S(1)}, bf16[256,512]{1,0:T(8,128)(2,1)S(1)}, u32[]{:S(2)}, u32[]{:S(2)}) collective-permute-start(bf16[256,512]{1,0:T(8,128)(2,1)S(1)} %convolution_convert_fusion.1), channel_id=1, source_target_pairs={{0,4},{1,5},{2,12},{3,13},{4,0},{5,1},{6,8},{7,9},{8,6},{9,7},{10,... | collective-permute-start | bytes 786440 | tf_op jit(solution)/shard_map/ppermute | solution.py:50
  21.8 10.7 %collective-permute-start.2 = (bf16[256,512]{1,0:T(8,128)(2,1)S(1)}, bf16[256,512]{1,0:T(8,128)(2,1)S(1)}, u32[]{:S(2)}, u32[]{:S(2)}) collective-permute-start(bf16[256,512]{1,0:T(8,128)(2,1)S(1)} %dynamic-slice_bitcast_fusion), channel_id=1, source_target_pairs={{0,2},{1,3},{2,0},{3,1},{4,6},{5,7},{6,4},{7,5},{8,10},{9,11},{10,... | collective-permute-start | bytes 786440 | tf_op jit(solution)/shard_map/ppermute | solution.py:50
  22.0 13.4 %collective-permute-start.5 = (bf16[256,512]{1,0:T(8,128)(2,1)S(1)}, bf16[256,512]{1,0:T(8,128)(2,1)S(1)}, u32[]{:S(2)}, u32[]{:S(2)}) collective-permute-start(bf16[256,512]{1,0:T(8,128)(2,1)S(1)} %convolution_convert_fusion), channel_id=1, source_target_pairs={{0,12},{1,13},{2,4},{3,5},{4,8},{5,9},{6,0},{7,1},{8,14},{9,15},{1... | collective-permute-start | bytes 786440 | tf_op jit(solution)/shard_map/ppermute | solution.py:50
  24.2 8.7 %collective-permute-start.7 = (bf16[256,512]{1,0:T(8,128)(2,1)S(1)}, bf16[256,512]{1,0:T(8,128)(2,1)S(1)}, u32[]{:S(2)}, u32[]{:S(2)}) collective-permute-start(bf16[256,512]{1,0:T(8,128)(2,1)S(1)} %collective-permute-done.6), channel_id=1, source_target_pairs={{0,1},{1,0},{2,3},{3,2},{4,5},{5,4},{6,7},{7,6},{8,9},{9,8},{10,11... | collective-permute-start | bytes 786440 | tf_op jit(solution)/shard_map/ppermute | solution.py:50
  26.4 7.5 %collective-permute-start.9 = (bf16[256,512]{1,0:T(8,128)(2,1)S(1)}, bf16[256,512]{1,0:T(8,128)(2,1)S(1)}, u32[]{:S(2)}, u32[]{:S(2)}) collective-permute-start(bf16[256,512]{1,0:T(8,128)(2,1)S(1)} %collective-permute-done.8), channel_id=1, source_target_pairs={{0,1},{1,0},{2,3},{3,2},{4,5},{5,4},{6,7},{7,6},{8,9},{9,8},{10,11... | collective-permute-start | bytes 786440 | tf_op jit(solution)/shard_map/ppermute | solution.py:50
  31.1 2.5 %collective-permute-start.4 = (bf16[256,512]{1,0:T(8,128)(2,1)S(1)}, bf16[256,512]{1,0:T(8,128)(2,1)S(1)}, u32[]{:S(2)}, u32[]{:S(2)}) collective-permute-start(bf16[256,512]{1,0:T(8,128)(2,1)S(1)} %collective-permute-done.3), channel_id=1, source_target_pairs={{0,1},{1,0},{2,3},{3,2},{4,5},{5,4},{6,7},{7,6},{8,9},{9,8},{10,11... | collective-permute-start | bytes 786440 | tf_op jit(solution)/shard_map/ppermute | solution.py:50
  35.4 1.5 %collective-permute-start.10 = (bf16[256,512]{1,0:T(8,128)(2,1)S(1)}, bf16[256,512]{1,0:T(8,128)(2,1)S(1)}, u32[]{:S(2)}, u32[]{:S(2)}) collective-permute-start(bf16[256,512]{1,0:T(8,128)(2,1)S(1)} %collective-permute-done.5), channel_id=1, source_target_pairs={{0,1},{1,0},{2,3},{3,2},{4,5},{5,4},{6,7},{7,6},{8,9},{9,8},{10,11... | collective-permute-start | bytes 786440 | tf_op jit(solution)/shard_map/ppermute | solution.py:50
  35.8 1.4 %copy-start.1 = (bf16[1,2,256,512]{3,2,1,0:T(8,128)(2,1)}, bf16[1,2,256,512]{3,2,1,0:T(8,128)(2,1)S(1)}, u32[]{:S(2)}) copy-start(bf16[1,2,256,512]{3,2,1,0:T(8,128)(2,1)S(1)} %bitcast_dynamic-update-slice_fusion) | copy-start | bytes 1572868
